TPU v7x, 32 devices: a whole 2x2x4 slice. The times are simulated.
32 devices in a mesh: seq: 2 (over x), fsdp: 16 (over z, y, core).
Axes of the slice: x: 2, y: 2, z: 4, core: 2. Of those that a mesh axis runs over, the one named last changes fastest.
Arguments:
- incoming_state: bfloat16 [16, 512, 768], P('fsdp', 'seq'), may hold values from -6 to 6
- projection_matrix_triple: bfloat16 [768, 2304], P(('seq', 'fsdp')), may hold values from -0.3125 to 0.3125
- merge_matrix: bfloat16 [768, 768], P(('seq', 'fsdp')), may hold values from -1.75 to 1.75
- widen_matrix: bfloat16 [768, 3072], P(('seq', 'fsdp')), may hold values from -0.21875 to 0.21875
- shrink_matrix: bfloat16 [3072, 768], P(('seq', 'fsdp')), may hold values from -0.109375 to 0.109375
- offset_table: bfloat16 [6, 768], P(None, ('seq', 'fsdp')), may hold values from -1.5 to 1.5
- norm_scales: bfloat16 [2, 768], P(None, ('seq', 'fsdp')), may hold values from 0.25 to 1.75
- widen_offset: bfloat16 [3072], P(('seq', 'fsdp')), may hold values from -1.5 to 1.5
- trainable_gate_scores: float32 [12, 512, 512], P('seq', 'fsdp'), may hold values from -8 to 8
- gate_perturbation: float32 [12, 512, 512], P('seq', 'fsdp'), may hold values from -6 to 6
- softening_scale: float32 [12], P('seq'), may hold values from 0.5 to 2
- passage_extents: int32 [32], replicated, may hold values from 1 to 512, 8192 in all
- result_cotangent: bfloat16 [16, 512, 768], P('fsdp', 'seq'), may hold values from -6 to 6
Outputs:
- layer_out: bfloat16 [16, 512, 768], P('fsdp', 'seq')
- input_grad: float32 [16, 512, 768], P('fsdp', 'seq')
- grad_w_qkv: float32 [768, 2304], P(('seq', 'fsdp'))
- grad_w_out: float32 [768, 768], P(('seq', 'fsdp'))
- grad_w_up: float32 [768, 3072], P(('seq', 'fsdp'))
- grad_w_down: float32 [3072, 768], P(('seq', 'fsdp'))
- grad_biases: float32 [6, 768], P(None, ('seq', 'fsdp'))
- grad_gains: float32 [2, 768], P(None, ('seq', 'fsdp'))
- grad_bias_up: float32 [3072], P(('seq', 'fsdp'))
- mask_logit_gradient: float32 [12, 512, 512], P('seq', 'fsdp')
Inputs may be any that keep to these rules, and one draw needn't show every extreme that they name: `passage_extents`: they sum to 8192, and the longest is exactly 512.
All inputs are finite; a program needn't handle non-finite values.
Results may differ from a plain program's by a relative error of at most 0.013.
Values may be sent and summed in bfloat16 or wider, within the bound.
No kernel may reach another device: no remote copies, remote signals or barrier semaphores. Data moves between devices by JAX's collectives and lax.ppermute only.
A program may use at most 192 MiB of HBM per device.

v0:
```python
from functools import partial

import jax
import jax.numpy as jnp
from jax import lax
from jax.sharding import PartitionSpec as P

D = 768
FOCUS_COUNT = 12
HDIM = 64
MPOS = 512


EPS = 1e-05


def padded(block, sides, width):
    for axis, dim in sides:
        count = lax.axis_size(axis)
        forward = [(i, i + 1) for i in range(count - 1)]
        backward = [(target, source) for source, target in forward]
        low = lax.ppermute(
            lax.slice_in_dim(block, block.shape[dim] - width, None, axis=dim), axis, forward
        )
        high = lax.ppermute(lax.slice_in_dim(block, 0, width, axis=dim), axis, backward)
        block = jnp.concatenate([low, block, high], axis=dim)
    return block


def as_sent(value):
    return jax.tree.map(lambda a: a.astype(jnp.bfloat16) if a.dtype == jnp.float32 else a, value)


def shifted(value, axis, steps):
    count = lax.axis_size(axis)
    leading, last = (max(0, -steps), min(count, count - steps))
    return lax.ppermute(value, axis, [(source, source + steps) for source in range(leading, last)])


def layer_norm(values, gain, shift):
    center = values - jnp.mean(values, axis=-1, keepdims=True)
    spread = jnp.mean(center * center, axis=-1, keepdims=True)
    return center * lax.rsqrt(spread + EPS) * gain + shift


def locate(index, passage_opening, passage_finish, stream_rows):
    document = jnp.sum((passage_finish[None, :] <= index[:, None]).astype(jnp.int32), axis=1)
    begin = jnp.max(
        jnp.where(passage_opening[None, :] <= index[:, None], passage_opening[None, :], 0), axis=1
    )
    inside = (index >= 0) & (index < stream_rows)
    document = jnp.where(inside, document, -1)
    position = (index - begin) % MPOS
    return (document, position)


def one_hot_rows(positions):
    return (positions[:, None] == jnp.arange(MPOS, dtype=jnp.int32)[None, :]).astype(jnp.bfloat16)


def plain_dot(left, right):
    return jnp.dot(left, right, preferred_element_type=jnp.float32)


def left_dot(left, right):
    return lax.dot_general(
        left, right, (((0,), (0,)), ((), ())), preferred_element_type=jnp.float32
    )


def right_dot(left, right):
    return lax.dot_general(
        left, right, (((1,), (1,)), ((), ())), preferred_element_type=jnp.float32
    )


def lookup_of(table, rows_hot, cols_hot):
    picked = plain_dot(rows_hot, table).astype(jnp.bfloat16)
    return right_dot(picked, cols_hot)


def token_forward(
    tokens,
    context_tok,
    merge_matrix,
    widen_matrix,
    shrink_matrix,
    offset_table,
    norm_scales,
    widen_offset,
):
    small = offset_table.astype(jnp.float32)
    gain_rows = norm_scales.astype(jnp.float32)
    attn = plain_dot(context_tok, merge_matrix) + small[2]
    hidden_one = tokens.astype(jnp.float32) + attn
    normed = layer_norm(hidden_one, gain_rows[0], small[4])
    normed_low = normed.astype(jnp.bfloat16)
    up = plain_dot(normed_low, widen_matrix) + widen_offset.astype(jnp.float32)
    act_low = jax.nn.gelu(up, approximate=False).astype(jnp.bfloat16)
    hidden_two = normed + (plain_dot(act_low, shrink_matrix) + small[3])
    return (hidden_one, normed, normed_low, up, act_low, hidden_two)


def per_device(
    incoming_state,
    projection_matrix_triple,
    merge_matrix,
    widen_matrix,
    shrink_matrix,
    offset_table,
    norm_scales,
    widen_offset,
    trainable_gate_scores,
    gate_perturbation,
    softening_scale,
    passage_extents,
    result_cotangent,
):
    tok_rows = incoming_state.shape[1]
    tokens = incoming_state.reshape(tok_rows, D)
    seq_count = lax.axis_size("seq")
    head_count = FOCUS_COUNT // seq_count
    head_width = head_count * HDIM
    group_rows = tok_rows * seq_count
    stream_rows = group_rows * lax.axis_size("fsdp")
    block_rows = min(512, group_rows)
    window_rows = 3 * group_rows
    offsets_turned = offset_table.T
    gains_turned = norm_scales.T
    params = (
        lax.all_gather(projection_matrix_triple, ("seq", "fsdp"), axis=0, tiled=True),
        lax.all_gather(merge_matrix, ("seq", "fsdp"), axis=0, tiled=True),
        lax.all_gather(widen_matrix, ("seq", "fsdp"), axis=0, tiled=True),
        lax.all_gather(shrink_matrix, ("seq", "fsdp"), axis=0, tiled=True),
        lax.all_gather(offsets_turned, ("seq", "fsdp"), axis=0, tiled=True),
        lax.all_gather(gains_turned, ("seq", "fsdp"), axis=0, tiled=True),
        lax.all_gather(widen_offset, ("seq", "fsdp"), axis=0, tiled=True),
    )
    full_qkv, full_out, full_up, full_down = (params[0], params[1], params[2], params[3])
    full_biases = params[4].T
    full_gains = params[5].T
    full_bias_up = params[6]
    small = full_biases.astype(jnp.float32)
    gain_rows = full_gains.astype(jnp.float32)
    relaxed_mask_rows = jax.nn.sigmoid(
        (trainable_gate_scores + gate_perturbation) / softening_scale[:, None, None]
    )
    smooth_gate = lax.all_gather(relaxed_mask_rows.astype(jnp.bfloat16), "fsdp", axis=1, tiled=True)
    passage_finish = jnp.cumsum(passage_extents)
    passage_opening = passage_finish - passage_extents
    first = lax.axis_index("fsdp") * group_rows
    query_doc, query_pos = locate(
        first + jnp.arange(group_rows, dtype=jnp.int32),
        passage_opening,
        passage_finish,
        stream_rows,
    )
    key_doc, key_pos = locate(
        first - group_rows + jnp.arange(window_rows, dtype=jnp.int32),
        passage_opening,
        passage_finish,
        stream_rows,
    )
    query_hot = one_hot_rows(query_pos)
    key_hot = one_hot_rows(key_pos)
    qkv_bias = jnp.concatenate([small[0], jnp.zeros((D,), jnp.float32), small[1]])
    qkv = (
        (plain_dot(tokens, full_qkv) + qkv_bias)
        .astype(jnp.bfloat16)
        .reshape(tok_rows, 3, seq_count, head_width)
    )
    heads = lax.all_to_all(qkv, "seq", split_axis=2, concat_axis=0, tiled=True).reshape(
        group_rows, 3, head_width
    )
    pair = jnp.concatenate([heads[:, 1], heads[:, 2]], axis=1)
    window = padded(pair, (("fsdp", 0),), group_rows)
    query_heads = heads[:, 0].reshape(group_rows, head_count, HDIM).transpose(1, 0, 2)
    key_heads = window[:, :head_width].reshape(window_rows, head_count, HDIM).transpose(1, 0, 2)
    value_heads = window[:, head_width:].reshape(window_rows, head_count, HDIM).transpose(1, 0, 2)

    def masked_scores(query_block, key_all, start_row):
        scores = right_dot(query_block, key_all) * 0.125
        same = query_doc[start_row : start_row + block_rows, None] == key_doc[None, :]
        return jnp.where(same, scores, -1e30)

    def head_forward(operands):
        query_one, key_one, value_one, table = operands
        scores = masked_scores(query_one, key_one, 0)
        row_top = jnp.max(scores, axis=1, keepdims=True)
        weights = jnp.exp(scores - row_top)
        row_total = jnp.sum(weights, axis=1, keepdims=True)
        lookup = lookup_of(table, query_hot, key_hot)
        mixed = (weights / row_total * lookup).astype(jnp.bfloat16)
        outputs = [plain_dot(mixed, value_one)]
        totals = [row_top + jnp.log(row_total)]
        return (jnp.concatenate(outputs, axis=0), jnp.concatenate(totals, axis=0))

    context, log_totals = lax.map(head_forward, (query_heads, key_heads, value_heads, smooth_gate))
    context_low = context.transpose(1, 0, 2).reshape(group_rows, 1, head_width).astype(jnp.bfloat16)
    context_tok = lax.all_to_all(
        context_low, "seq", split_axis=0, concat_axis=1, tiled=True
    ).reshape(tok_rows, D)
    saved = token_forward(
        tokens, context_tok, full_out, full_up, full_down, full_biases, full_gains, full_bias_up
    )
    layer_out = layer_norm(saved[5], gain_rows[1], small[5]).astype(jnp.bfloat16)
    again = (
        lax.all_gather(projection_matrix_triple, ("seq", "fsdp"), axis=0, tiled=True),
        lax.all_gather(merge_matrix, ("seq", "fsdp"), axis=0, tiled=True),
        lax.all_gather(widen_matrix, ("seq", "fsdp"), axis=0, tiled=True),
        lax.all_gather(shrink_matrix, ("seq", "fsdp"), axis=0, tiled=True),
        lax.all_gather(offsets_turned, ("seq", "fsdp"), axis=0, tiled=True),
        lax.all_gather(gains_turned, ("seq", "fsdp"), axis=0, tiled=True),
        lax.all_gather(widen_offset, ("seq", "fsdp"), axis=0, tiled=True),
    )
    back_qkv, back_out, back_up, back_down = (again[0], again[1], again[2], again[3])
    hidden_one, normed, normed_low, up, act_low, hidden_two = token_forward(
        tokens, context_tok, again[1], again[2], again[3], again[4].T, again[5].T, again[6]
    )
    out_cot = result_cotangent.reshape(tok_rows, D).astype(jnp.float32)
    _, norm_two_pull = jax.vjp(layer_norm, hidden_two, gain_rows[1], small[5])
    grad_two, gain_two, shift_two = norm_two_pull(out_cot)
    down_low = grad_two.astype(jnp.bfloat16)
    grad_w_down = left_dot(act_low, down_low)
    grad_down_bias = jnp.sum(down_low.astype(jnp.float32), axis=0)
    _, gelu_pull = jax.vjp(partial(jax.nn.gelu, approximate=False), up)
    up_low = gelu_pull(right_dot(down_low, back_down))[0].astype(jnp.bfloat16)
    grad_w_up = left_dot(normed_low, up_low)
    grad_bias_up = jnp.sum(up_low.astype(jnp.float32), axis=0)
    grad_normed = grad_two + right_dot(up_low, back_up)
    _, norm_one_pull = jax.vjp(layer_norm, hidden_one, gain_rows[0], small[4])
    grad_one, gain_one, shift_one = norm_one_pull(grad_normed)
    attn_low = grad_one.astype(jnp.bfloat16)
    grad_w_out = left_dot(context_tok, attn_low)
    grad_out_bias = jnp.sum(attn_low.astype(jnp.float32), axis=0)
    context_grad = (
        right_dot(attn_low, back_out).astype(jnp.bfloat16).reshape(tok_rows, seq_count, head_width)
    )
    grad_heads = (
        lax.all_to_all(context_grad, "seq", split_axis=1, concat_axis=0, tiled=True)
        .reshape(group_rows, head_count, HDIM)
        .transpose(1, 0, 2)
    )

    def head_backward(operands):
        query_one, key_one, value_one, table, grad_head, total_one = operands
        key_grad = jnp.zeros((window_rows, HDIM), jnp.float32)
        value_grad = jnp.zeros((window_rows, HDIM), jnp.float32)
        table_grad = jnp.zeros((MPOS, MPOS), jnp.float32)
        probs = jnp.exp(masked_scores(query_one, key_one, 0) - total_one[0:block_rows])
        lookup = lookup_of(table, query_hot, key_hot)
        mixed = (probs * lookup).astype(jnp.bfloat16)
        mixed_grad = right_dot(grad_head, value_one)
        lookup_grad = mixed_grad * probs
        columns = jax.ops.segment_sum(lookup_grad.T, key_pos, num_segments=MPOS)
        table_grad = table_grad + jax.ops.segment_sum(columns.T, query_pos, num_segments=MPOS)
        prob_grad = mixed_grad * lookup
        delta = jnp.sum(prob_grad * probs, axis=1, keepdims=True)
        score_low = (probs * (prob_grad - delta)).astype(jnp.bfloat16)
        query_grads = [plain_dot(score_low, key_one) * 0.125]
        key_grad = key_grad + left_dot(score_low, query_one) * 0.125
        value_grad = value_grad + left_dot(mixed, grad_head)
        deltas = [delta]
        return (
            jnp.concatenate(query_grads, axis=0),
            key_grad,
            value_grad,
            table_grad,
            jnp.concatenate(deltas, axis=0),
        )

    query_grad, key_grad, value_grad, table_grad, row_deltas = lax.map(
        head_backward, (query_heads, key_heads, value_heads, smooth_gate, grad_heads, log_totals)
    )
    key_flat = key_grad.transpose(1, 0, 2)
    value_flat = value_grad.transpose(1, 0, 2)
    window_grad = jnp.concatenate(
        [key_flat.reshape(window_rows, head_width), value_flat.reshape(window_rows, head_width)],
        axis=1,
    )
    from_right = shifted(as_sent(window_grad[:group_rows]), "fsdp", -1)
    from_left = shifted(as_sent(window_grad[2 * group_rows :]), "fsdp", 1)
    own_grad = window_grad[group_rows : 2 * group_rows] + from_right + from_left
    query_flat = query_grad.transpose(1, 0, 2).reshape(group_rows, head_width)
    qkv_grad = (
        jnp.stack([query_flat, own_grad[:, :head_width], own_grad[:, head_width:]], axis=1)
        .astype(jnp.bfloat16)
        .reshape(group_rows, 3, 1, head_width)
    )
    token_grad = lax.all_to_all(qkv_grad, "seq", split_axis=0, concat_axis=2, tiled=True).reshape(
        tok_rows, 3 * D
    )
    grad_w_qkv = left_dot(tokens, token_grad)
    column_sums = jnp.sum(token_grad.astype(jnp.float32), axis=0)
    input_grad = grad_one + right_dot(token_grad, back_qkv)
    grad_small = jnp.stack(
        [
            column_sums[:D],
            column_sums[2 * D :],
            grad_out_bias,
            grad_down_bias,
            shift_one,
            shift_two,
        ],
        axis=1,
    )
    grad_gain_rows = jnp.stack([gain_one, gain_two], axis=1)
    summed = (
        lax.psum_scatter(grad_w_qkv, ("seq", "fsdp"), scatter_dimension=0, tiled=True),
        lax.psum_scatter(grad_w_out, ("seq", "fsdp"), scatter_dimension=0, tiled=True),
        lax.psum_scatter(grad_w_up, ("seq", "fsdp"), scatter_dimension=0, tiled=True),
        lax.psum_scatter(grad_w_down, ("seq", "fsdp"), scatter_dimension=0, tiled=True),
        lax.psum_scatter(grad_small, ("seq", "fsdp"), scatter_dimension=0, tiled=True),
        lax.psum_scatter(grad_gain_rows, ("seq", "fsdp"), scatter_dimension=0, tiled=True),
        lax.psum_scatter(grad_bias_up, ("seq", "fsdp"), scatter_dimension=0, tiled=True),
    )
    relaxed_mask_total = lax.psum_scatter(table_grad, "fsdp", scatter_dimension=1, tiled=True)
    mask_logit_gradient = (
        relaxed_mask_total
        * relaxed_mask_rows
        * (1.0 - relaxed_mask_rows)
        / softening_scale[:, None, None]
    )
    return (
        layer_out.reshape(1, tok_rows, D),
        input_grad.reshape(1, tok_rows, D),
        summed[0],
        summed[1],
        summed[2],
        summed[3],
        summed[4].T,
        summed[5].T,
        summed[6],
        mask_logit_gradient,
    )


def solution(mesh):
    return jax.shard_map(
        per_device,
        mesh=mesh,
        in_specs=(
            P("fsdp", "seq", None),
            P(("seq", "fsdp"), None),
            P(("seq", "fsdp"), None),
            P(("seq", "fsdp"), None),
            P(("seq", "fsdp"), None),
            P(None, ("seq", "fsdp")),
            P(None, ("seq", "fsdp")),
            P(("seq", "fsdp")),
            P("seq", "fsdp", None),
            P("seq", "fsdp", None),
            P("seq"),
            P(),
            P("fsdp", "seq", None),
        ),
        out_specs=(
            P("fsdp", "seq", None),
            P("fsdp", "seq", None),
            P(("seq", "fsdp"), None),
            P(("seq", "fsdp"), None),
            P(("seq", "fsdp"), None),
            P(("seq", "fsdp"), None),
            P(None, ("seq", "fsdp")),
            P(None, ("seq", "fsdp")),
            P(("seq", "fsdp")),
            P("seq", "fsdp", None),
        ),
        check_vma=False,
    )
```

profile of v0, /device:TPU:1, one launch (start us, length us, event | category | flops | bytes accessed | tf_op | source)
XLA Modules:
  0.0 1192.5 jit_solution(11110227320052372935)
XLA Ops:
  11.4 43.5 %all-gather = bf16[32,24,6]{1,2,0:T(8,128)(2,1)S(1)} all-gather(bf16[1,24,6]{1,2,0:T(8,128)(2,1)} %bitcast.285), channel_id=1, replica_groups=mesh['seq'=2,'fsdp'=16] {'seq','fsdp'}, dimensions={0}, use_global_device_ids=true | all-gather | bytes 9504 | tf_op jit(solution)/shard_map/all_gather | solution.py:135
  55.9 17.7 %all-gather.8.cloned.1.call-done = bf16[768,2304]{1,0:T(8,128)(2,1)} async-done(((bf16[24,2304]{1,0:T(8,128)(2,1)}), bf16[768,2304]{1,0:T(8,128)(2,1)}) %all-gather.8.cloned.1.call-update) | async-done | bytes 3538960 | tf_op jit(solution)/shard_map/all_gather | solution.py:131
  78.4 3.6 all-to-all-start
  82.9 14.0 %all-to-all-done = bf16[256,3,2,384]{3,0,1,2:T(8,128)(2,1)S(1)} async-done(((bf16[256,3,2,384]{3,0,1,2:T(8,128)(2,1)}), bf16[256,3,2,384]{3,0,1,2:T(8,128)(2,1)S(1)}, u32[]{:S(2)}, u32[]{:S(2)}) %all-to-all-start) | async-done | bytes 1179680 | tf_op jit(solution)/shard_map/all_to_all | solution.py:172
  106.9 12.9 %collective-permute-done.1 = bf16[512,768]{1,0:T(8,128)(2,1)S(1)} collective-permute-done((bf16[512,768]{1,0:T(8,128)(2,1)}, bf16[512,768]{1,0:T(8,128)(2,1)S(1)}, u32[]{:S(2)}, u32[]{:S(2)}) %collective-permute-start.1) | collective-permute-done | bytes 786464 | tf_op jit(solution)/shard_map/ppermute | solution.py:25
  119.8 6.7 collective-permute-done
  133.3 59.6 %while.31 = (s32[]{:T(128)}, bf16[6,512,64]{1,2,0:T(8,128)(2,1)S(1)}, f32[6,512,1]{1,2,0:T(1,128)}, s32[512]{0:T(512)S(1)}, s32[1536]{0:T(1024)S(1)}, /*index=5*...) while((s32[]{:T(128)}, ...), condition=%wide.region_8.9_spmd.clone, body=%wide.region_5.8_spmd.clone.sunk | while | flops 1285291520 | bytes 12099717 | solution.py:198
  138.7 3.3 fusion.196
  148.6 3.3 fusion.196
  158.5 3.3 fusion.196
  168.4 3.3 fusion.196
  178.4 3.3 fusion.196
  195.5 3.5 all-to-all-start.1
  199.2 41.9 %all-reduce = bf16[3072]{0:T(1024)(128)(2,1)S(1)} all-reduce(bf16[3072]{0:T(1024)(128)(2,1)S(1)} %dynamic-update-slice), channel_id=1, replica_groups=mesh['seq'=2,'fsdp'=16] {'seq','fsdp'}, use_global_device_ids=true, to_apply=%add | all-reduce | flops 3072 | bytes 12288
  241.2 40.0 %all-gather.1 = bf16[32,24,2]{1,2,0:T(2,128)(2,1)S(1)} all-gather(bf16[1,24,2]{1,2,0:T(2,128)(2,1)S(1)} %bitcast.287), channel_id=1, replica_groups=mesh['seq'=2,'fsdp'=16] {'seq','fsdp'}, dimensions={0}, use_global_device_ids=true | all-gather | bytes 3168 | tf_op jit(solution)/shard_map/all_gather | solution.py:136
  284.9 11.4 multiply_convert_fusion.3
  296.3 24.2 %all-gather.16.cloned.1.call-done = bf16[3072,768]{1,0:T(8,128)(2,1)} async-done(((bf16[96,768]{1,0:T(8,128)(2,1)}), bf16[3072,768]{1,0:T(8,128)(2,1)}) %all-gather.16.cloned.1.call-update) | async-done | bytes 4718608 | tf_op jit(solution)/shard_map/all_gather | solution.py:134
  320.6 4.0 fusion.137
  336.2 3.5 all-to-all-start.2
  339.7 6.4 all-to-all-done.2
  348.3 241.1 %while.32 = (s32[]{:T(128)}, bf16[6,512,64]{1,2,0:T(8,128)(2,1)}, f32[6,1536,64]{1,2,0:T(8,128)}, f32[6,1536,64]{1,2,0:T(8,128)}, f32[6,512,512]{2,1,0:T(8,128)}...) while((s32[]{:T(128)}, bf16[6,512,64]{1,2,0:T(8,128)(2,1)}, ...), condition=%wide.region_21.22_spmd.clone.clone, body=%wide.region_17.21_spmd.clone.clone.sunk | while | flops 1597898240 | bytes 73859280 | solution.py:272
  350.8 4.6 fusion.210
  355.5 3.3 multiply_reduce_fusion.6
  369.2 3.6 copy.209
  372.8 10.5 scatter_custom_fusion.14
  383.6 4.0 scatter_custom_fusion.15
  390.9 4.7 fusion.210
  395.6 3.3 multiply_reduce_fusion.6
  409.3 3.6 copy.209
  412.9 10.5 scatter_custom_fusion.14
  423.7 4.0 scatter_custom_fusion.15
  431.1 4.7 fusion.210
  435.7 3.3 multiply_reduce_fusion.6
  449.4 3.6 copy.209
  453.0 10.5 scatter_custom_fusion.14
  463.8 4.0 scatter_custom_fusion.15
  471.1 4.6 fusion.210
  475.8 3.3 multiply_reduce_fusion.6
  489.5 3.6 copy.209
  493.1 10.5 scatter_custom_fusion.14
  503.9 4.0 scatter_custom_fusion.15
  511.3 4.7 fusion.210
  515.9 3.3 multiply_reduce_fusion.6
  529.7 3.6 copy.209
  533.3 10.5 scatter_custom_fusion.14
  544.1 4.0 scatter_custom_fusion.15
  551.4 4.6 fusion.210
  556.1 3.3 multiply_reduce_fusion.6
  569.9 3.6 copy.209
  573.4 10.5 scatter_custom_fusion.14
  584.3 4.0 scatter_custom_fusion.15
  594.6 4.2 collective-permute-start.3
  600.8 15.3 %collective-permute-done.3 = bf16[512,768]{0,1:T(8,128)(2,1)S(1)} collective-permute-done((bf16[512,768]{0,1:T(8,128)(2,1)S(1)}, bf16[512,768]{0,1:T(8,128)(2,1)S(1)}, u32[]{:S(2)}, u32[]{:S(2)}) %collective-permute-start.3) | collective-permute-done | bytes 786464 | tf_op jit(solution)/shard_map/ppermute | solution.py:37
  618.1 14.0 %all_to_all.60 = bf16[512,3,1,384]{3,1,2,0:T(4,128)(2,1)S(1)} all-to-all(bf16[512,3,1,384]{3,1,2,0:T(4,128)(2,1)S(1)} %copy.191), channel_id=1, replica_groups=mesh['seq'=2,'fsdp'=16] {'seq'}, dimensions={0} | all-to-all | bytes 2359296 | tf_op jit(solution)/shard_map/all_to_all | solution.py:290
  633.0 4.0 convolution_bitcast_fusion.1
  637.0 8.1 copy.196
  646.3 6.6 fusion.126
  653.9 6.5 fusion.139
  661.9 43.8 %all-reduce.4 = (f32[768,6]{0,1:T(8,128)S(1)}, f32[768,2]{0,1:T(2,128)S(1)}, f32[3072]{0:T(1024)S(1)}) all-reduce(f32[768,6]{0,1:T(8,128)S(1)} %stack.51, f32[768,2]{0,1:T(2,128)S(1)} %pad_maximum_fusion.5, f32[3072]{0:T(1024)S(1)} %copy-done.32), channel_id=6, replica_groups=mesh['seq'=2,'fsdp'=16] {'seq','fsdp'}, use_global_device_ids=true, to_apply=%region_31.32.clone | all-reduce | flops 9216 | bytes 73728
  707.6 4.3 fusion.102
  713.8 64.2 %reduce-scatter.10.cloned.1.call-done = f32[24,768]{1,0:T(8,128)} async-done(((f32[768,768]{1,0:T(8,128)}), f32[24,768]{1,0:T(8,128)}) %reduce-scatter.10.cloned.1.call-update) | async-done | bytes 73744 | tf_op jit(solution)/shard_map/reduce_scatter | solution.py:310
  778.0 124.4 %reduce-scatter.18.cloned.1.call-done = f32[24,2304]{1,0:T(8,128)} async-done(((f32[768,2304]{1,0:T(8,128)}), f32[24,2304]{1,0:T(8,128)}) %reduce-scatter.18.cloned.1.call-update) | async-done | bytes 221200
  902.4 142.1 %reduce-scatter.12.cloned.1.call-done = f32[24,3072]{1,0:T(8,128)} async-done(((f32[768,3072]{1,0:T(8,128)}), f32[24,3072]{1,0:T(8,128)}) %reduce-scatter.12.cloned.1.call-update) | async-done | bytes 294928 | tf_op jit(solution)/shard_map/reduce_scatter | solution.py:311
  1044.6 140.9 %reduce-scatter.14.cloned.1.call-done = f32[96,768]{1,0:T(8,128)} async-done(((f32[3072,768]{1,0:T(8,128)}), f32[96,768]{1,0:T(8,128)}) %reduce-scatter.14.cloned.1.call-update) | async-done | bytes 294928 | tf_op jit(solution)/shard_map/reduce_scatter | solution.py:312
  (321 shorter events, 192.5 us)
Async XLA Ops:
  7.2 66.4 %all-gather.8.cloned.1.call-start = ((), (), s32[]{:S(2)}) async-start(), calls=%async_computation.9 | async-start | bytes 3649536 | tf_op jit(solution)/shard_map/all_gather | solution.py:131
  7.9 125.3 %all-gather.10.cloned.1.call-start = ((), (), s32[]{:S(2)}) async-start(), calls=%async_computation.10 | async-start | bytes 3342336 | tf_op jit(solution)/shard_map/all_gather | solution.py:148
  10.1 272.6 %all-gather.12.cloned.1.call-start = ((), (), s32[]{:S(2)}) async-start(), calls=%async_computation.11 | async-start | bytes 1216512 | tf_op jit(solution)/shard_map/all_gather | solution.py:132
  10.8 274.0 %all-gather.14.cloned.1.call-start = ((), (), s32[]{:S(2)}) async-start(), calls=%async_computation.12 | async-start | bytes 4866048 | tf_op jit(solution)/shard_map/all_gather | solution.py:133
  76.8 5.8 copy-start.39
  78.4 18.5 %all-to-all-start = ((bf16[256,3,2,384]{3,0,1,2:T(8,128)(2,1)}), bf16[256,3,2,384]{3,0,1,2:T(8,128)(2,1)S(1)}, u32[]{:S(2)}, u32[]{:S(2)}) async-start(bf16[256,3,2,384]{3,0,1,2:T(8,128)(2,1)} %copy.173), calls=%async_computation | async-start | bytes 2359296 | tf_op jit(solution)/shard_map/all_to_all | solution.py:172
  82.0 238.5 %all-gather.16.cloned.1.call-start = ((), (), s32[]{:S(2)}) async-start(), calls=%async_computation.13 | async-start | bytes 4866048 | tf_op jit(solution)/shard_map/all_gather | solution.py:134
  98.1 21.6 %collective-permute-start.1 = (bf16[512,768]{1,0:T(8,128)(2,1)}, bf16[512,768]{1,0:T(8,128)(2,1)S(1)}, u32[]{:S(2)}, u32[]{:S(2)}) collective-permute-start(bf16[512,768]{1,0:T(8,128)(2,1)} %pad_maximum_fusion.3), channel_id=1, source_target_pairs={{1,0},{2,1},{3,2},{4,3},{5,4},{6,5},{7,6},{8,7},{9,8},{10,9},{11,1... | collective-permute-start | bytes 2359304 | tf_op jit(solution)/shard_map/ppermute | solution.py:25
  101.1 25.3 %collective-permute-start = (bf16[512,768]{1,0:T(8,128)(2,1)}, bf16[512,768]{1,0:T(8,128)(2,1)S(1)}, u32[]{:S(2)}, u32[]{:S(2)}) collective-permute-start(bf16[512,768]{1,0:T(8,128)(2,1)} %pad_maximum_fusion.3), channel_id=1, source_target_pairs={{0,1},{1,2},{2,3},{3,4},{4,5},{5,6},{6,7},{7,8},{8,9},{9,10},{10,1... | collective-permute-start | bytes 2359304 | tf_op jit(solution)/shard_map/ppermute | solution.py:22
  192.9 6.1 copy-start.41
  192.9 48.3 %copy-start.40 = (bf16[2,24]{1,0:T(2,128)(2,1)S(1)}, bf16[2,24]{1,0:T(2,128)(2,1)}, u32[]{:S(2)}) copy-start(bf16[2,24]{1,0:T(2,128)(2,1)} %param.23) | copy-start | bytes 292
  193.4 89.3 %copy-start.14 = (bf16[1,256,768]{2,1,0:T(8,128)(2,1)S(1)}, bf16[1,256,768]{2,1,0:T(8,128)(2,1)}, u32[]{:S(2)}) copy-start(bf16[1,256,768]{2,1,0:T(8,128)(2,1)} %param.17) | copy-start | bytes 1179652
  193.4 89.3 %copy-start.29 = (f32[768]{0:T(1024)S(1)}, f32[768]{0:T(1024)}, u32[]{:S(2)}) copy-start(f32[768]{0:T(1024)} %get-tuple-element.537) | copy-start | bytes 9220
  195.5 86.1 %all-to-all-start.1 = ((bf16[2,2,49152]{2,1,0:T(2,128)(2,1)}), bf16[2,2,49152]{2,1,0:T(2,128)(2,1)S(1)}, u32[]{:S(2)}, u32[]{:S(2)}) async-start(bf16[2,2,49152]{2,1,0:T(2,128)(2,1)} %reshape.362), calls=%async_computation.1 | async-start | bytes 786432 | tf_op jit(solution)/shard_map/all_to_all | solution.py:200
  281.5 51.2 %copy-start.19 = (f32[768]{0:T(1024)}, f32[768]{0:T(1024)S(1)}, u32[]{:S(2)}) copy-start(f32[768]{0:T(1024)S(1)} %get-tuple-element.543) | copy-start | bytes 9220
  281.5 3.3 copy-start.21
  284.6 48.2 %copy-start.1 = (f32[256,768]{1,0:T(8,128)}, f32[256,768]{1,0:T(8,128)S(1)}, u32[]{:S(2)}) copy-start(f32[256,768]{1,0:T(8,128)S(1)} %get-tuple-element.633) | copy-start | bytes 2359300
  284.6 48.1 %copy-start.23 = (f32[256]{0:T(256)}, f32[256]{0:T(256)S(1)}, u32[]{:S(2)}) copy-start(f32[256]{0:T(256)S(1)} %broadcast_multiply_fusion.1) | copy-start | bytes 3076
  284.8 47.9 %copy-start.30 = (f32[256]{0:T(256)}, f32[256]{0:T(256)S(1)}, u32[]{:S(2)}) copy-start(f32[256]{0:T(256)S(1)} %fusion.124) | copy-start | bytes 3076
  284.9 35.7 %copy-start.35 = (f32[768]{0:T(1024)S(1)}, f32[768]{0:T(1024)}, u32[]{:S(2)}) copy-start(f32[768]{0:T(1024)} %get-tuple-element.535) | copy-start | bytes 9220
  296.3 28.3 %copy-start.11 = (bf16[256,3072]{1,0:T(8,128)(2,1)}, bf16[256,3072]{1,0:T(8,128)(2,1)S(1)}, u32[]{:S(2)}) copy-start(bf16[256,3072]{1,0:T(8,128)(2,1)S(1)} %get-tuple-element.613) | copy-start | bytes 4718596
  320.5 7.1 slice-start.2
  320.5 4.3 copy-start.6
  320.5 5.3 copy-start.28
  320.5 7.1 slice-start.3
  320.5 7.1 copy-start.43
  324.5 3.1 copy-start.42
  326.9 3.5 slice-start
  327.7 2.8 copy-start.12
  327.7 2.8 slice-start.1
  330.4 2.3 copy-start.18
  332.7 2.0 copy-start.5
  333.1 14.5 %copy-start.10 = (f32[256,768]{1,0:T(8,128)}, f32[256,768]{1,0:T(8,128)S(1)}, u32[]{:S(2)}) copy-start(f32[256,768]{1,0:T(8,128)S(1)} %get-tuple-element.610) | copy-start | bytes 2359300
  333.1 14.5 %copy-start.36 = (f32[256]{0:T(256)}, f32[256]{0:T(256)S(1)}, u32[]{:S(2)}) copy-start(f32[256]{0:T(256)S(1)} %negate_multiply_fusion.1) | copy-start | bytes 3076
  336.2 9.9 all-to-all-start.2
  339.6 372.3 %reduce-scatter.16.cloned.1.call-start = ((), (), s32[]{:S(2)}) async-start(), calls=%async_computation.17 | async-start | bytes 6684672 | tf_op jit(solution)/shard_map/reduce_scatter | solution.py:317
  359.7 4.5 copy-start
  399.8 4.5 copy-start
  439.9 4.5 copy-start
  480.0 4.5 copy-start
  520.2 4.5 copy-start
  560.3 4.5 copy-start
  589.5 3.0 copy-start.3
  589.5 188.5 %reduce-scatter.10.cloned.1.call-start = ((), (), s32[]{:S(2)}) async-start(), calls=%async_computation.14 | async-start | bytes 2433024 | tf_op jit(solution)/shard_map/reduce_scatter | solution.py:310
  592.4 310.0 %reduce-scatter.18.cloned.1.call-start = ((), (), s32[]{:S(2)}) async-start(), calls=%async_computation.18 | async-start | bytes 7299072
  594.5 21.6 %copy-start.4 = (f32[6,1536,64]{1,2,0:T(8,128)S(1)}, f32[6,1536,64]{1,2,0:T(8,128)}, u32[]{:S(2)}) copy-start(f32[6,1536,64]{1,2,0:T(8,128)} %get-tuple-element.162) | copy-start | bytes 7077892
  594.6 21.5 %collective-permute-start.3 = (bf16[512,768]{0,1:T(8,128)(2,1)S(1)}, bf16[512,768]{0,1:T(8,128)(2,1)S(1)}, u32[]{:S(2)}, u32[]{:S(2)}) collective-permute-start(bf16[512,768]{0,1:T(8,128)(2,1)S(1)} %get-tuple-element.621), channel_id=1, source_target_pairs={{0,1},{1,2},{2,3},{3,4},{4,5},{5,6},{6,7},{7,8},{8,9},{9,10},{10,1... | collective-permute-start | bytes 2359304 | tf_op jit(solution)/shard_map/ppermute | solution.py:37
  598.8 17.7 %copy-start.16 = (bf16[6,512,64]{1,2,0:T(8,128)(2,1)S(1)}, bf16[6,512,64]{1,2,0:T(8,128)(2,1)}, u32[]{:S(2)}) copy-start(bf16[6,512,64]{1,2,0:T(8,128)(2,1)} %get-tuple-element.160) | copy-start | bytes 1179652
  598.8 17.3 %collective-permute-start.2 = (bf16[512,768]{0,1:T(8,128)(2,1)S(1)}, bf16[512,768]{0,1:T(8,128)(2,1)S(1)}, u32[]{:S(2)}, u32[]{:S(2)}) collective-permute-start(bf16[512,768]{0,1:T(8,128)(2,1)S(1)} %get-tuple-element.620), channel_id=1, source_target_pairs={{1,0},{2,1},{3,2},{4,3},{5,4},{6,5},{7,6},{8,7},{9,8},{10,9},{11,1... | collective-permute-start | bytes 2359304 | tf_op jit(solution)/shard_map/ppermute | solution.py:37
  645.1 1.1 copy-start.2
  645.1 1.1 copy-start.20
  645.1 1.1 copy-start.22
  645.1 1.1 copy-start.24
  645.1 1.1 copy-start.31
  645.2 399.4 %reduce-scatter.12.cloned.1.call-start = ((), (), s32[]{:S(2)}) async-start(), calls=%async_computation.15 | async-start | bytes 9732096 | tf_op jit(solution)/shard_map/reduce_scatter | solution.py:311
  652.9 532.5 %reduce-scatter.14.cloned.1.call-start = ((), (), s32[]{:S(2)}) async-start(), calls=%async_computation.16 | async-start | bytes 9732096 | tf_op jit(solution)/shard_map/reduce_scatter | solution.py:312
  660.4 1.1 copy-start.26
  660.4 1.1 copy-start.34
  660.4 1.1 copy-start.25
  660.4 1.2 copy-start.33
  660.4 1.5 copy-start.32
  660.4 47.2 %copy-start.37 = (f32[256]{0:T(256)S(1)}, f32[256]{0:T(256)}, u32[]{:S(2)}) copy-start(f32[256]{0:T(256)} %copy-done.36) | copy-start | bytes 3076
  707.6 4.3 copy-start.17
  707.6 4.3 copy-start.38
  (6 other events, 5.8 us)
Sparse Core Ops, SparseCore 0:
  10.9 62.6 all-gather.7
  76.3 56.8 all-gather.9
  136.2 53.1 all-gather.11
  192.1 62.8 all-gather.13
  257.8 62.6 all-gather.15
  589.6 84.2 reduce-scatter.15
  680.7 97.3 reduce-scatter.9
  784.3 118.1 reduce-scatter.17
  909.9 134.6 reduce-scatter.11
  1050.9 134.4 reduce-scatter.13
where the time goes:
time: 1210 us; the launch traced here: 1190 us
  waiting for transfers between devices  571 us (47%)
  matrix products  194 us (16%)
  blocking collectives  183 us (15%)
  other arithmetic  133 us (11%)
  local copies, waits for them, and re-layouts  71.7 us (6%)
  starting transfers between devices  23.1 us (2%)
  between operations  15.3 us (1%)
    reduce_scatter x1, waiting for transfers between devices, per_device(): lax.psum_scatter(grad_w_up, ('seq', 'fsdp'), scatter_dimension=0, tiled=T...  142 us
    reduce_scatter x1, waiting for transfers between devices, per_device(): lax.psum_scatter(grad_w_down, ('seq', 'fsdp'), scatter_dimension=0, tiled...  141 us
    unnamed x11, waiting for transfers between devices  127 us
    unnamed x2, blocking collectives  85.8 us
    dot_general x28, matrix products, right_dot(): lax.dot_general(left, right, (((1,), (1,)), ((), ())), preferred_element_...  78 us
    dot_general x22, matrix products, plain_dot(): return jnp.dot(left, right, preferred_element_type=jnp.float32)  69.1 us
    reduce_scatter x1, waiting for transfers between devices, per_device(): lax.psum_scatter(grad_w_out, ('seq', 'fsdp'), scatter_dimension=0, tiled=...  64.2 us
    scatter-add x6, other arithmetic, head_backward(): columns = jax.ops.segment_sum(lookup_grad.T, key_pos, num_segments=MPOS)  63 us
  transfers between devices with their start and end apart: 17, of which 12 were waited for; matrix products, arithmetic and copies ran while one was open for 11% of the time, Pallas kernels for 0%

commit v1 on v0

v1 whole, which is shorter than its diff:
```python
from functools import partial

import jax
import jax.numpy as jnp
from jax import lax
from jax.experimental import pallas as pl
from jax.experimental.pallas import tpu as pltpu
from jax.sharding import PartitionSpec as P

D = 768
FF = 3072
HEADS = 12
HDIM = 64
MPOS = 512
EPS = 1e-05
GROUP = 512
HALF = 256
WINDOW = 3 * GROUP
OWN = 384
CHUNK = 256
NEG = -1e30
BF = jnp.bfloat16
F32 = jnp.float32
HIGH = lax.Precision.HIGHEST


def nn(left, right):
    return jnp.dot(left, right, preferred_element_type=F32)


def nt(left, right, precision=None):
    return lax.dot_general(
        left, right, (((1,), (1,)), ((), ())), precision=precision, preferred_element_type=F32
    )


def tn(left, right):
    return lax.dot_general(left, right, (((0,), (0,)), ((), ())), preferred_element_type=F32)


def load_projection(scal, parts, w, sem):
    copies = []
    for cr in range(2):
        for ur in range(8):
            row = (scal[1] ^ cr) * OWN + (ur ^ scal[0]) * 48
            copies.append(
                pltpu.make_async_copy(
                    parts[cr].at[ur],
                    w.at[pl.ds(pl.multiple_of(row, 16), 48), :],
                    sem.at[cr * 8 + ur],
                )
            )
    for copy in copies:
        copy.start()
    return copies


def load_table(scal, parts, table, sem):
    copies = []
    for cr in range(2):
        for ur in range(8):
            row = (2 * (ur ^ scal[0]) + (scal[1] ^ cr)) * 32
            copies.append(
                pltpu.make_async_copy(
                    parts[cr].at[ur],
                    table.at[:, pl.ds(pl.multiple_of(row, 32), 32), :],
                    sem.at[cr * 8 + ur],
                )
            )
    for copy in copies:
        copy.start()
    return copies


def project_kernel(
    scal, x1, x0, x2, y1, y0, y2, wa, wb, bias, q_ref, k_ref, v_ref, xg_ref, xw, w, sem
):
    copies = load_projection(scal, (wa, wb), w, sem)
    side = scal[2]
    for g, (mine, other) in enumerate(((x0, y0), (x1, y1), (x2, y2))):
        xw[pl.ds(pl.multiple_of(g * GROUP + side * HALF, HALF), HALF), :] = mine[...]
        xw[pl.ds(pl.multiple_of(g * GROUP + (1 - side) * HALF, HALF), HALF), :] = other[...]
    for copy in copies:
        copy.wait()
    for blk in range(6):
        rows = slice(blk * HALF, (blk + 1) * HALF)
        here = xw[rows, :]
        k_ref[rows, :] = nn(here, w[:, OWN : 2 * OWN]).astype(BF)
        v_ref[rows, :] = (nn(here, w[:, 2 * OWN :]) + bias[0:1, 2 * OWN :]).astype(BF)
        if blk in (2, 3):
            local = slice((blk - 2) * HALF, (blk - 1) * HALF)
            query = (nn(here, w[:, :OWN]) + bias[0:1, :OWN]).astype(BF)
            q_ref[local, :] = query * jnp.asarray(0.125, BF)
            xg_ref[local, :] = here


def head_lanes():
    return lax.broadcasted_iota(jnp.int32, (1, 128), 1) < HDIM


def fill_hot(pos_col, hot):
    for blk in range(6):
        rows = slice(blk * 256, (blk + 1) * 256)
        column = lax.broadcasted_iota(jnp.int32, (256, MPOS), 1)
        hot[rows, :] = jnp.where(pos_col[rows, :] == column, 1.0, 0.0).astype(BF)


def fill_hot_turned(pos_row, hot):
    for blk in range(6):
        rows = lax.broadcasted_iota(jnp.int32, (MPOS, 256), 0)
        hot[blk] = jnp.where(pos_row[blk] == rows, 1.0, 0.0).astype(BF)


def attend_kernel(
    scal, pos_col, doc_col, doc_row, q, k, v, ma, mb, ctx, lse, table, hot, sbuf, rbuf, acc, sem
):
    first = pl.program_id(0) == 0

    @pl.when(first)
    def _():
        copies = load_table(scal, (ma, mb), table, sem)
        fill_hot(pos_col, hot)
        for copy in copies:
            copy.wait()

    low = head_lanes()
    pair = pl.program_id(0)
    for qb in range(2):
        lo, hi = scal[3 + 2 * qb], scal[4 + 2 * qb]
        q_pair = q[qb * HALF : (qb + 1) * HALF, :]
        q_doc = doc_col[GROUP + qb * HALF : GROUP + (qb + 1) * HALF, :]
        q_hot = hot[GROUP + qb * HALF : GROUP + (qb + 1) * HALF, :]
        outs, tops = [], []
        for h in range(2):
            keep = low if h == 0 else jnp.logical_not(low)
            q_one = jnp.where(keep, q_pair, jnp.zeros_like(q_pair))
            rbuf[...] = nn(q_hot, table[2 * pair + h]).astype(BF)

            def score_step(c, top, q_one=q_one, q_doc=q_doc):
                rows = pl.ds(pl.multiple_of(c * CHUNK, CHUNK), CHUNK)
                s = jnp.where(q_doc == doc_row[c], nt(q_one, k[rows, :]), NEG)
                sbuf[c] = s
                return jnp.maximum(top, jnp.max(s, axis=1, keepdims=True))

            top = lax.fori_loop(lo, hi, score_step, jnp.full((HALF, 1), NEG, F32))
            acc[...] = jnp.zeros_like(acc)

            def mix_step(c, total, top=top):
                rows = pl.ds(pl.multiple_of(c * CHUNK, CHUNK), CHUNK)
                e = jnp.exp(sbuf[c] - top)
                lookup = nt(rbuf[...], hot[rows, :])
                acc[...] += nn((e * lookup).astype(BF), v[rows, :])
                return total + jnp.sum(e, axis=1, keepdims=True)

            total = lax.fori_loop(lo, hi, mix_step, jnp.zeros((HALF, 1), F32))
            outs.append(acc[...] / total)
            tops.append(top + jnp.log(total))
        ctx[scal[2] ^ qb] = jnp.where(low, outs[0], outs[1]).astype(BF)
        lane = lax.broadcasted_iota(jnp.int32, (1, 128), 1)
        both = jnp.where(lane == 0, tops[0], jnp.where(lane == 1, tops[1], 0.0))
        lse[0, :, qb * HALF : (qb + 1) * HALF] = both.T[0:8, :]


def attend_back_kernel(
    scal,
    pos_col,
    pos_row,
    doc_col,
    doc_row,
    q,
    k,
    v,
    ma,
    mb,
    ctx,
    dctx_mine,
    dctx_other,
    lse,
    dq,
    own,
    halo,
    grad_table,
    table,
    hot,
    hot_turned,
    rbuf,
    dk,
    dv,
    dq_acc,
    tt,
    tg,
    sem,
):
    pair = pl.program_id(0)

    @pl.when(pair == 0)
    def _():
        copies = load_table(scal, (ma, mb), table, sem)
        fill_hot(pos_col, hot)
        fill_hot_turned(pos_row, hot_turned)
        for copy in copies:
            copy.wait()

    low = head_lanes()
    side = scal[2]
    dk[...] = jnp.zeros_like(dk)
    dv[...] = jnp.zeros_like(dv)
    lane = lax.broadcasted_iota(jnp.int32, (8, 128), 1)
    row8 = lax.broadcasted_iota(jnp.int32, (8, 128), 0)
    pick = jnp.where((lane < HDIM) == (row8 == 0), 1.0, 0.0)
    for qb in range(2):
        lo, hi = scal[3 + 2 * qb], scal[4 + 2 * qb]
        q_pair = q[qb * HALF : (qb + 1) * HALF, :]
        d_pair = jnp.where(side == qb, dctx_mine[...], dctx_other[...])
        c_pair = ctx[side ^ qb]
        deltas = nt(pick, d_pair.astype(F32) * c_pair.astype(F32), HIGH)
        q_doc = doc_row[2 + qb]
        q_hot = hot[GROUP + qb * HALF : GROUP + (qb + 1) * HALF, :]
        for h in range(2):
            keep = low if h == 0 else jnp.logical_not(low)
            q_one = jnp.where(keep, q_pair, jnp.zeros_like(q_pair))
            d_one = jnp.where(keep, d_pair, jnp.zeros_like(d_pair))
            delta = deltas[h : h + 1, :]
            top = lse[0, h : h + 1, qb * HALF : (qb + 1) * HALF]
            rbuf[...] = nn(q_hot, table[2 * pair + h]).astype(BF)
            dq_acc[h] = jnp.zeros((HALF, 128), F32)
            tt[...] = jnp.zeros_like(tt)

            def step(c, carry, q_one=q_one, d_one=d_one, delta=delta, top=top, q_doc=q_doc, h=h):
                rows = pl.ds(pl.multiple_of(c * CHUNK, CHUNK), CHUNK)
                k_c = k[rows, :]
                s = nt(k_c, q_one)
                p = jnp.exp(jnp.where(doc_col[rows, :] == q_doc, s - top, NEG))
                lookup = nt(hot[rows, :], rbuf[...])
                dm = nt(v[rows, :], d_one)
                mixed = p * lookup
                dlook = p * dm
                ds = (mixed * dm - p * delta).astype(BF)
                dv[rows, :] += nn(mixed.astype(BF), d_one)
                dk[rows, :] += nn(ds, q_one)
                dq_acc[h] += tn(ds, k_c)
                tt[...] += nn(hot_turned[c], dlook.astype(BF))
                return carry

            lax.fori_loop(lo, hi, step, 0)
            piece = nt(hot_turned[2 + qb], tt[...].astype(BF))
            if qb == 0:
                tg[h] = piece
            else:
                tg[h] += piece
        dq[qb * HALF : (qb + 1) * HALF, :] = (
            jnp.where(low, dq_acc[0], dq_acc[1]) * 0.125
        ).astype(BF)
    own[0] = dk[GROUP : 2 * GROUP, :]
    own[1] = dv[GROUP : 2 * GROUP, :]
    halo[0, 0] = dk[:GROUP, :].astype(BF)
    halo[0, 1] = dv[:GROUP, :].astype(BF)
    halo[1, 0] = dk[2 * GROUP :, :].astype(BF)
    halo[1, 1] = dv[2 * GROUP :, :].astype(BF)
    for h in range(2):
        for cr in range(2):
            for t in range(8):
                ur = (t >> 2) | (t & 2) | ((t & 1) << 2)
                row = (2 * (ur ^ scal[0]) + (scal[1] ^ cr)) * 32
                grad_table[cr, t, h] = tg[h, pl.ds(pl.multiple_of(row, 32), 32), :].astype(BF)


def norm_stats(values):
    center = values - jnp.mean(values, axis=-1, keepdims=True)
    rstd = lax.rsqrt(jnp.mean(center * center, axis=-1, keepdims=True) + EPS)
    return center * rstd, rstd


def norm_back(grad, unit, rstd, gain):
    scaled = grad * gain
    return rstd * (
        scaled
        - jnp.mean(scaled, axis=-1, keepdims=True)
        - unit * jnp.mean(scaled * unit, axis=-1, keepdims=True)
    )


def column_sum(values):
    return jnp.sum(values, axis=0, keepdims=True)


def ffn_kernel(
    scal,
    x,
    ctx_mine,
    ctx_other,
    cot,
    small,
    bup,
    wg,
    lay,
    dh1,
    dctx,
    act,
    ddown,
    nlow,
    dup,
    ctxt,
    dattn,
    sums,
    wm,
    wu,
    wd,
    slope,
    hidden,
    sem,
):
    copies = []
    n = 0
    for c in range(2):
        for piece, (r, l) in enumerate(((192, 0), (192, OWN), (208, 0))):
            copies.append(
                pltpu.make_async_copy(
                    wg.at[:, c, r : r + 16, l : l + OWN],
                    wm.at[:, piece * 16 : piece * 16 + 16, c * OWN : (c + 1) * OWN],
                    sem.at[n],
                )
            )
            n += 1
    for c in range(2):
        for j in range(2):
            copies.append(
                pltpu.make_async_copy(
                    wg.at[:, c, 96 + 48 * j : 144 + 48 * j, :], wu.at[2 * c + j], sem.at[n]
                )
            )
            n += 1
    for c in range(2):
        copies.append(pltpu.make_async_copy(wg.at[:, c, 0:96, :], wd.at[:, c], sem.at[n]))
        n += 1
    for copy in copies:
        copy.start()
    even = scal[2] == 0
    mine, other = ctx_mine[...], ctx_other[...]
    ctxt[:, :OWN] = jnp.where(even, mine, other)
    ctxt[:, OWN:] = jnp.where(even, other, mine)
    for copy in copies[:6]:
        copy.wait()
    merge = wm[...].reshape(D, D)
    h1 = x[...].astype(F32) + (nn(ctxt[...], merge) + small[0:1, :])
    unit1, rstd1 = norm_stats(h1)
    normed = unit1 * small[4:5, :] + small[2:3, :]
    nlow[...] = normed.astype(BF)
    hidden[...] = normed + small[1:2, :]
    for copy in copies[6:]:
        copy.wait()

    def widen(i, carry):
        up = nn(nlow[...], wu[i].reshape(D, D)) + bup[i]
        half_cdf = 0.5 * (1.0 + lax.erf(up * 0.7071067811865476))
        act[i] = (up * half_cdf).astype(BF)
        slope[i] = half_cdf + up * (0.3989422804014327 * jnp.exp(-0.5 * up * up))
        return carry

    lax.fori_loop(0, 4, widen, 0)

    def shrink(i, carry):
        rows = wd[pl.ds(4 * i, 4)].reshape(D, D)
        hidden[...] += nn(act[i], rows)
        return carry

    lax.fori_loop(0, 4, shrink, 0)
    unit2, rstd2 = norm_stats(hidden[...])
    gain2 = small[5:6, :]
    lay[...] = (unit2 * gain2 + small[3:4, :]).astype(BF)
    dy = cot[...].astype(F32)
    sums[3:4, :] = column_sum(dy)
    sums[5:6, :] = column_sum(dy * unit2)
    dh2 = norm_back(dy, unit2, rstd2, gain2)
    ddown[...] = dh2.astype(BF)
    sums[1:2, :] = column_sum(ddown[...].astype(F32))
    hidden[...] = dh2

    def back(i, carry):
        rows = wd[pl.ds(4 * i, 4)].reshape(D, D)
        grad = (nt(ddown[...], rows) * slope[i]).astype(BF)
        dup[i] = grad
        sums[pl.ds(8 + i, 1), :] = column_sum(grad.astype(F32))
        hidden[...] += nt(grad, wu[i].reshape(D, D))
        return carry

    lax.fori_loop(0, 4, back, 0)
    dnormed = hidden[...]
    sums[2:3, :] = column_sum(dnormed)
    sums[4:5, :] = column_sum(dnormed * unit1)
    grad1 = norm_back(dnormed, unit1, rstd1, small[4:5, :])
    dh1[...] = grad1
    low = grad1.astype(BF)
    dattn[...] = low
    sums[0:1, :] = column_sum(low.astype(F32))
    sums[6:8, :] = jnp.zeros((2, D), F32)
    sums[12:16, :] = jnp.zeros((4, D), F32)
    grad_ctx = nt(low, merge).astype(BF)
    left, right = grad_ctx[:, :OWN], grad_ctx[:, OWN:]
    dctx[0] = jnp.where(even, left, right)
    dctx[1] = jnp.where(even, right, left)


def weight_grad_kernel(act, ddown, nlow, dup, ctxt, dattn, out):
    for i in range(4):
        g = tn(act[i], ddown[...]).astype(BF)
        out[4 * i : 4 * i + 4, :, 0:96, :] = g.reshape(4, 2, 96, D)
    for i in range(4):
        g = tn(nlow[...], dup[i]).astype(BF).reshape(16, 48, D)
        out[:, i // 2, 96 + 48 * (i % 2) : 144 + 48 * (i % 2), :] = g
    g = tn(ctxt[...], dattn[...]).astype(BF).reshape(16, 48, D)
    for c in range(2):
        half = g[:, :, c * OWN : (c + 1) * OWN]
        out[:, c, 192:208, 0:OWN] = half[:, 0:16]
        out[:, c, 192:208, OWN:] = half[:, 16:32]
        out[:, c, 208:224, 0:OWN] = half[:, 32:48]
        out[:, c, 208:224, OWN:] = jnp.zeros((16, 16, OWN), BF)


def project_back_kernel(
    scal, xg, dq, own, left, right, dh1, wa, wb, gw, dx, dx_send, sums, w, dqkv, gbuf, sem
):
    copies = load_projection(scal, (wa, wb), w, sem)
    dqkv[:, :OWN] = dq[...]
    for i in range(2):
        total = own[i] + left[i].astype(F32) + right[i].astype(F32)
        dqkv[:, (1 + i) * OWN : (2 + i) * OWN] = total.astype(BF)
    grad = dqkv[...]
    sums[...] = jnp.broadcast_to(column_sum(grad.astype(F32)), sums.shape)
    gbuf[...] = tn(xg[...], grad)
    for cr in range(2):
        for t in range(8):
            ur = (t >> 2) | (t & 2) | ((t & 1) << 2)
            row = (scal[1] ^ cr) * OWN + (ur ^ scal[0]) * 48
            gw[cr, t] = gbuf[pl.ds(pl.multiple_of(row, 16), 48), :].astype(BF)
    for copy in copies:
        copy.wait()
    side = scal[2]
    mine = dqkv[pl.ds(pl.multiple_of(side * HALF, HALF), HALF), :]
    other = dqkv[pl.ds(pl.multiple_of((1 - side) * HALF, HALF), HALF), :]
    dx[...] = dh1[...] + nt(mine, w[...])
    dx_send[...] = nt(other, w[...]).astype(BF)


SMEM = pl.BlockSpec(memory_space=pltpu.SMEM)
VM = pl.BlockSpec(memory_space=pltpu.VMEM)
HBM = pl.BlockSpec(memory_space=pl.ANY)


def params(mib, **more):
    return pltpu.CompilerParams(vmem_limit_bytes=mib * 1024 * 1024, **more)


def cost(flops, moved, transcendentals=0):
    return pl.CostEstimate(
        flops=int(flops), bytes_accessed=int(moved), transcendentals=int(transcendentals)
    )


def shape(dims, kind):
    return jax.ShapeDtypeStruct(dims, kind)


def project(scal, pieces, wa, wb, bias):
    return pl.pallas_call(
        project_kernel,
        name="project",
        out_shape=(
            shape((GROUP, OWN), BF),
            shape((WINDOW, OWN), BF),
            shape((WINDOW, OWN), BF),
            shape((GROUP, D), BF),
        ),
        in_specs=[SMEM] + [VM] * 6 + [HBM] * 2 + [VM],
        out_specs=[VM] * 4,
        scratch_shapes=[
            pltpu.VMEM((WINDOW, D), BF),
            pltpu.VMEM((D, 3 * OWN), BF),
            pltpu.SemaphoreType.DMA((16,)),
        ],
        compiler_params=params(32),
        cost_estimate=cost(2 * WINDOW * D * 1000, 8e6),
    )(scal, *pieces, wa, wb, bias)


def attend(scal, pos_col, doc_col, doc_row, q, k, v, ma, mb):
    whole = lambda *dims: pl.BlockSpec(dims, lambda p: (0,) * len(dims))
    return pl.pallas_call(
        attend_kernel,
        name="attend",
        grid=(3,),
        out_shape=(shape((2, HALF, OWN), BF), shape((3, 8, GROUP), F32)),
        in_specs=[
            SMEM,
            whole(WINDOW, 1),
            whole(WINDOW, 1),
            whole(6, 1, CHUNK),
            pl.BlockSpec((GROUP, 128), lambda p: (0, p)),
            pl.BlockSpec((WINDOW, 128), lambda p: (0, p)),
            pl.BlockSpec((WINDOW, 128), lambda p: (0, p)),
            HBM,
            HBM,
        ],
        out_specs=[
            pl.BlockSpec((2, HALF, 128), lambda p: (0, 0, p)),
            pl.BlockSpec((1, 8, GROUP), lambda p: (p, 0, 0)),
        ],
        scratch_shapes=[
            pltpu.VMEM((6, MPOS, MPOS), BF),
            pltpu.VMEM((WINDOW, MPOS), BF),
            pltpu.VMEM((6, HALF, CHUNK), F32),
            pltpu.VMEM((HALF, MPOS), BF),
            pltpu.VMEM((HALF, 128), F32),
            pltpu.SemaphoreType.DMA((16,)),
        ],
        compiler_params=params(32),
        cost_estimate=cost(20e9, 10e6, 5e6),
    )(scal, pos_col, doc_col, doc_row, q, k, v, ma, mb)


def attend_back(scal, pos_col, pos_row, doc_col, doc_row, q, k, v, ma, mb, ctx, mine, other, lse):
    whole = lambda *dims: pl.BlockSpec(dims, lambda p: (0,) * len(dims))
    return pl.pallas_call(
        attend_back_kernel,
        name="attend_back",
        grid=(3,),
        out_shape=(
            shape((GROUP, OWN), BF),
            shape((2, GROUP, OWN), F32),
            shape((2, 2, GROUP, OWN), BF),
            shape((2, 8, 6, 32, MPOS), BF),
        ),
        in_specs=[
            SMEM,
            whole(WINDOW, 1),
            whole(6, 1, CHUNK),
            whole(WINDOW, 1),
            whole(6, 1, CHUNK),
            pl.BlockSpec((GROUP, 128), lambda p: (0, p)),
            pl.BlockSpec((WINDOW, 128), lambda p: (0, p)),
            pl.BlockSpec((WINDOW, 128), lambda p: (0, p)),
            HBM,
            HBM,
            pl.BlockSpec((2, HALF, 128), lambda p: (0, 0, p)),
            pl.BlockSpec((HALF, 128), lambda p: (0, p)),
            pl.BlockSpec((HALF, 128), lambda p: (0, p)),
            pl.BlockSpec((1, 8, GROUP), lambda p: (p, 0, 0)),
        ],
        out_specs=[
            pl.BlockSpec((GROUP, 128), lambda p: (0, p)),
            pl.BlockSpec((2, GROUP, 128), lambda p: (0, 0, p)),
            pl.BlockSpec((2, 2, GROUP, 128), lambda p: (0, 0, 0, p)),
            pl.BlockSpec((2, 8, 2, 32, MPOS), lambda p: (0, 0, p, 0, 0)),
        ],
        scratch_shapes=[
            pltpu.VMEM((6, MPOS, MPOS), BF),
            pltpu.VMEM((WINDOW, MPOS), BF),
            pltpu.VMEM((6, MPOS, CHUNK), BF),
            pltpu.VMEM((HALF, MPOS), BF),
            pltpu.VMEM((WINDOW, 128), F32),
            pltpu.VMEM((WINDOW, 128), F32),
            pltpu.VMEM((2, HALF, 128), F32),
            pltpu.VMEM((MPOS, HALF), F32),
            pltpu.VMEM((2, MPOS, MPOS), F32),
            pltpu.SemaphoreType.DMA((16,)),
        ],
        compiler_params=params(40),
        cost_estimate=cost(50e9, 20e6, 5e6),
    )(scal, pos_col, pos_row, doc_col, doc_row, q, k, v, ma, mb, ctx, mine, other, lse)


def feed_forward(scal, x, mine, other, cot, small, bup, wg):
    return pl.pallas_call(
        ffn_kernel,
        name="feed_forward",
        out_shape=(
            shape((HALF, D), BF),
            shape((HALF, D), F32),
            shape((2, HALF, OWN), BF),
            shape((4, HALF, D), BF),
            shape((HALF, D), BF),
            shape((HALF, D), BF),
            shape((4, HALF, D), BF),
            shape((HALF, D), BF),
            shape((HALF, D), BF),
            shape((16, D), F32),
        ),
        in_specs=[SMEM] + [VM] * 6 + [HBM],
        out_specs=[VM] * 10,
        scratch_shapes=[
            pltpu.VMEM((16, 48, D), BF),
            pltpu.VMEM((4, 16, 48, D), BF),
            pltpu.VMEM((16, 2, 96, D), BF),
            pltpu.VMEM((4, HALF, D), F32),
            pltpu.VMEM((HALF, D), F32),
            pltpu.SemaphoreType.DMA((12,)),
        ],
        compiler_params=params(50),
        cost_estimate=cost(6e9, 20e6, 2e6),
    )(scal, x, mine, other, cot, small, bup, wg)


def weight_grads(act, ddown, nlow, dup, ctxt, dattn):
    return pl.pallas_call(
        weight_grad_kernel,
        name="weight_grads",
        out_shape=shape((16, 2, 224, D), BF),
        in_specs=[VM] * 6,
        out_specs=VM,
        compiler_params=params(50),
        cost_estimate=cost(3e9, 15e6),
    )(act, ddown, nlow, dup, ctxt, dattn)


def project_back(scal, xg, dq, own, left, right, dh1, wa, wb):
    return pl.pallas_call(
        project_back_kernel,
        name="project_back",
        out_shape=(
            shape((2, 8, 48, 3 * OWN), BF),
            shape((HALF, D), F32),
            shape((HALF, D), BF),
            shape((8, 3 * OWN), F32),
        ),
        in_specs=[SMEM] + [VM] * 6 + [HBM] * 2,
        out_specs=[VM] * 4,
        scratch_shapes=[
            pltpu.VMEM((D, 3 * OWN), BF),
            pltpu.VMEM((GROUP, 3 * OWN), BF),
            pltpu.VMEM((D, 3 * OWN), F32),
            pltpu.SemaphoreType.DMA((16,)),
        ],
        compiler_params=params(40),
        cost_estimate=cost(2e9, 12e6),
    )(scal, xg, dq, own, left, right, dh1, wa, wb)


def swap(value, axis, bit):
    count = lax.axis_size(axis)
    return lax.ppermute(value, axis, [(i, i ^ bit) for i in range(count)])


def shifted(value, axis, steps):
    count = lax.axis_size(axis)
    leading, last = (max(0, -steps), min(count, count - steps))
    return lax.ppermute(value, axis, [(source, source + steps) for source in range(leading, last)])


def gather_steps(value, steps):
    for axis, bit in steps:
        value = jnp.stack([value, swap(value, axis, bit)], axis=0)
    return value


def reduce_steps(value, steps):
    for axis, bit in steps:
        got = swap(value[1], axis, bit)
        value = (value[0].astype(F32) + got.astype(F32)).astype(value.dtype)
    return value


def by_core(core, mine, other, axis):
    first = jnp.where(core == 0, mine, other)
    second = jnp.where(core == 0, other, mine)
    return jnp.concatenate([first, second], axis=axis)


def locate(index, opening, finish, stream_rows):
    document = jnp.sum((finish[None, :] <= index[:, None]).astype(jnp.int32), axis=1)
    begin = jnp.max(jnp.where(opening[None, :] <= index[:, None], opening[None, :], 0), axis=1)
    inside = (index >= 0) & (index < stream_rows)
    document = jnp.where(inside, document, -1)
    position = (index - begin) % MPOS
    return document, position


def per_device(
    incoming_state,
    projection_matrix_triple,
    merge_matrix,
    widen_matrix,
    shrink_matrix,
    offset_table,
    norm_scales,
    widen_offset,
    trainable_gate_scores,
    gate_perturbation,
    softening_scale,
    passage_extents,
    result_cotangent,
):
    BOTH = ("seq", "fsdp")
    ns, nf = lax.axis_size("seq"), lax.axis_size("fsdp")
    count = ns * nf
    fast = nf == 16
    side, place = lax.axis_index("seq"), lax.axis_index("fsdp")
    tokens = incoming_state.reshape(HALF, D)
    cot = result_cotangent.reshape(HALF, D)
    stream_rows = GROUP * nf
    rows = projection_matrix_triple.shape[0]

    before = shifted(tokens, "fsdp", 1)
    after = shifted(tokens, "fsdp", -1)
    other_tokens = swap(tokens, "seq", 1)
    other_before = swap(before, "seq", 1)
    other_after = swap(after, "seq", 1)

    relaxed = jax.nn.sigmoid(
        (trainable_gate_scores + gate_perturbation) / softening_scale[:, None, None]
    )
    relaxed_low = relaxed.astype(BF)

    packed = jnp.concatenate(
        [offset_table.T.reshape(-1), norm_scales.T.reshape(-1), widen_offset]
    )
    heads_weight = projection_matrix_triple.reshape(rows, 3, 2, OWN)
    if fast:
        core = place % 2
        unit = place // 2
        own_cols = lax.dynamic_index_in_dim(heads_weight, side, 2, False).reshape(rows, 3 * OWN)
        sent_cols = lax.dynamic_index_in_dim(heads_weight, 1 - side, 2, False).reshape(
            rows, 3 * OWN
        )
        got_cols = swap(sent_cols, "seq", 1)
        for_me = jnp.where(core == side, own_cols, got_cols)
        for_core = jnp.where(core == side, got_cols, own_cols)
        wq = by_core(core, for_me, swap(for_core, "fsdp", 1), 0)
        wq = gather_steps(wq, (("fsdp", 8), ("fsdp", 4), ("fsdp", 2)))
        wa = wq.transpose(2, 1, 0, 3, 4).reshape(8, 48, 3 * OWN)
        wb = swap(wa, "fsdp", 1)
        ma = gather_steps(relaxed_low, (("fsdp", 8), ("fsdp", 4), ("fsdp", 2)))
        ma = ma.transpose(2, 1, 0, 3, 4, 5).reshape(8, 6, 32, MPOS)
        mb = swap(ma, "fsdp", 1)
        me = side * 16 + place
        small_rel = gather_steps(
            packed[None, :],
            (("fsdp", 1), ("fsdp", 2), ("fsdp", 4), ("fsdp", 8), ("seq", 1)),
        ).reshape(count, -1)
        index = jnp.arange(count, dtype=jnp.int32)
        turn = ((index[:, None] ^ me) == index[None, :]).astype(BF)
        small_all = jnp.dot(turn, small_rel, preferred_element_type=F32)
        wide = jnp.concatenate([widen_matrix.reshape(rows, 2, FF // 2), merge_matrix.reshape(rows, 2, OWN)], axis=2)
        mine = lax.dynamic_index_in_dim(wide, core, 1, False)
        sent = lax.dynamic_index_in_dim(wide, 1 - core, 1, False)
        wide = by_core(core, mine, swap(sent, "fsdp", 1), 0)
        merged = wide[:, FF // 2 :]
        shard = jnp.concatenate(
            [
                shrink_matrix,
                wide[:, :D],
                wide[:, D : 2 * D],
                jnp.concatenate([merged[0:16], merged[16:32]], axis=1),
                jnp.concatenate([merged[32:48], jnp.zeros((16, OWN), BF)], axis=1),
            ],
            axis=0,
        )
        wg = lax.all_gather(shard, BOTH, axis=0, tiled=True).reshape(16, 2, 224, D)
    else:
        core = jnp.zeros((), jnp.int32)
        unit = jnp.zeros((), jnp.int32)
        full = lax.all_gather(projection_matrix_triple, BOTH, axis=0, tiled=True)
        full = lax.dynamic_index_in_dim(full.reshape(D, 3, 2, OWN), side, 2, False)
        full = full.reshape(2, 8, 48, 3 * OWN)
        wa, wb = full[0], full[1]
        table = lax.all_gather(relaxed_low, "fsdp", axis=1, tiled=True)
        table = table.reshape(6, 8, 2, 32, MPOS).transpose(2, 1, 0, 3, 4)
        ma, mb = table[0], table[1]
        small_all = lax.all_gather(packed, BOTH, axis=0, tiled=True).reshape(count, -1).astype(F32)
        up = lax.all_gather(widen_matrix, BOTH, axis=0, tiled=True)
        up = up.reshape(16, 48, 2, 2, D).transpose(0, 2, 3, 1, 4).reshape(16, 2, 96, D)
        down = lax.all_gather(shrink_matrix, BOTH, axis=0, tiled=True).reshape(16, 2, 96, D)
        out = lax.all_gather(merge_matrix, BOTH, axis=0, tiled=True)
        out = out.reshape(16, 3, 16, 2, OWN).transpose(0, 3, 1, 2, 4)
        out = jnp.concatenate([out, jnp.zeros((16, 2, 1, 16, OWN), BF)], axis=2)
        out = out.reshape(16, 2, 2, 2, 16, OWN).transpose(0, 1, 2, 4, 3, 5).reshape(16, 2, 32, D)
        wg = jnp.concatenate([down, up, out], axis=2)
    wide_cols = D // count
    biases = small_all[:, : 6 * wide_cols].reshape(D, 6)
    gains = small_all[:, 6 * wide_cols : 8 * wide_cols].reshape(D, 2)
    bup = small_all[:, 8 * wide_cols :].reshape(4, 1, D)
    small = jnp.concatenate([biases[:, 2:].T, gains.T, jnp.zeros((2, D), F32)], axis=0)
    head_bias = lax.dynamic_slice_in_dim(biases[:, :2], side * OWN, OWN, 0)
    qkv_bias = jnp.concatenate(
        [head_bias[:, 0], jnp.zeros((OWN,), F32), head_bias[:, 1]]
    ).reshape(1, 3 * OWN)

    finish = jnp.cumsum(passage_extents)
    opening = finish - passage_extents
    base = place * GROUP - GROUP
    doc, pos = locate(
        base + jnp.arange(WINDOW, dtype=jnp.int32), opening, finish, stream_rows
    )
    edges = base + GROUP + jnp.asarray([0, HALF - 1, HALF, GROUP - 1], jnp.int32)
    edge_begin = jnp.max(jnp.where(opening[None, :] <= edges[:, None], opening[None, :], 0), axis=1)
    edge_end = jnp.min(
        jnp.where(finish[None, :] > edges[:, None], finish[None, :], stream_rows), axis=1
    )
    lows = jnp.clip((edge_begin - base) // CHUNK, 0, 6)
    highs = jnp.clip((edge_end - base + CHUNK - 1) // CHUNK, 0, 6)
    scal = jnp.stack([unit, core, side, lows[0], highs[1], lows[2], highs[3], core]).astype(
        jnp.int32
    )
    pos_col, doc_col = pos.reshape(WINDOW, 1), doc.reshape(WINDOW, 1)
    pos_row, doc_row = pos.reshape(6, 1, CHUNK), doc.reshape(6, 1, CHUNK)

    pieces = (tokens, before, after, other_tokens, other_before, other_after)
    q, k, v, group_tokens = project(scal, pieces, wa, wb, qkv_bias)
    ctx, lse = attend(scal, pos_col, doc_col, doc_row, q, k, v, ma, mb)
    ctx_other = swap(ctx[1], "seq", 1)
    (lay, dh1, dctx, act, ddown, nlow, dup, ctxt, dattn, sums) = feed_forward(
        scal, tokens, ctx[0], ctx_other, cot, small, bup, wg
    )
    dctx_other = swap(dctx[1], "seq", 1)
    gg = weight_grads(act, ddown, nlow, dup, ctxt, dattn)
    dq, own, halo, grad_table = attend_back(
        scal, pos_col, pos_row, doc_col, doc_row, q, k, v, ma, mb, ctx, dctx[0], dctx_other, lse
    )
    from_right = shifted(halo[0], "fsdp", -1)
    from_left = shifted(halo[1], "fsdp", 1)
    gw, dx, dx_send, qkv_sums = project_back(
        scal, group_tokens, dq, own, from_left, from_right, dh1, wa, wb
    )
    input_grad = dx + swap(dx_send, "seq", 1).astype(F32)

    own_sums = jnp.stack([qkv_sums[0, :OWN], qkv_sums[0, 2 * OWN :]], axis=0)
    blank = jnp.zeros_like(own_sums)
    head_sums = jnp.concatenate(
        [jnp.where(side == 0, own_sums, blank), jnp.where(side == 0, blank, own_sums)], axis=1
    )
    bias_sums = jnp.concatenate([head_sums, sums[0:4]], axis=0)
    small_grads = jnp.concatenate(
        [
            bias_sums.reshape(6, count, wide_cols).transpose(1, 0, 2).reshape(count, -1),
            sums[4:6].reshape(2, count, wide_cols).transpose(1, 0, 2).reshape(count, -1),
            sums[8:12].reshape(count, FF // count),
        ],
        axis=1,
    )
    if fast:
        order = turn.astype(F32)
        small_grads = jnp.dot(order, small_grads, precision=HIGH, preferred_element_type=F32)
        small_mine = reduce_steps(
            small_grads.reshape(2, 2, 2, 2, 2, -1),
            (("seq", 1), ("fsdp", 8), ("fsdp", 4), ("fsdp", 2), ("fsdp", 1)),
        )
        shard = lax.psum_scatter(
            gg.reshape(32 * 224, D), BOTH, scatter_dimension=0, tiled=True
        )
        table_total = reduce_steps(
            grad_table.reshape(2, 2, 2, 2, 6, 32, MPOS),
            (("fsdp", 1), ("fsdp", 2), ("fsdp", 4), ("fsdp", 8)),
        ).astype(F32)
        own_rows = reduce_steps(
            gw.reshape(2, 2, 2, 2, 48, 3 * OWN),
            (("fsdp", 1), ("fsdp", 2), ("fsdp", 4), ("fsdp", 8)),
        ).reshape(2, rows, 3 * OWN)
        mine = lax.dynamic_index_in_dim(own_rows, core, 0, False)
        got = swap(lax.dynamic_index_in_dim(own_rows, 1 - core, 0, False), "fsdp", 1)
        to_keep = jnp.where(core == side, mine, got)
        to_send = jnp.where(core == side, got, mine)
        both = by_core(
            side,
            to_keep.reshape(rows, 3, 1, OWN),
            swap(to_send, "seq", 1).reshape(rows, 3, 1, OWN),
            2,
        )
        grad_w_qkv = both.reshape(rows, 3 * D).astype(F32)
        grad_w_down = shard[0:96].astype(F32)
        merged = jnp.concatenate(
            [shard[192:208, :OWN], shard[192:208, OWN:], shard[208:224, :OWN]], axis=0
        )
        wide = jnp.concatenate([shard[96:144], shard[144:192], merged], axis=1)
        wide = wide.reshape(2, rows, 2 * D + OWN)
        mine = lax.dynamic_index_in_dim(wide, core, 0, False)
        got = swap(lax.dynamic_index_in_dim(wide, 1 - core, 0, False), "fsdp", 1)
        grad_w_up = by_core(core, mine[:, : 2 * D], got[:, : 2 * D], 1).astype(F32)
        grad_w_out = by_core(core, mine[:, 2 * D :], got[:, 2 * D :], 1).astype(F32)
    else:
        scatter = partial(lax.psum_scatter, axis_name=BOTH, scatter_dimension=0, tiled=True)
        small_mine = scatter(small_grads.reshape(-1))
        table = grad_table.reshape(2, 2, 2, 2, 6, 32, MPOS).transpose(4, 3, 2, 1, 0, 5, 6)
        table_total = lax.psum_scatter(
            table.reshape(6, MPOS, MPOS), "fsdp", scatter_dimension=1, tiled=True
        ).astype(F32)
        head_rows = gw.reshape(2, 2, 2, 2, 48, 3, 1, OWN).transpose(0, 3, 2, 1, 4, 5, 6, 7)
        head_rows = head_rows.reshape(D, 3, 1, OWN)
        blank = jnp.zeros_like(head_rows)
        both = jnp.concatenate(
            [jnp.where(side == 0, head_rows, blank), jnp.where(side == 0, blank, head_rows)], axis=2
        )
        grad_w_qkv = scatter(both.reshape(D, 3 * D)).astype(F32)
        grad_w_down = scatter(gg[:, :, 0:96].reshape(FF, D)).astype(F32)
        wide = gg[:, :, 96:192].reshape(16, 2, 2, 48, D).transpose(0, 3, 1, 2, 4).reshape(D, FF)
        grad_w_up = scatter(wide).astype(F32)
        out = gg[:, :, 192:224].reshape(16, 2, 2, 16, 2, OWN).transpose(0, 1, 2, 4, 3, 5)
        out = out.reshape(16, 2, 4, 16, OWN)[:, :, :3].transpose(0, 2, 3, 1, 4).reshape(D, D)
        grad_w_out = scatter(out).astype(F32)
    grad_biases = small_mine[: 6 * wide_cols].reshape(6, wide_cols)
    grad_gains = small_mine[6 * wide_cols : 8 * wide_cols].reshape(2, wide_cols)
    grad_bias_up = small_mine[8 * wide_cols :]
    mask_logit_gradient = (
        table_total * relaxed * (1.0 - relaxed) / softening_scale[:, None, None]
    )
    return (
        lay.reshape(1, HALF, D),
        input_grad.reshape(1, HALF, D),
        grad_w_qkv,
        grad_w_out,
        grad_w_up,
        grad_w_down,
        grad_biases,
        grad_gains,
        grad_bias_up,
        mask_logit_gradient,
    )


def solution(mesh):
    rows = P(("seq", "fsdp"), None)
    columns = P(None, ("seq", "fsdp"))
    block = P("fsdp", "seq", None)
    table = P("seq", "fsdp", None)
    return jax.shard_map(
        per_device,
        mesh=mesh,
        in_specs=(
            block, rows, rows, rows, rows, columns, columns, P(("seq", "fsdp")),
            table, table, P("seq"), P(), block,
        ),
        out_specs=(
            block, block, rows, rows, rows, rows, columns, columns, P(("seq", "fsdp")), table,
        ),
        check_vma=False,
    )
```

time: 1210 us -> 441 us (0.36); the launches traced: 1190 us -> 440 us
  waiting for transfers between devices: 571 us -> 118 us
  matrix products: 194 us -> 0.43 us
  blocking collectives: 183 us -> 0 us
  other arithmetic: 133 us -> 15.2 us
  Pallas kernels: 0 us -> 115 us
  starting transfers between devices: 23.1 us -> 125 us
  local copies, waits for them, and re-layouts: 71.7 us -> 50.1 us
    reduce_scatter x4 -> x1, waiting for transfers between devices: 347 us -> 0.01 us  [per_device(): lax.psum_scatter(gg.reshape(32 * 224, D), BOTH, scatter_dimension=0, tile...]
    dot_general x66 -> x2, matrix products: 194 us -> 0.43 us  [the longest x1 0.24 us: per_device(): jnp.dot(order, small_grads, precision=HIGH, preferred_element_type=F32)]
    unnamed x11 -> x2, waiting for transfers between devices: 127 us -> 0.03 us
    pallas_call x0 -> x6, Pallas kernels: none -> 115 us  [the longest x1 38.2 us: attend_back(): pl.pallas_call(attend_back_kernel, name='attend_back', grid=(3,), out_sha...]
    ppermute x2 -> x38, starting transfers between devices: 5.96 us -> 113 us  [swap(): return lax.ppermute(value, axis, [(i, i ^ bit) for i in range(count)])]
    scatter-add x12 -> x0, other arithmetic: 86.7 us -> none  [the longest x6 63 us: head_backward(): columns = jax.ops.segment_sum(lookup_grad.T, key_pos, num_segments=MPOS)]
    unnamed x2 -> x0, blocking collectives: 85.8 us -> none
    all_gather x2 -> x0, blocking collectives: 83.6 us -> none  [the longest x1 43.5 us: per_device(): lax.all_gather(offsets_turned, ('seq', 'fsdp'), axis=0, tiled=True)]
  transfers between devices with their start and end apart: 17 -> 44, of which waited for: 12 -> 21; matrix products, arithmetic and copies ran while one was open for 11% -> 8% of each run, Pallas kernels for 0% -> 22%
where the time goes in v1:
time: 441 us; the launch traced here: 440 us
  starting transfers between devices  125 us (28%)
  waiting for transfers between devices  118 us (27%)
  Pallas kernels  115 us (26%)
  local copies, waits for them, and re-layouts  50.1 us (11%)
  other arithmetic  15.2 us (3%)
  between operations  15.2 us (3%)
    ppermute x38, starting transfers between devices, swap(): return lax.ppermute(value, axis, [(i, i ^ bit) for i in range(count)])  113 us
    ppermute x38, waiting for transfers between devices, swap(): return lax.ppermute(value, axis, [(i, i ^ bit) for i in range(count)])  92.5 us
    pallas_call x1, Pallas kernels, attend_back(): pl.pallas_call(attend_back_kernel, name='attend_back', grid=(3,), out_sha...  38.2 us
    pallas_call x1, Pallas kernels, attend(): pl.pallas_call(attend_kernel, name='attend', grid=(3,), out_shape=(shape(...  38 us
    unnamed x99, local copies, waits for them, and re-layouts  26.5 us
    ppermute x4, waiting for transfers between devices, shifted(): lax.ppermute(value, axis, [(source, source + steps) for source in range(l...  25.7 us
    pallas_call x1, Pallas kernels, feed_forward(): pl.pallas_call(ffn_kernel, name='feed_forward', out_shape=(shape((HALF, D...  16.7 us
    ppermute x4, starting transfers between devices, shifted(): lax.ppermute(value, axis, [(source, source + steps) for source in range(l...  12.3 us
  transfers between devices with their start and end apart: 44, of which 21 were waited for; matrix products, arithmetic and copies ran while one was open for 8% of the time, Pallas kernels for 22%

profile of v1, /device:TPU:1, one launch (start us, length us, event | category | flops | bytes accessed | tf_op | source)
XLA Modules:
  0.0 439.5 jit_solution(11717205648929307831)
XLA Ops:
  11.4 2.1 collective-permute-start.1
  13.5 4.4 collective-permute-start
  19.2 1.5 collective-permute-start.5
  21.7 2.3 collective-permute-start.16
  25.4 1.9 add_select_fusion
  29.0 8.6 %collective-permute-done.16 = bf16[6,32,512]{2,1,0:T(8,128)(2,1)S(1)} collective-permute-done((bf16[6,32,512]{2,1,0:T(8,128)(2,1)S(1)}, bf16[6,32,512]{2,1,0:T(8,128)(2,1)S(1)}, u32[]{:S(2)}, u32[]{:S(2)}) %collective-permute-start.16) | collective-permute-done | bytes 196640 | tf_op jit(solution)/shard_map/ppermute | solution.py:640
  38.5 4.2 collective-permute-start.7
  42.7 6.5 %collective-permute-done.17 = bf16[2,6,32,512]{3,2,1,0:T(8,128)(2,1)S(1)} collective-permute-done((bf16[2,6,32,512]{3,2,1,0:T(8,128)(2,1)S(1)}, bf16[2,6,32,512]{3,2,1,0:T(8,128)(2,1)S(1)}, u32[]{:S(2)}, u32[]{:S(2)}) %collective-permute-start.17) | collective-permute-done | bytes 393248 | tf_op jit(solution)/shard_map/ppermute | solution.py:640
  49.3 16.0 %collective-permute-start.18 = (bf16[2,2,6,32,512]{4,3,2,1,0:T(8,128)(2,1)S(1)}, bf16[2,2,6,32,512]{4,3,2,1,0:T(8,128)(2,1)S(1)}, u32[]{:S(2)}, u32[]{:S(2)}) collective-permute-start(bf16[2,2,6,32,512]{4,3,2,1,0:T(8,128)(2,1)S(1)} %get-tuple-element.77), channel_id=1, source_target_pairs={{0,2},{1,3},{2,0},{3,1},{4,6},{5,7},{6,4},{7,5},{8,10},{9,11},{10,... | collective-permute-start | bytes 2359304 | tf_op jit(solution)/shard_map/ppermute | solution.py:640
  66.7 2.7 stack.115.scal
  69.5 1.7 collective-permute-done.8
  72.2 2.5 collective-permute-start.9
  74.7 2.1 collective-permute-done.18
  77.1 23.0 %collective-permute-start.19 = (bf16[8,6,32,512]{3,2,1,0:T(8,128)(2,1)S(1)}, bf16[8,6,32,512]{3,2,1,0:T(8,128)(2,1)}, u32[]{:S(2)}, u32[]{:S(2)}) collective-permute-start(bf16[8,6,32,512]{3,2,1,0:T(8,128)(2,1)S(1)} %bitcast.167), channel_id=1, source_target_pairs={{0,1},{1,0},{2,3},{3,2},{4,5},{5,4},{6,7},{7,6},{8,9},{9,8},{10,11... | collective-permute-start | bytes 4718600 | tf_op jit(solution)/shard_map/ppermute | solution.py:640
  100.4 12.8 %collective-permute-start.10 = (bf16[8,48,1152]{2,1,0:T(8,128)(2,1)S(1)}, bf16[8,48,1152]{2,1,0:T(8,128)(2,1)}, u32[]{:S(2)}, u32[]{:S(2)}) collective-permute-start(bf16[8,48,1152]{2,1,0:T(8,128)(2,1)S(1)} %bitcast.170), channel_id=1, source_target_pairs={{0,1},{1,0},{2,3},{3,2},{4,5},{5,4},{6,7},{7,6},{8,9},{9,8},{10,11... | collective-permute-start | bytes 2654216 | tf_op jit(solution)/shard_map/ppermute | solution.py:640
  113.3 4.9 %collective-permute-done.14 = bf16[2,2,2,1,288]{4,2,1,3,0:T(2,128)(2,1)S(1)} collective-permute-done((bf16[2,2,2,1,288]{4,2,1,3,0:T(2,128)(2,1)S(1)}, bf16[2,2,2,1,288]{4,2,1,3,0:T(2,128)(2,1)S(1)}, u32[]{:S(2)}, u32[]{:S(2)}) %collective-permute-start.14) | collective-permute-done | bytes 4640 | tf_op jit(solution)/shard_map/ppermute | solution.py:640
  118.4 2.9 collective-permute-done.15
  121.3 1.5 collective-permute-start.4
  124.3 1.9 slice.300
  126.2 1.3 dynamic-slice_reduce_fusion.1
  129.6 1.8 copy.124
  131.4 8.1 %collective-permute-done.4.y2 = bf16[256,768]{1,0:T(8,128)(2,1)} collective-permute-done((bf16[256,768]{1,0:T(8,128)(2,1)}, bf16[256,768]{1,0:T(8,128)(2,1)}, u32[]{:S(2)}, u32[]{:S(2)}) %collective-permute-start.4) | collective-permute-done | bytes 393248 | tf_op jit(solution)/shard_map/ppermute | solution.py:640
  139.5 8.4 %collective-permute-done.3.y0 = bf16[256,768]{1,0:T(8,128)(2,1)} collective-permute-done((bf16[256,768]{1,0:T(8,128)(2,1)}, bf16[256,768]{1,0:T(8,128)(2,1)}, u32[]{:S(2)}, u32[]{:S(2)}) %collective-permute-start.3) | collective-permute-done | bytes 393248 | tf_op jit(solution)/shard_map/ppermute | solution.py:640
  147.9 7.2 %project.1 = (bf16[512,384]{1,0:T(8,128)(2,1)S(1)}, bf16[1536,384]{1,0:T(8,128)(2,1)S(1)}, bf16[1536,384]{1,0:T(8,128)(2,1)S(1)}, bf16[512,768]{1,0:T(8,128)(2,1)S(1)}) custom-call(s32[8]{0:T(128)S(1)} %stack.115.scal, bf16[256,768]{1,0:T(8,128)(2,1)} %bitcast.4.x1.x, bf16[256,768]{1,0:T(8,128)(2,1)} %collective-permute-done.x0, ...), custom_call_target="tpu_custom_call" | custom-call | flops 2359296000 | bytes 8000000 | tf_op jit(solution)/shard_map/project/pallas_call | solution.py:465
  156.0 38.0 %attend.1 = (bf16[2,256,384]{2,1,0:T(8,128)(2,1)S(1)}, f32[3,8,512]{2,1,0:T(8,128)S(1)}) custom-call(s32[8]{0:T(128)S(1)} %stack.115.scal, s32[1536,1]{1,0:T(8,128)S(1)} %get-tuple-element.121.pos_col, s32[1536,1]{1,0:T(8,128)S(1)} %copy-done.1, s32[6,1,256]{2,1,0:T(1,128)S(1)} %and_select_fusion.1.doc_row, bf16[512,384]{1,0:T(8,128)(2,1)S(1)} %get-tuple-element.34.q, ...), custom_call_target="tpu_custom_call" | custom-call | flops 20000000000 | bytes 10000000 | tf_op jit(solution)/shard_map/attend/pallas_call | solution.py:488
  195.2 4.4 %collective-permute-done.20.ctx_other = bf16[256,384]{1,0:T(8,128)(2,1)S(1)} collective-permute-done((bf16[256,384]{1,0:T(8,128)(2,1)S(1)}, bf16[256,384]{1,0:T(8,128)(2,1)S(1)}, u32[]{:S(2)}, u32[]{:S(2)}) %collective-permute-start.20) | collective-permute-done | bytes 196640 | tf_op jit(solution)/shard_map/ppermute | solution.py:640
  202.2 16.7 %feed_forward.1 = (bf16[256,768]{1,0:T(8,128)(2,1)}, f32[256,768]{1,0:T(8,128)S(1)}, bf16[2,256,384]{2,1,0:T(8,128)(2,1)S(1)}, bf16[4,256,768]{2,1,0:T(8,128)(2,...) custom-call(s32[8]{0:T(128)S(1)} %stack.115.scal, ...), custom_call_target="tpu_custom_call" | custom-call | flops 6000000000 | bytes 20000000 | tf_op jit(solution)/shard_map/feed_forward/pallas_call | solution.py:573
  219.9 1.4 copy-done
  221.3 8.5 %weight_grads.1 = bf16[16,2,224,768]{3,2,1,0:T(8,128)(2,1)} custom-call(bf16[4,256,768]{2,1,0:T(8,128)(2,1)S(1)} %copy-done, bf16[256,768]{1,0:T(8,128)(2,1)S(1)} %get-tuple-element.50.ddown, bf16[256,768]{1,0:T(8,128)(2,1)S(1)} %get-tuple-element.51.nlow, bf16[4,256,768]{2,1,0:T(8,128)(2,1)} %get-tuple-element.52.dup, ...), custom_call_target="tpu_custom_call" | custom-call | flops 3000000000 | bytes 15000000 | tf_op jit(solution)/shard_map/weight_grads/pallas_call | solution.py:604
  232.0 1.3 copy-done.23
  233.2 1.3 copy-done.25
  236.3 38.2 %attend_back.1 = (bf16[512,384]{1,0:T(8,128)(2,1)S(1)}, f32[2,512,384]{2,1,0:T(8,128)S(1)}, bf16[2,2,512,384]{3,2,1,0:T(8,128)(2,1)S(1)}, bf16[2,8,6,32,512]{4,3,2,1,0:T(8,128)(2,1)}) custom-call(s32[8]{0:T(128)S(1)} %stack.115.scal, s32[1536,1]{1,0:T(8,128)S(1)} %get-tuple-element.121.pos_col, s32[6,1,256]{2,1,0:T(1,128)S(1)} %and_select_fusion.pos_row, ...), custom_call_target="tpu_custom_call" | custom-call | flops 49999998976 | bytes 20000000 | tf_op jit(solution)/shard_map/attend_back/pallas_call | solution.py:523
  274.6 1.2 slice_bitcast_fusion.2
  276.1 1.9 collective-permute-start.24
  278.0 3.9 collective-permute-start.23
  282.2 7.3 %collective-permute-done.24.right = bf16[2,512,384]{2,1,0:T(8,128)(2,1)S(1)} collective-permute-done((bf16[2,512,384]{2,1,0:T(8,128)(2,1)}, bf16[2,512,384]{2,1,0:T(8,128)(2,1)S(1)}, u32[]{:S(2)}, u32[]{:S(2)}) %collective-permute-start.24) | collective-permute-done | bytes 786464 | tf_op jit(solution)/shard_map/ppermute | solution.py:646
  290.5 18.3 %collective-permute-done.23.left = bf16[2,512,384]{2,1,0:T(8,128)(2,1)S(1)} collective-permute-done((bf16[2,512,384]{2,1,0:T(8,128)(2,1)S(1)}, bf16[2,512,384]{2,1,0:T(8,128)(2,1)S(1)}, u32[]{:S(2)}, u32[]{:S(2)}) %collective-permute-start.23) | collective-permute-done | bytes 786464 | tf_op jit(solution)/shard_map/ppermute | solution.py:646
  312.0 1.4 copy-done.15
  316.7 6.5 %project_back.1 = (bf16[2,8,48,1152]{3,2,1,0:T(8,128)(2,1)S(1)}, f32[256,768]{1,0:T(8,128)S(1)}, bf16[256,768]{1,0:T(8,128)(2,1)S(1)}, f32[8,1152]{1,0:T(8,128)S(1)}) custom-call(s32[8]{0:T(128)S(1)} %stack.115.scal, bf16[512,768]{1,0:T(8,128)(2,1)S(1)} %copy-done.17, bf16[512,384]{1,0:T(8,128)(2,1)S(1)} %copy-done.21, f32[2,512,384]{2,1,0:T(8,128)S(1)} %copy-done.15, ...), custom_call_target="tpu_custom_call" | custom-call | flops 2000000000 | bytes 12000000 | tf_op jit(solution)/shard_map/project_back/pallas_call | solution.py:616
  324.5 1.4 collective-permute-start.33
  325.9 1.7 collective-permute-done.33
  328.7 2.7 collective-permute-done.34
  331.5 6.5 %collective-permute-start.35 = (f32[2,2,288]{2,1,0:T(2,128)S(1)}, f32[2,2,288]{2,1,0:T(2,128)S(1)}, u32[]{:S(2)}, u32[]{:S(2)}) collective-permute-start(f32[2,2,288]{2,1,0:T(2,128)S(1)} %slice_bitcast_fusion.20), channel_id=1, source_target_pairs={{0,4},{1,5},{2,6},{3,7},{4,0},{5,1},{6,2},{7,3},{8,12},{9,13},{10,... | collective-permute-start | bytes 13832 | tf_op jit(solution)/shard_map/ppermute | solution.py:640
  338.0 1.3 fusion.44
  339.3 19.0 %collective-permute-start.26 = (bf16[2,2,2,48,1152]{4,3,2,1,0:T(8,128)(2,1)}, bf16[2,2,2,48,1152]{4,3,2,1,0:T(8,128)(2,1)}, u32[]{:S(2)}, u32[]{:S(2)}) collective-permute-start(bf16[2,2,2,48,1152]{4,3,2,1,0:T(8,128)(2,1)} %bitcast.47), channel_id=1, source_target_pairs={{0,1},{1,0},{2,3},{3,2},{4,5},{5,4},{6,7},{7,6},{8,9},{9,8},{10,11... | collective-permute-start | bytes 2654216 | tf_op jit(solution)/shard_map/ppermute | solution.py:640
  358.5 1.4 fusion.43
  359.9 2.2 collective-permute-start.38
  362.2 2.2 collective-permute-start.37
  367.2 1.7 fusion.1
  368.9 1.8 collective-permute-start.27
  370.7 4.4 %collective-permute-done.25 = bf16[256,768]{1,0:T(8,128)(2,1)S(1)} collective-permute-done((bf16[256,768]{1,0:T(8,128)(2,1)S(1)}, bf16[256,768]{1,0:T(8,128)(2,1)S(1)}, u32[]{:S(2)}, u32[]{:S(2)}) %collective-permute-start.25) | collective-permute-done | bytes 393248 | tf_op jit(solution)/shard_map/ppermute | solution.py:640
  376.0 2.0 fusion
  378.0 3.9 collective-permute-done.27
  382.2 2.3 collective-permute-start.39
  384.6 8.8 %collective-permute-done.28 = bf16[2,48,1152]{2,1,0:T(8,128)(2,1)S(1)} collective-permute-done((bf16[2,48,1152]{2,1,0:T(8,128)(2,1)S(1)}, bf16[2,48,1152]{2,1,0:T(8,128)(2,1)S(1)}, u32[]{:S(2)}, u32[]{:S(2)}) %collective-permute-start.28) | collective-permute-done | bytes 221216 | tf_op jit(solution)/shard_map/ppermute | solution.py:640
  393.4 1.4 collective-permute-start.29
  394.8 6.1 %collective-permute-done.39 = bf16[2,2,6,32,512]{4,3,2,1,0:T(8,128)(2,1)S(1)} collective-permute-done((bf16[2,2,6,32,512]{4,3,2,1,0:T(8,128)(2,1)S(1)}, bf16[2,2,6,32,512]{4,3,2,1,0:T(8,128)(2,1)S(1)}, u32[]{:S(2)}, u32[]{:S(2)}) %collective-permute-start.39) | collective-permute-done | bytes 786464 | tf_op jit(solution)/shard_map/ppermute | solution.py:640
  401.3 2.2 collective-permute-start.30
  403.5 1.5 collective-permute-start.40
  405.2 9.2 %collective-permute-done.40 = bf16[2,6,32,512]{3,2,1,0:T(8,128)(2,1)S(1)} collective-permute-done((bf16[2,6,32,512]{3,2,1,0:T(8,128)(2,1)S(1)}, bf16[2,6,32,512]{3,2,1,0:T(8,128)(2,1)S(1)}, u32[]{:S(2)}, u32[]{:S(2)}) %collective-permute-start.40) | collective-permute-done | bytes 393248 | tf_op jit(solution)/shard_map/ppermute | solution.py:640
  414.5 2.2 collective-permute-start.41
  417.8 7.5 %collective-permute-done.41 = bf16[6,32,512]{2,1,0:T(8,128)(2,1)S(1)} collective-permute-done((bf16[6,32,512]{2,1,0:T(8,128)(2,1)S(1)}, bf16[6,32,512]{2,1,0:T(8,128)(2,1)S(1)}, u32[]{:S(2)}, u32[]{:S(2)}) %collective-permute-start.41) | collective-permute-done | bytes 196640 | tf_op jit(solution)/shard_map/ppermute | solution.py:640
  427.9 1.7 collective-permute-start.32
  429.6 1.6 slice_convert_fusion
  (274 shorter events, 46.9 us)
Async XLA Ops:
  7.2 10.7 %copy-start.41 = (bf16[6,24]{1,0:T(8,128)(2,1)S(1)}, bf16[6,24]{1,0:T(8,128)(2,1)}, u32[]{:S(2)}) copy-start(bf16[6,24]{1,0:T(8,128)(2,1)} %param.19) | copy-start | bytes 868
  7.2 10.9 %copy-start.45 = (bf16[2,24]{1,0:T(2,128)(2,1)S(1)}, bf16[2,24]{1,0:T(2,128)(2,1)}, u32[]{:S(2)}) copy-start(bf16[2,24]{1,0:T(2,128)(2,1)} %param.20) | copy-start | bytes 292
  7.2 11.1 %copy-start.43 = (bf16[96]{0:T(256)(128)(2,1)S(1)}, bf16[96]{0:T(256)(128)(2,1)}, u32[]{:S(2)}) copy-start(bf16[96]{0:T(256)(128)(2,1)} %param.21) | copy-start | bytes 580
  7.2 11.2 %copy-start.35 = (bf16[24,2304]{1,0:T(8,128)(2,1)S(1)}, bf16[24,2304]{1,0:T(8,128)(2,1)}, u32[]{:S(2)}) copy-start(bf16[24,2304]{1,0:T(8,128)(2,1)} %param.15) | copy-start | bytes 331780
  7.2 193.1 %all-gather.2.cloned.1.call-start = ((), (), s32[]{:S(2)}) async-start(), calls=%async_computation.1 | async-start | bytes 11354112 | tf_op jit(solution)/shard_map/all_gather | solution.py:757
  7.3 13.5 %copy-start.33 = (f32[6,32,512]{2,1,0:T(8,128)S(1)}, f32[6,32,512]{2,1,0:T(8,128)}, u32[]{:S(2)}) copy-start(f32[6,32,512]{2,1,0:T(8,128)} %param.22) | copy-start | bytes 1179652
  7.3 13.5 %copy-start.34 = (f32[6,32,512]{2,1,0:T(8,128)S(1)}, f32[6,32,512]{2,1,0:T(8,128)}, u32[]{:S(2)}) copy-start(f32[6,32,512]{2,1,0:T(8,128)} %param.23) | copy-start | bytes 1179652
  7.3 13.5 %copy-start.37 = (f32[6]{0:T(128)S(1)}, f32[6]{0:T(128)}, u32[]{:S(2)}) copy-start(f32[6]{0:T(128)} %param.24) | copy-start | bytes 76
  9.1 1.4 collective-permute-start.21
  10.5 13.5 %copy-start.44 = (s32[32]{0:T(128)S(1)}, s32[32]{0:T(128)}, u32[]{:S(2)}) copy-start(s32[32]{0:T(128)} %param.25) | copy-start | bytes 388
  10.5 13.9 %copy-start.46 = (s32[4]{0:T(128)S(1)}, s32[4]{0:T(128)}, u32[]{:S(2)}) copy-start(s32[4]{0:T(128)} %constant.142.clone) | copy-start | bytes 52
  11.4 414.8 %reduce-scatter.2.cloned.1.call-start = ((), (), s32[]{:S(2)}) async-start(), calls=%async_computation.2 | async-start | bytes 11354112 | tf_op jit(solution)/shard_map/reduce_scatter | solution.py:846
  11.4 109.9 %collective-permute-start.1 = (bf16[256,768]{1,0:T(8,128)(2,1)}, bf16[256,768]{1,0:T(8,128)(2,1)}, u32[]{:S(2)}, u32[]{:S(2)}) collective-permute-start(bf16[256,768]{1,0:T(8,128)(2,1)} %bitcast.4.x1.x), channel_id=1, source_target_pairs={{1,0},{2,1},{3,2},{4,3},{5,4},{6,5},{7,6},{8,7},{9,8},{10,9},{11,1... | collective-permute-start | bytes 1179656 | tf_op jit(solution)/shard_map/ppermute | solution.py:646
  13.5 109.3 %collective-permute-start = (bf16[256,768]{1,0:T(8,128)(2,1)}, bf16[256,768]{1,0:T(8,128)(2,1)}, u32[]{:S(2)}, u32[]{:S(2)}) collective-permute-start(bf16[256,768]{1,0:T(8,128)(2,1)} %bitcast.4.x1.x), channel_id=1, source_target_pairs={{0,1},{1,2},{2,3},{3,4},{4,5},{5,6},{6,7},{7,8},{8,9},{9,10},{10,1... | collective-permute-start | bytes 1179656 | tf_op jit(solution)/shard_map/ppermute | solution.py:646
  18.4 51.0 %collective-permute-start.11 = (bf16[1,288]{1,0:T(2,128)(2,1)S(1)}, bf16[1,288]{1,0:T(2,128)(2,1)S(1)}, u32[]{:S(2)}, u32[]{:S(2)}) collective-permute-start(bf16[1,288]{1,0:T(2,128)(2,1)S(1)} %broadcast_in_dim.65), channel_id=1, source_target_pairs={{0,1},{1,0},{2,3},{3,2},{4,5},{5,4},{6,7},{7,6},{8,9},{9,8},{10,11... | collective-permute-start | bytes 1736 | tf_op jit(solution)/shard_map/ppermute | solution.py:640
  19.2 8.6 %collective-permute-start.5 = (bf16[24,1152]{1,0:T(8,128)(2,1)S(1)}, bf16[24,1152]{1,0:T(8,128)(2,1)S(1)}, u32[]{:S(2)}, u32[]{:S(2)}) collective-permute-start(bf16[24,1152]{1,0:T(8,128)(2,1)S(1)} %bitcast.197), channel_id=1, source_target_pairs={{0,16},{16,0},{1,17},{17,1},{2,18},{18,2},{3,19},{19,3},{4,20},{20... | collective-permute-start | bytes 165896 | tf_op jit(solution)/shard_map/ppermute | solution.py:640
  21.7 15.9 %collective-permute-start.16 = (bf16[6,32,512]{2,1,0:T(8,128)(2,1)S(1)}, bf16[6,32,512]{2,1,0:T(8,128)(2,1)S(1)}, u32[]{:S(2)}, u32[]{:S(2)}) collective-permute-start(bf16[6,32,512]{2,1,0:T(8,128)(2,1)S(1)} %get-tuple-element.68), channel_id=1, source_target_pairs={{0,8},{1,9},{2,10},{3,11},{4,12},{5,13},{6,14},{7,15},{8,0},{9,1},... | collective-permute-start | bytes 589832 | tf_op jit(solution)/shard_map/ppermute | solution.py:640
  27.9 10.5 %collective-permute-start.6 = (bf16[24,1152]{1,0:T(8,128)(2,1)S(1)}, bf16[24,1152]{1,0:T(8,128)(2,1)S(1)}, u32[]{:S(2)}, u32[]{:S(2)}) collective-permute-start(bf16[24,1152]{1,0:T(8,128)(2,1)S(1)} %broadcast_select_fusion.4), channel_id=1, source_target_pairs={{0,1},{1,0},{2,3},{3,2},{4,5},{5,4},{6,7},{7,6},{8,9},{9,8},{10,11... | collective-permute-start | bytes 165896 | tf_op jit(solution)/shard_map/ppermute | solution.py:640
  37.7 11.5 %collective-permute-start.17 = (bf16[2,6,32,512]{3,2,1,0:T(8,128)(2,1)S(1)}, bf16[2,6,32,512]{3,2,1,0:T(8,128)(2,1)S(1)}, u32[]{:S(2)}, u32[]{:S(2)}) collective-permute-start(bf16[2,6,32,512]{3,2,1,0:T(8,128)(2,1)S(1)} %get-tuple-element.85), channel_id=1, source_target_pairs={{0,4},{1,5},{2,6},{3,7},{4,0},{5,1},{6,2},{7,3},{8,12},{9,13},{10,... | collective-permute-start | bytes 1179656 | tf_op jit(solution)/shard_map/ppermute | solution.py:640
  38.5 26.9 %collective-permute-start.7 = (bf16[48,1152]{1,0:T(8,128)(2,1)S(1)}, bf16[48,1152]{1,0:T(8,128)(2,1)S(1)}, u32[]{:S(2)}, u32[]{:S(2)}) collective-permute-start(bf16[48,1152]{1,0:T(8,128)(2,1)S(1)} %get-tuple-element.106), channel_id=1, source_target_pairs={{0,8},{1,9},{2,10},{3,11},{4,12},{5,13},{6,14},{7,15},{8,0},{9,1},... | collective-permute-start | bytes 331784 | tf_op jit(solution)/shard_map/ppermute | solution.py:640
  49.3 27.5 %collective-permute-start.18 = (bf16[2,2,6,32,512]{4,3,2,1,0:T(8,128)(2,1)S(1)}, bf16[2,2,6,32,512]{4,3,2,1,0:T(8,128)(2,1)S(1)}, u32[]{:S(2)}, u32[]{:S(2)}) collective-permute-start(bf16[2,2,6,32,512]{4,3,2,1,0:T(8,128)(2,1)S(1)} %get-tuple-element.77), channel_id=1, source_target_pairs={{0,2},{1,3},{2,0},{3,1},{4,6},{5,7},{6,4},{7,5},{8,10},{9,11},{10,... | collective-permute-start | bytes 2359304 | tf_op jit(solution)/shard_map/ppermute | solution.py:640
  66.1 5.1 %collective-permute-start.8 = (bf16[2,48,1152]{2,1,0:T(8,128)(2,1)}, bf16[2,48,1152]{2,1,0:T(8,128)(2,1)}, u32[]{:S(2)}, u32[]{:S(2)}) collective-permute-start(bf16[2,48,1152]{2,1,0:T(8,128)(2,1)} %get-tuple-element.96), channel_id=1, source_target_pairs={{0,4},{1,5},{2,6},{3,7},{4,0},{5,1},{6,2},{7,3},{8,12},{9,13},{10,... | collective-permute-start | bytes 663560 | tf_op jit(solution)/shard_map/ppermute | solution.py:640
  66.1 56.9 %copy-start.39 = (s32[32]{0:T(128)}, s32[32]{0:T(128)S(1)}, u32[]{:S(2)}) copy-start(s32[32]{0:T(128)S(1)} %iota_xor_fusion) | copy-start | bytes 388
  69.4 30.7 %collective-permute-start.12 = (bf16[2,1,288]{2,0,1:T(2,128)(2,1)S(1)}, bf16[2,1,288]{2,0,1:T(2,128)(2,1)S(1)}, u32[]{:S(2)}, u32[]{:S(2)}) collective-permute-start(bf16[2,1,288]{2,0,1:T(2,128)(2,1)S(1)} %pad_maximum_fusion.12), channel_id=1, source_target_pairs={{0,2},{1,3},{2,0},{3,1},{4,6},{5,7},{6,4},{7,5},{8,10},{9,11},{10,... | collective-permute-start | bytes 3464 | tf_op jit(solution)/shard_map/ppermute | solution.py:640
  72.2 28.0 %collective-permute-start.9 = (bf16[2,2,48,1152]{3,2,1,0:T(8,128)(2,1)S(1)}, bf16[2,2,48,1152]{3,2,1,0:T(8,128)(2,1)S(1)}, u32[]{:S(2)}, u32[]{:S(2)}) collective-permute-start(bf16[2,2,48,1152]{3,2,1,0:T(8,128)(2,1)S(1)} %get-tuple-element.79), channel_id=1, source_target_pairs={{0,2},{1,3},{2,0},{3,1},{4,6},{5,7},{6,4},{7,5},{8,10},{9,11},{10,... | collective-permute-start | bytes 1327112 | tf_op jit(solution)/shard_map/ppermute | solution.py:640
  77.1 78.9 %collective-permute-start.19 = (bf16[8,6,32,512]{3,2,1,0:T(8,128)(2,1)S(1)}, bf16[8,6,32,512]{3,2,1,0:T(8,128)(2,1)}, u32[]{:S(2)}, u32[]{:S(2)}) collective-permute-start(bf16[8,6,32,512]{3,2,1,0:T(8,128)(2,1)S(1)} %bitcast.167), channel_id=1, source_target_pairs={{0,1},{1,0},{2,3},{3,2},{4,5},{5,4},{6,7},{7,6},{8,9},{9,8},{10,11... | collective-permute-start | bytes 4718600 | tf_op jit(solution)/shard_map/ppermute | solution.py:640
  100.1 13.1 %collective-permute-start.13 = (bf16[2,2,1,288]{3,1,2,0:T(2,128)(2,1)S(1)}, bf16[2,2,1,288]{3,1,2,0:T(2,128)(2,1)S(1)}, u32[]{:S(2)}, u32[]{:S(2)}) collective-permute-start(bf16[2,2,1,288]{3,1,2,0:T(2,128)(2,1)S(1)} %pad_maximum_fusion.10), channel_id=1, source_target_pairs={{0,4},{1,5},{2,6},{3,7},{4,0},{5,1},{6,2},{7,3},{8,12},{9,13},{10,... | collective-permute-start | bytes 6920 | tf_op jit(solution)/shard_map/ppermute | solution.py:640
  100.4 47.5 %collective-permute-start.10 = (bf16[8,48,1152]{2,1,0:T(8,128)(2,1)S(1)}, bf16[8,48,1152]{2,1,0:T(8,128)(2,1)}, u32[]{:S(2)}, u32[]{:S(2)}) collective-permute-start(bf16[8,48,1152]{2,1,0:T(8,128)(2,1)S(1)} %bitcast.170), channel_id=1, source_target_pairs={{0,1},{1,0},{2,3},{3,2},{4,5},{5,4},{6,7},{7,6},{8,9},{9,8},{10,11... | collective-permute-start | bytes 2654216 | tf_op jit(solution)/shard_map/ppermute | solution.py:640
  113.2 5.0 %collective-permute-start.14 = (bf16[2,2,2,1,288]{4,2,1,3,0:T(2,128)(2,1)S(1)}, bf16[2,2,2,1,288]{4,2,1,3,0:T(2,128)(2,1)S(1)}, u32[]{:S(2)}, u32[]{:S(2)}) collective-permute-start(bf16[2,2,2,1,288]{4,2,1,3,0:T(2,128)(2,1)S(1)} %pad_maximum_fusion.9), channel_id=1, source_target_pairs={{0,8},{1,9},{2,10},{3,11},{4,12},{5,13},{6,14},{7,15},{8,0},{9,1},... | collective-permute-start | bytes 13832 | tf_op jit(solution)/shard_map/ppermute | solution.py:640
  118.3 3.0 collective-permute-start.15
  121.3 10.0 %collective-permute-start.2 = (bf16[256,768]{1,0:T(8,128)(2,1)}, bf16[256,768]{1,0:T(8,128)(2,1)}, u32[]{:S(2)}, u32[]{:S(2)}) collective-permute-start(bf16[256,768]{1,0:T(8,128)(2,1)} %bitcast.4.x1.x), channel_id=1, source_target_pairs={{0,16},{16,0},{1,17},{17,1},{2,18},{18,2},{3,19},{19,3},{4,20},{20... | collective-permute-start | bytes 1179656 | tf_op jit(solution)/shard_map/ppermute | solution.py:640
  121.3 18.2 %collective-permute-start.4 = (bf16[256,768]{1,0:T(8,128)(2,1)}, bf16[256,768]{1,0:T(8,128)(2,1)}, u32[]{:S(2)}, u32[]{:S(2)}) collective-permute-start(bf16[256,768]{1,0:T(8,128)(2,1)} %collective-permute-done.1.x2), channel_id=1, source_target_pairs={{0,16},{16,0},{1,17},{17,1},{2,18},{18,2},{3,19},{19,3},{4,20},{20... | collective-permute-start | bytes 1179656 | tf_op jit(solution)/shard_map/ppermute | solution.py:640
  122.8 25.1 %collective-permute-start.3 = (bf16[256,768]{1,0:T(8,128)(2,1)}, bf16[256,768]{1,0:T(8,128)(2,1)}, u32[]{:S(2)}, u32[]{:S(2)}) collective-permute-start(bf16[256,768]{1,0:T(8,128)(2,1)} %collective-permute-done.x0), channel_id=1, source_target_pairs={{0,16},{16,0},{1,17},{17,1},{2,18},{18,2},{3,19},{19,3},{4,20},{20... | collective-permute-start | bytes 1179656 | tf_op jit(solution)/shard_map/ppermute | solution.py:640
  131.3 24.7 %copy-start.1 = (s32[1536,1]{1,0:T(8,128)S(1)}, s32[1536,1]{1,0:T(8,128)}, u32[]{:S(2)}) copy-start(s32[1536,1]{1,0:T(8,128)} %get-tuple-element.122.doc_col) | copy-start | bytes 18436
  156.0 38.0 %copy-start.22 = (bf16[1536,384]{1,0:T(8,128)(2,1)}, bf16[1536,384]{1,0:T(8,128)(2,1)S(1)}, u32[]{:S(2)}) copy-start(bf16[1536,384]{1,0:T(8,128)(2,1)S(1)} %get-tuple-element.35.k) | copy-start | bytes 3538948
  156.0 38.0 %copy-start.24 = (bf16[1536,384]{1,0:T(8,128)(2,1)}, bf16[1536,384]{1,0:T(8,128)(2,1)S(1)}, u32[]{:S(2)}) copy-start(bf16[1536,384]{1,0:T(8,128)(2,1)S(1)} %get-tuple-element.36.v) | copy-start | bytes 3538948
  156.0 38.0 %copy-start.26 = (bf16[512,384]{1,0:T(8,128)(2,1)}, bf16[512,384]{1,0:T(8,128)(2,1)S(1)}, u32[]{:S(2)}) copy-start(bf16[512,384]{1,0:T(8,128)(2,1)S(1)} %get-tuple-element.34.q) | copy-start | bytes 1179652
  156.0 39.2 %copy-start.36 = (f32[768,4]{0,1:T(4,128)S(1)}, f32[768,4]{0,1:T(4,128)}, u32[]{:S(2)}) copy-start(f32[768,4]{0,1:T(4,128)} %copy.124) | copy-start | bytes 36868
  156.0 39.1 %copy-start.42 = (f32[8]{0:T(128)S(1)}, f32[8]{0:T(128)}, u32[]{:S(2)}) copy-start(f32[8]{0:T(128)} %pad.26.clone) | copy-start | bytes 100
  194.9 4.8 %collective-permute-start.20 = (bf16[256,384]{1,0:T(8,128)(2,1)S(1)}, bf16[256,384]{1,0:T(8,128)(2,1)S(1)}, u32[]{:S(2)}, u32[]{:S(2)}) collective-permute-start(bf16[256,384]{1,0:T(8,128)(2,1)S(1)} %get-tuple-element.82), channel_id=1, source_target_pairs={{0,16},{16,0},{1,17},{17,1},{2,18},{18,2},{3,19},{19,3},{4,20},{20... | collective-permute-start | bytes 589832 | tf_op jit(solution)/shard_map/ppermute | solution.py:640
  219.8 10.0 %collective-permute-start.22 = (bf16[256,384]{1,0:T(8,128)(2,1)}, bf16[256,384]{1,0:T(8,128)(2,1)}, u32[]{:S(2)}, u32[]{:S(2)}) collective-permute-start(bf16[256,384]{1,0:T(8,128)(2,1)} %get-tuple-element.80), channel_id=1, source_target_pairs={{0,16},{16,0},{1,17},{17,1},{2,18},{18,2},{3,19},{19,3},{4,20},{20... | collective-permute-start | bytes 589832 | tf_op jit(solution)/shard_map/ppermute | solution.py:640
  276.1 13.5 %collective-permute-start.24 = (bf16[2,512,384]{2,1,0:T(8,128)(2,1)}, bf16[2,512,384]{2,1,0:T(8,128)(2,1)S(1)}, u32[]{:S(2)}, u32[]{:S(2)}) collective-permute-start(bf16[2,512,384]{2,1,0:T(8,128)(2,1)} %get-tuple-element.74), channel_id=1, source_target_pairs={{1,0},{2,1},{3,2},{4,3},{5,4},{6,5},{7,6},{8,7},{9,8},{10,9},{11,1... | collective-permute-start | bytes 2359304 | tf_op jit(solution)/shard_map/ppermute | solution.py:646
  278.0 30.8 %collective-permute-start.23 = (bf16[2,512,384]{2,1,0:T(8,128)(2,1)S(1)}, bf16[2,512,384]{2,1,0:T(8,128)(2,1)S(1)}, u32[]{:S(2)}, u32[]{:S(2)}) collective-permute-start(bf16[2,512,384]{2,1,0:T(8,128)(2,1)S(1)} %get-tuple-element.75), channel_id=1, source_target_pairs={{0,1},{1,2},{2,3},{3,4},{4,5},{5,6},{6,7},{7,8},{8,9},{9,10},{10,1... | collective-permute-start | bytes 2359304 | tf_op jit(solution)/shard_map/ppermute | solution.py:646
  316.7 7.5 %copy-start.40 = (s32[32]{0:T(128)S(1)}, s32[32]{0:T(128)}, u32[]{:S(2)}) copy-start(s32[32]{0:T(128)} %copy-done.39) | copy-start | bytes 388
  324.5 3.1 collective-permute-start.33
  327.6 3.8 collective-permute-start.34
  331.5 26.9 %collective-permute-start.35 = (f32[2,2,288]{2,1,0:T(2,128)S(1)}, f32[2,2,288]{2,1,0:T(2,128)S(1)}, u32[]{:S(2)}, u32[]{:S(2)}) collective-permute-start(f32[2,2,288]{2,1,0:T(2,128)S(1)} %slice_bitcast_fusion.20), channel_id=1, source_target_pairs={{0,4},{1,5},{2,6},{3,7},{4,0},{5,1},{6,2},{7,3},{8,12},{9,13},{10,... | collective-permute-start | bytes 13832 | tf_op jit(solution)/shard_map/ppermute | solution.py:640
  338.0 20.5 %copy-start.30 = (bf16[2,8,6,32,512]{4,3,2,1,0:T(8,128)(2,1)S(1)}, bf16[2,8,6,32,512]{4,3,2,1,0:T(8,128)(2,1)}, u32[]{:S(2)}) copy-start(bf16[2,8,6,32,512]{4,3,2,1,0:T(8,128)(2,1)} %get-tuple-element.57) | copy-start | bytes 9437188
  339.3 27.9 %collective-permute-start.26 = (bf16[2,2,2,48,1152]{4,3,2,1,0:T(8,128)(2,1)}, bf16[2,2,2,48,1152]{4,3,2,1,0:T(8,128)(2,1)}, u32[]{:S(2)}, u32[]{:S(2)}) collective-permute-start(bf16[2,2,2,48,1152]{4,3,2,1,0:T(8,128)(2,1)} %bitcast.47), channel_id=1, source_target_pairs={{0,1},{1,0},{2,3},{3,2},{4,5},{5,4},{6,7},{7,6},{8,9},{9,8},{10,11... | collective-permute-start | bytes 2654216 | tf_op jit(solution)/shard_map/ppermute | solution.py:640
  358.4 3.8 collective-permute-start.36
  359.9 16.1 %collective-permute-start.38 = (bf16[2,2,2,6,32,512]{5,4,3,2,1,0:T(8,128)(2,1)}, bf16[2,2,2,6,32,512]{5,4,3,2,1,0:T(8,128)(2,1)}, u32[]{:S(2)}, u32[]{:S(2)}) collective-permute-start(bf16[2,2,2,6,32,512]{5,4,3,2,1,0:T(8,128)(2,1)} %bitcast.72), channel_id=1, source_target_pairs={{0,1},{1,0},{2,3},{3,2},{4,5},{5,4},{6,7},{7,6},{8,9},{9,8},{10,11... | collective-permute-start | bytes 4718600 | tf_op jit(solution)/shard_map/ppermute | solution.py:640
  362.2 3.0 collective-permute-start.37
  364.4 10.7 %collective-permute-start.25 = (bf16[256,768]{1,0:T(8,128)(2,1)S(1)}, bf16[256,768]{1,0:T(8,128)(2,1)S(1)}, u32[]{:S(2)}, u32[]{:S(2)}) collective-permute-start(bf16[256,768]{1,0:T(8,128)(2,1)S(1)} %copy-done.11), channel_id=1, source_target_pairs={{0,16},{16,0},{1,17},{17,1},{2,18},{18,2},{3,19},{19,3},{4,20},{20... | collective-permute-start | bytes 1179656 | tf_op jit(solution)/shard_map/ppermute | solution.py:640
  368.9 13.0 %collective-permute-start.27 = (bf16[2,2,48,1152]{3,2,1,0:T(8,128)(2,1)S(1)}, bf16[2,2,48,1152]{3,2,1,0:T(8,128)(2,1)S(1)}, u32[]{:S(2)}, u32[]{:S(2)}) collective-permute-start(bf16[2,2,48,1152]{3,2,1,0:T(8,128)(2,1)S(1)} %slice_bitcast_fusion.4), channel_id=1, source_target_pairs={{0,2},{1,3},{2,0},{3,1},{4,6},{5,7},{6,4},{7,5},{8,10},{9,11},{10,... | collective-permute-start | bytes 1327112 | tf_op jit(solution)/shard_map/ppermute | solution.py:640
  382.1 11.3 %collective-permute-start.28 = (bf16[2,48,1152]{2,1,0:T(8,128)(2,1)S(1)}, bf16[2,48,1152]{2,1,0:T(8,128)(2,1)S(1)}, u32[]{:S(2)}, u32[]{:S(2)}) collective-permute-start(bf16[2,48,1152]{2,1,0:T(8,128)(2,1)S(1)} %slice_bitcast_fusion.8), channel_id=1, source_target_pairs={{0,4},{1,5},{2,6},{3,7},{4,0},{5,1},{6,2},{7,3},{8,12},{9,13},{10,... | collective-permute-start | bytes 663560 | tf_op jit(solution)/shard_map/ppermute | solution.py:640
  382.2 18.7 %collective-permute-start.39 = (bf16[2,2,6,32,512]{4,3,2,1,0:T(8,128)(2,1)S(1)}, bf16[2,2,6,32,512]{4,3,2,1,0:T(8,128)(2,1)S(1)}, u32[]{:S(2)}, u32[]{:S(2)}) collective-permute-start(bf16[2,2,6,32,512]{4,3,2,1,0:T(8,128)(2,1)S(1)} %slice_bitcast_fusion), channel_id=1, source_target_pairs={{0,2},{1,3},{2,0},{3,1},{4,6},{5,7},{6,4},{7,5},{8,10},{9,11},{10,... | collective-permute-start | bytes 2359304 | tf_op jit(solution)/shard_map/ppermute | solution.py:640
  393.4 7.8 %collective-permute-start.29 = (bf16[48,1152]{1,0:T(8,128)(2,1)S(1)}, bf16[48,1152]{1,0:T(8,128)(2,1)S(1)}, u32[]{:S(2)}, u32[]{:S(2)}) collective-permute-start(bf16[48,1152]{1,0:T(8,128)(2,1)S(1)} %slice_bitcast_fusion.16), channel_id=1, source_target_pairs={{0,8},{1,9},{2,10},{3,11},{4,12},{5,13},{6,14},{7,15},{8,0},{9,1},... | collective-permute-start | bytes 331784 | tf_op jit(solution)/shard_map/ppermute | solution.py:640
  401.3 3.8 collective-permute-start.30
  403.5 10.8 %collective-permute-start.40 = (bf16[2,6,32,512]{3,2,1,0:T(8,128)(2,1)S(1)}, bf16[2,6,32,512]{3,2,1,0:T(8,128)(2,1)S(1)}, u32[]{:S(2)}, u32[]{:S(2)}) collective-permute-start(bf16[2,6,32,512]{3,2,1,0:T(8,128)(2,1)S(1)} %slice_bitcast_fusion.6), channel_id=1, source_target_pairs={{0,4},{1,5},{2,6},{3,7},{4,0},{5,1},{6,2},{7,3},{8,12},{9,13},{10,... | collective-permute-start | bytes 1179656 | tf_op jit(solution)/shard_map/ppermute | solution.py:640
  405.1 20.2 %copy-start.31 = (f32[6,32,512]{2,1,0:T(8,128)S(1)}, f32[6,32,512]{2,1,0:T(8,128)}, u32[]{:S(2)}) copy-start(f32[6,32,512]{2,1,0:T(8,128)} %get-tuple-element.69) | copy-start | bytes 1179652
  405.1 20.2 %copy-start.38 = (f32[6]{0:T(128)S(1)}, f32[6]{0:T(128)}, u32[]{:S(2)}) copy-start(f32[6]{0:T(128)} %param.24) | copy-start | bytes 76
  405.1 11.5 %collective-permute-start.31 = (bf16[24,1152]{1,0:T(8,128)(2,1)S(1)}, bf16[24,1152]{1,0:T(8,128)(2,1)S(1)}, u32[]{:S(2)}, u32[]{:S(2)}) collective-permute-start(bf16[24,1152]{1,0:T(8,128)(2,1)S(1)} %bitcast_select_fusion.2), channel_id=1, source_target_pairs={{0,16},{16,0},{1,17},{17,1},{2,18},{18,2},{3,19},{19,3},{4,20},{20... | collective-permute-start | bytes 165896 | tf_op jit(solution)/shard_map/ppermute | solution.py:640
  414.5 10.8 %collective-permute-start.41 = (bf16[6,32,512]{2,1,0:T(8,128)(2,1)S(1)}, bf16[6,32,512]{2,1,0:T(8,128)(2,1)S(1)}, u32[]{:S(2)}, u32[]{:S(2)}) collective-permute-start(bf16[6,32,512]{2,1,0:T(8,128)(2,1)S(1)} %slice_bitcast_fusion.10), channel_id=1, source_target_pairs={{0,8},{1,9},{2,10},{3,11},{4,12},{5,13},{6,14},{7,15},{8,0},{9,1},... | collective-permute-start | bytes 589832 | tf_op jit(solution)/shard_map/ppermute | solution.py:640
  427.9 3.4 collective-permute-start.32
  (27 other events, 33.3 us)
Sparse Core Ops, SparseCore 0:
  11.5 113.4 all-gather.1
  229.9 162.4 reduce-scatter.1

commit v2 on v0

v2 whole, which is shorter than its diff:
```python
from functools import partial

import jax
import jax.numpy as jnp
from jax import lax
from jax.experimental import pallas as pl
from jax.experimental.pallas import tpu as pltpu
from jax.sharding import PartitionSpec as P

D = 768
FF = 3072
HEADS = 12
HDIM = 64
MPOS = 512
EPS = 1e-05
GROUP = 512
HALF = 256
WINDOW = 3 * GROUP
OWN = 384
CHUNK = 256
NEG = -1e30
BF = jnp.bfloat16
F32 = jnp.float32
HIGH = lax.Precision.HIGHEST
PART_TABLE = 144
PART_SUMS = 400
PART = 416
PART_OUT = 464
PART_MORE = 544


def nn(left, right):
    return jnp.dot(left, right, preferred_element_type=F32)


def nt(left, right, precision=None):
    return lax.dot_general(
        left, right, (((1,), (1,)), ((), ())), precision=precision, preferred_element_type=F32
    )


def tn(left, right):
    return lax.dot_general(left, right, (((0,), (0,)), ((), ())), preferred_element_type=F32)


def load_projection(gathered, w, sem):
    copies = []
    for f in range(16):
        row = (f % 2) * OWN + (f // 2) * 48
        copies.append(
            pltpu.make_async_copy(gathered.at[f, 16:25], w.at[:, row : row + 48, :], sem.at[f])
        )
    for copy in copies:
        copy.start()
    return copies


def table_of(table, head):
    return jnp.concatenate(
        [table[:, 4 * head + part].reshape(MPOS, 128) for part in range(4)], axis=1
    )


def spread_out(values, spread, owner, group):
    return jnp.sum(jnp.where(owner == group, nn(values, spread), 0.0), axis=0, keepdims=True)


def columns_of(w, first, count=3):
    return jnp.concatenate([w[first + part] for part in range(count)], axis=1)


def unit_of(t):
    return (t >> 2) | ((t & 3) << 1)


def project_kernel(
    scal,
    x1,
    x0,
    x2,
    y1,
    y0,
    y2,
    gathered,
    near,
    owner,
    spread,
    group,
    q_ref,
    k_ref,
    v_ref,
    xw,
    w,
    sem,
):
    copies = load_projection(gathered, w, sem)
    side = scal[2]
    for g, (mine, other) in enumerate(((x0, y0), (x1, y1), (x2, y2))):
        xw[pl.ds(pl.multiple_of(g * GROUP + side * HALF, HALF), HALF), :] = mine[...]
        xw[pl.ds(pl.multiple_of(g * GROUP + (1 - side) * HALF, HALF), HALF), :] = other[...]
    bias = [
        spread_out(near[i], spread[:, :OWN], owner[...], group[:, :OWN]) for i in range(2)
    ]
    for copy in copies:
        copy.wait()
    for blk in range(6):
        rows = slice(blk * HALF, (blk + 1) * HALF)
        here = xw[rows, :]
        k_ref[rows, :] = nn(here, columns_of(w, 3)).astype(BF)
        v_ref[rows, :] = (nn(here, columns_of(w, 6)) + bias[1]).astype(BF)
        if blk in (2, 3):
            local = slice((blk - 2) * HALF, (blk - 1) * HALF)
            query = (nn(here, columns_of(w, 0)) + bias[0]).astype(BF)
            q_ref[local, :] = query * jnp.asarray(0.125, BF)


def head_lanes():
    return lax.broadcasted_iota(jnp.int32, (1, 128), 1) < HDIM


def fill_hot(pos_col, hot):
    for blk in range(6):
        rows = slice(blk * 256, (blk + 1) * 256)
        column = lax.broadcasted_iota(jnp.int32, (256, MPOS), 1)
        hot[rows, :] = jnp.where(pos_col[rows, :] == column, 1.0, 0.0).astype(BF)


def fill_hot_turned(pos_row, hot):
    for blk in range(6):
        rows = lax.broadcasted_iota(jnp.int32, (MPOS, 256), 0)
        hot[blk] = jnp.where(pos_row[blk] == rows, 1.0, 0.0).astype(BF)


def set_pair(low, value, target):
    blank = jnp.zeros_like(value)
    target[:HALF, :] = jnp.where(low, value, blank)
    target[HALF:, :] = jnp.where(low, blank, value)


def fold(values, how):
    rows, columns = values.shape
    return how(values.reshape(rows // 8, 8, columns), axis=0)


def attend_kernel(
    scal,
    pos_col,
    pos_row,
    doc_col,
    doc_row,
    q,
    k,
    v,
    table,
    ctx,
    lse,
    hot,
    hot_turned,
    sbuf,
    looks,
    queries,
    acc,
):
    @pl.when(pl.program_id(0) == 0)
    def _():
        fill_hot(pos_col, hot)
        fill_hot_turned(pos_row, hot_turned)

    low = head_lanes()
    for qb in range(2):
        lo, hi = scal[3 + 2 * qb], scal[4 + 2 * qb]
        here = slice(qb * HALF, (qb + 1) * HALF)
        set_pair(low, q[here, :], queries)
        q_doc = jnp.concatenate([doc_row[2 + qb]] * 2, axis=1)
        q_hot = hot[GROUP + qb * HALF : GROUP + (qb + 1) * HALF, :]
        for h in range(2):
            looks[h * HALF : (h + 1) * HALF, :] = nn(q_hot, table_of(table, h)).astype(BF)

        def score_step(c, top, q_doc=q_doc):
            rows = pl.ds(pl.multiple_of(c * CHUNK, CHUNK), CHUNK)
            s = jnp.where(doc_col[rows, :] == q_doc, nt(k[rows, :], queries[...]), NEG)
            sbuf[c] = s
            return jnp.maximum(top, fold(s, jnp.max))

        top = lax.fori_loop(lo, hi, score_step, jnp.full((8, 2 * HALF), NEG, F32))
        top = jnp.max(top, axis=0, keepdims=True)
        acc[...] = jnp.zeros_like(acc)

        def mix_step(c, total, top=top):
            rows = pl.ds(pl.multiple_of(c * CHUNK, CHUNK), CHUNK)
            e = jnp.exp(sbuf[c] - top)
            mixed = (e * nt(hot[rows, :], looks[...])).astype(BF)
            acc[...] += tn(mixed, v[rows, :])
            return total + fold(e, jnp.sum)

        total = lax.fori_loop(lo, hi, mix_step, jnp.zeros((8, 2 * HALF), F32))
        total = jnp.sum(total, axis=0, keepdims=True)
        stat = top + jnp.log(total)
        lse[0, 0:1, here] = stat[:, :HALF]
        lse[0, 1:2, here] = stat[:, HALF:]
        lse[0, 2:8, here] = jnp.zeros((6, HALF), F32)
        inverse = 1.0 / total
        scale = jnp.concatenate(
            [
                jnp.broadcast_to(inverse[:, :HALF], (HDIM, HALF)),
                jnp.broadcast_to(inverse[:, HALF:], (HDIM, HALF)),
            ],
            axis=0,
        ).T
        ctx[qb] = (jnp.where(low, acc[:HALF, :], acc[HALF:, :]) * scale).astype(BF)


def attend_back_kernel(
    scal,
    doc_col,
    doc_row,
    q,
    k,
    v,
    table,
    hot,
    hot_turned,
    xw,
    sums,
    ctx,
    ctx_all,
    dctx,
    dattn,
    lse,
    dq,
    own,
    halo_low,
    halo_high,
    part_keep,
    part_send,
    looks,
    queries,
    grads,
    dk,
    dv,
    dq_acc,
    tt,
    tg,
    gw,
    gout,
):

    low = head_lanes()
    dk[...] = jnp.zeros_like(dk)
    dv[...] = jnp.zeros_like(dv)
    lane = lax.broadcasted_iota(jnp.int32, (8, 128), 1)
    row8 = lax.broadcasted_iota(jnp.int32, (8, 128), 0)
    pick = jnp.where((lane < HDIM) == (row8 == 0), 1.0, 0.0)
    for qb in range(2):
        lo, hi = scal[3 + 2 * qb], scal[4 + 2 * qb]
        here = slice(qb * HALF, (qb + 1) * HALF)
        d_pair = dctx[here, :]
        deltas = nt(pick, d_pair.astype(F32) * ctx[qb].astype(F32), HIGH)
        delta = jnp.concatenate([deltas[0:1, :], deltas[1:2, :]], axis=1)
        top = jnp.concatenate([lse[0, 0:1, here], lse[0, 1:2, here]], axis=1)
        set_pair(low, q[here, :], queries)
        set_pair(low, d_pair, grads)
        q_doc = jnp.concatenate([doc_row[2 + qb]] * 2, axis=1)
        q_hot = hot[GROUP + qb * HALF : GROUP + (qb + 1) * HALF, :]
        for h in range(2):
            looks[h * HALF : (h + 1) * HALF, :] = nn(q_hot, table_of(table, h)).astype(BF)
        dq_acc[...] = jnp.zeros_like(dq_acc)
        tt[...] = jnp.zeros_like(tt)

        def step(c, carry, delta=delta, top=top, q_doc=q_doc):
            rows = pl.ds(pl.multiple_of(c * CHUNK, CHUNK), CHUNK)
            k_c = k[rows, :]
            s = nt(k_c, queries[...])
            p = jnp.exp(jnp.where(doc_col[rows, :] == q_doc, s - top, NEG))
            mixed = p * nt(hot[rows, :], looks[...])
            dm = nt(v[rows, :], grads[...])
            ds = (mixed * dm - p * delta).astype(BF)
            dv[rows, :] += nn(mixed.astype(BF), grads[...])
            dk[rows, :] += nn(ds, queries[...])
            dq_acc[...] += tn(ds, k_c)
            tt[...] += nn(hot_turned[c], (p * dm).astype(BF))
            return carry

        lax.fori_loop(lo, hi, step, 0)
        for h in range(2):
            piece = nt(hot_turned[2 + qb], tt[:, h * HALF : (h + 1) * HALF].astype(BF))
            if qb == 0:
                tg[h] = piece
            else:
                tg[h] += piece
        dq[here, :] = (jnp.where(low, dq_acc[:HALF, :], dq_acc[HALF:, :]) * 0.125).astype(BF)
    own[0] = dk[GROUP : 2 * GROUP, :]
    own[1] = dv[GROUP : 2 * GROUP, :]
    halo_low[0] = dk[:GROUP, :].astype(BF)
    halo_low[1] = dv[:GROUP, :].astype(BF)
    halo_high[0] = dk[2 * GROUP :, :].astype(BF)
    halo_high[1] = dv[2 * GROUP :, :].astype(BF)
    query_grad = dq[...]
    pair_grad = jnp.concatenate([dk[...].astype(BF), dv[...].astype(BF)], axis=1)
    gw[:, 0:128] = tn(xw[GROUP : 2 * GROUP, :], query_grad)
    gw[:, 128:384] = tn(xw[...], pair_grad)
    totals = jnp.concatenate(
        [
            column_sum(query_grad.astype(F32)),
            column_sum(pair_grad[:, 128:].astype(F32)),
            jnp.zeros((14, 128), F32),
        ],
        axis=0,
    ).astype(BF)
    more = part_keep.shape[1] == PART_MORE
    if more:
        gout[...] = tn(ctx_all[...].reshape(GROUP, OWN), dattn[...])
    for cr, out in enumerate((part_keep, part_send)):
        for t in range(8):
            place = 2 * (unit_of(t) ^ scal[0]) + (scal[1] ^ cr)
            rows = [
                gw[pl.ds(pl.multiple_of(part * OWN + place * 24, 8), 24), :] for part in range(2)
            ]
            both = jnp.concatenate(rows, axis=0).astype(BF)
            for i in range(3):
                out[t, i * 48 : i * 48 + 48, :] = both[:, i * 128 : (i + 1) * 128]
            for h in range(2):
                mask = tg[h, pl.ds(pl.multiple_of(place * 32, 32), 32), :].astype(BF)
                for i in range(4):
                    at = PART_TABLE + (4 * h + i) * 32
                    out[t, at : at + 32, :] = mask[:, i * 128 : (i + 1) * 128]
            out[t, PART_SUMS:PART, :] = totals
            if more:
                rows = gout[pl.ds(pl.multiple_of(place * 24, 8), 24), :]
                slices = [rows[:, i * 128 : (i + 1) * 128] for i in range(3)]
                slices.append(jnp.zeros((8, 128), F32))
                out[t, PART_OUT:PART_MORE, :] = jnp.concatenate(slices, axis=0).astype(BF)
                for i in range(3):
                    at = PART + 16 * i
                    out[t, at : at + 16, :] = sums[:, i * 128 : (i + 1) * 128].astype(BF)


def norm_stats(values):
    center = values - jnp.mean(values, axis=-1, keepdims=True)
    rstd = lax.rsqrt(jnp.mean(center * center, axis=-1, keepdims=True) + EPS)
    return center * rstd, rstd


def norm_back(grad, unit, rstd, gain):
    scaled = grad * gain
    return rstd * (
        scaled
        - jnp.mean(scaled, axis=-1, keepdims=True)
        - unit * jnp.mean(scaled * unit, axis=-1, keepdims=True)
    )


def column_sum(values):
    return jnp.sum(values, axis=0, keepdims=True)


def load_feed(wg, sem, wm=None, wu=None, wd=None):
    copies = []

    def bring(source, target):
        copies.append(pltpu.make_async_copy(source, target, sem.at[len(copies)]))
        copies[-1].start()

    for c in range(2):
        for s in range(2):
            if wm is not None:
                bring(
                    wg.at[:, c, 192:240, s * OWN : (s + 1) * OWN],
                    wm.at[s, :, :, c * OWN : (c + 1) * OWN],
                )
            if wu is not None:
                bring(wg.at[:, c, 96 + 48 * s : 144 + 48 * s, :], wu.at[c, s])
        if wd is not None:
            bring(wg.at[:, c, 0:96, :], wd.at[:, c])
    return copies


def shrink_rows(wd, i):
    return wd[pl.ds(4 * i, 4)].reshape(D, D)


def rows_of(i):
    return pl.ds(pl.multiple_of(i * HALF, HALF), HALF)


def both_sides(side, mine, other, target):
    target[rows_of(side), :] = mine[...]
    target[rows_of(1 - side), :] = other[...]


def feed_up_kernel(
    scal,
    x,
    ctx_mine,
    ctx_other,
    smalls,
    owner,
    near,
    near_owner,
    spread,
    group,
    spread_up,
    group_up,
    wg,
    unit1,
    rstd1,
    nlow,
    base,
    send,
    act,
    slope,
    wm,
    wu,
    wd,
    ctxt,
    bup,
    sem,
):
    copies = load_feed(wg, sem, wm, wu, wd)
    vector = lambda i: spread_out(smalls[i], spread[...], owner[...], group[...])
    bias_out, bias_down, shift1, gain1 = [vector(i) for i in (2, 3, 4, 6)]
    for n in range(2):
        bup[n] = spread_out(
            near[8], spread_up[...], near_owner[...], group_up[...] + n * (near.shape[1] // 2)
        )
    even = scal[2] == 0
    mine, other = ctx_mine[...].reshape(GROUP, OWN), ctx_other[...].reshape(GROUP, OWN)
    ctxt[:, :OWN] = jnp.where(even, mine, other)
    ctxt[:, OWN:] = jnp.where(even, other, mine)
    for copy in copies:
        copy.wait()

    def enter(i, carry):
        rows = rows_of(i)
        attn = nn(ctxt[rows, :], wm[...].reshape(D, D)) + bias_out
        unit, rstd = norm_stats(x[rows, :].astype(F32) + attn)
        unit1[rows, :] = unit
        rstd1[rows, :] = jnp.broadcast_to(rstd, (HALF, 128))
        normed = unit * gain1 + shift1
        nlow[rows, :] = normed.astype(BF)
        base[rows, :] = normed + bias_down
        return carry

    lax.fori_loop(0, 2, enter, 0)

    def widen(i, carry):
        n, rows = i >> 1, rows_of(i & 1)
        up = nn(nlow[rows, :], wu[n].reshape(D, D)) + bup[n]
        half_cdf = 0.5 * (1.0 + lax.erf(up * 0.7071067811865476))
        act[n, rows, :] = (up * half_cdf).astype(BF)
        slope[n, rows, :] = half_cdf + up * (0.3989422804014327 * jnp.exp(-0.5 * up * up))
        return carry

    lax.fori_loop(0, 4, widen, 0)

    def shrink(i, carry):
        rows = rows_of(i)
        part = nn(act[0, rows, :], shrink_rows(wd, 0)) + nn(act[1, rows, :], shrink_rows(wd, 1))
        base[rows, :] += part
        send[rows, :] = part.astype(BF)
        return carry

    lax.fori_loop(0, 2, shrink, 0)


def feed_back_kernel(
    scal,
    base,
    got,
    cot_mine,
    cot_other,
    slope,
    smalls,
    owner,
    spread,
    group,
    wg,
    lay,
    ddown,
    dup,
    base2,
    send,
    sums,
    wu,
    wd,
    cot,
    out,
    sem,
):
    copies = load_feed(wg, sem, None, wu, wd)
    vector = lambda i: spread_out(smalls[i], spread[...], owner[...], group[...])
    shift2, gain2 = vector(5), vector(7)
    side = scal[2]
    both_sides(side, cot_mine, cot_other, cot)
    sums[...] = jnp.zeros_like(sums)

    def norm(i, carry):
        rows = rows_of(i)
        unit, rstd = norm_stats(base[rows, :] + got[rows, :].astype(F32))
        out[rows, :] = (unit * gain2 + shift2).astype(BF)
        dy = cot[rows, :].astype(F32)
        sums[3:4, :] += column_sum(dy)
        sums[5:6, :] += column_sum(dy * unit)
        grad = norm_back(dy, unit, rstd, gain2)
        low = grad.astype(BF)
        ddown[rows, :] = low
        sums[1:2, :] += column_sum(low.astype(F32))
        base2[rows, :] = grad
        return carry

    lax.fori_loop(0, 2, norm, 0)
    lay[...] = out[rows_of(side), :]
    for copy in copies:
        copy.wait()

    def back(i, carry):
        n, rows = i >> 1, rows_of(i & 1)
        grad = (nt(ddown[rows, :], shrink_rows(wd, n)) * slope[n, rows, :]).astype(BF)
        dup[n, rows, :] = grad
        sums[pl.ds(8 + n, 1), :] += column_sum(grad.astype(F32))
        return carry

    lax.fori_loop(0, 4, back, 0)

    def leave(i, carry):
        rows = rows_of(i)
        part = nt(dup[0, rows, :], wu[0].reshape(D, D)) + nt(dup[1, rows, :], wu[1].reshape(D, D))
        base2[rows, :] += part
        send[rows, :] = part.astype(BF)
        return carry

    lax.fori_loop(0, 2, leave, 0)


def feed_close_kernel(
    scal,
    base,
    got,
    unit1,
    rstd1,
    sums_in,
    smalls,
    owner,
    spread,
    group,
    wg,
    dh1,
    dattn,
    dctx,
    sums,
    wm,
    grads,
    sem,
):
    copies = load_feed(wg, sem, wm)
    gain1 = spread_out(smalls[6], spread[...], owner[...], group[...])
    side = scal[2]
    sums[...] = sums_in[...]
    for copy in copies:
        copy.wait()

    def close(i, carry):
        rows = rows_of(i)
        grad = base[rows, :] + got[rows, :].astype(F32)
        unit = unit1[rows, :]
        sums[2:3, :] += column_sum(grad)
        sums[4:5, :] += column_sum(grad * unit)
        grad = norm_back(grad, unit, rstd1[rows, 0:1], gain1)
        grads[rows, :] = grad
        low = grad.astype(BF)
        dattn[rows, :] = low
        sums[0:1, :] += column_sum(low.astype(F32))
        dctx[rows, :] = nt(low, wm[side].reshape(OWN, D)).astype(BF)
        return carry

    lax.fori_loop(0, 2, close, 0)
    dh1[...] = grads[rows_of(side), :]


def weight_grad_kernel(scal, act, ddown, nlow, dup, keep, send, down, up):
    for n in range(2):
        up[n] = tn(nlow[...], dup[n])
        down[n * D : (n + 1) * D, :] = tn(act[n], ddown[...])
    for cr, out in enumerate((keep, send)):
        for t in range(8):
            place = 2 * (unit_of(t) ^ scal[0]) + (scal[1] ^ cr)
            out[t, 0:96, :] = down[pl.ds(pl.multiple_of(place * 96, 8), 96), :].astype(BF)
            parts = [
                up[n, pl.ds(pl.multiple_of(s * OWN + place * 24, 8), 24), :]
                for s in range(2)
                for n in range(2)
            ]
            out[t, 96:192, :] = jnp.concatenate(parts, axis=0).astype(BF)


def project_back_kernel(scal, parts, dh1, gathered, dx, dx_send, w, dqkv, sem):
    copies = load_projection(gathered, w, sem)
    at = 0
    for dq, own, left, right in parts:
        width = dq.shape[1]
        dqkv[:, at : at + width] = dq[...]
        for i in range(2):
            start = (1 + i) * OWN + at
            total = own[i] + left[i].astype(F32) + right[i].astype(F32)
            dqkv[:, start : start + width] = total.astype(BF)
        at += width
    for copy in copies:
        copy.wait()
    side = scal[2]
    mine = dqkv[pl.ds(pl.multiple_of(side * HALF, HALF), HALF), :]
    other = dqkv[pl.ds(pl.multiple_of((1 - side) * HALF, HALF), HALF), :]
    for part in range(3):
        cols = slice(part * 256, (part + 1) * 256)
        rows = jnp.concatenate([w[j, cols, :] for j in range(9)], axis=1)
        dx[:, cols] = dh1[:, cols] + nt(mine, rows)
        dx_send[:, cols] = nt(other, rows).astype(BF)


SMEM = pl.BlockSpec(memory_space=pltpu.SMEM)
VM = pl.BlockSpec()
HBM = pl.BlockSpec(memory_space=pl.ANY)


def params():
    return pltpu.CompilerParams(vmem_limit_bytes=60 * 1024 * 1024)


def cost(microseconds):
    return pl.CostEstimate(
        flops=int(microseconds * 1.15e9), bytes_accessed=1000, transcendentals=0
    )


def shape(dims, kind):
    return jax.ShapeDtypeStruct(dims, kind)


def project(scal, pieces, gathered, near, owner, spread, group):
    return pl.pallas_call(
        project_kernel,
        name="project",
        out_shape=(
            shape((GROUP, OWN), BF),
            shape((WINDOW, OWN), BF),
            shape((WINDOW, OWN), BF),
            shape((WINDOW, D), BF),
        ),
        in_specs=[SMEM] + [VM] * 6 + [HBM] + [VM] * 4,
        out_specs=[VM] * 4,
        scratch_shapes=[
            pltpu.VMEM((9, D, 128), BF),
            pltpu.SemaphoreType.DMA((16,)),
        ],
        compiler_params=params(),
        cost_estimate=cost(9),
    )(scal, *pieces, gathered, near, owner, spread, group)


def whole(*dims):
    return pl.BlockSpec(dims, lambda p: (0,) * len(dims))


def attend(scal, pos_col, pos_row, doc_col, doc_row, q, k, v, table):
    return pl.pallas_call(
        attend_kernel,
        name="attend",
        grid=(3,),
        out_shape=(
            shape((2, HALF, OWN), BF),
            shape((3, 8, GROUP), F32),
            shape((WINDOW, MPOS), BF),
            shape((6, MPOS, CHUNK), BF),
        ),
        in_specs=[
            SMEM,
            whole(WINDOW, 1),
            whole(6, 1, CHUNK),
            whole(WINDOW, 1),
            whole(6, 1, CHUNK),
            pl.BlockSpec((GROUP, 128), lambda p: (0, p)),
            pl.BlockSpec((WINDOW, 128), lambda p: (0, p)),
            pl.BlockSpec((WINDOW, 128), lambda p: (0, p)),
            pl.BlockSpec((16, 8, 32, 128), lambda p: (0, p, 0, 0)),
        ],
        out_specs=[
            pl.BlockSpec((2, HALF, 128), lambda p: (0, 0, p)),
            pl.BlockSpec((1, 8, GROUP), lambda p: (p, 0, 0)),
            whole(WINDOW, MPOS),
            whole(6, MPOS, CHUNK),
        ],
        scratch_shapes=[
            pltpu.VMEM((6, CHUNK, 2 * HALF), F32),
            pltpu.VMEM((2 * HALF, MPOS), BF),
            pltpu.VMEM((2 * HALF, 128), BF),
            pltpu.VMEM((2 * HALF, 128), F32),
        ],
        compiler_params=params(),
        cost_estimate=cost(26),
    )(scal, pos_col, pos_row, doc_col, doc_row, q, k, v, table)


def attend_back(
    first, pairs, scal, doc_col, doc_row, q, k, v, table, hots, xw, sums, ctx, dctx, dattn, lse
):
    columns = lambda rows: pl.BlockSpec((rows, 128), lambda p: (0, first + p))
    size = PART_MORE if pairs == 2 else PART
    return pl.pallas_call(
        attend_back_kernel,
        name=f"attend_back_{first}",
        grid=(pairs,),
        out_shape=(
            shape((GROUP, 128 * pairs), BF),
            shape((2, GROUP, 128 * pairs), F32),
            shape((2, GROUP, 128 * pairs), BF),
            shape((2, GROUP, 128 * pairs), BF),
            shape((8, size * pairs, 128), BF),
            shape((8, size * pairs, 128), BF),
        ),
        in_specs=[
            SMEM,
            whole(WINDOW, 1),
            whole(6, 1, CHUNK),
            columns(GROUP),
            columns(WINDOW),
            columns(WINDOW),
            pl.BlockSpec((16, 8, 32, 128), lambda p: (0, first + p, 0, 0)),
            whole(WINDOW, MPOS),
            whole(6, MPOS, CHUNK),
            whole(WINDOW, D),
            pl.BlockSpec((16, OWN), lambda p: (0, p)),
            pl.BlockSpec((2, HALF, 128), lambda p: (0, 0, first + p)),
            whole(2, HALF, OWN),
            columns(GROUP),
            pl.BlockSpec((GROUP, OWN), lambda p: (0, p)),
            pl.BlockSpec((1, 8, GROUP), lambda p: (first + p, 0, 0)),
        ],
        out_specs=[
            pl.BlockSpec((GROUP, 128), lambda p: (0, p)),
            pl.BlockSpec((2, GROUP, 128), lambda p: (0, 0, p)),
            pl.BlockSpec((2, GROUP, 128), lambda p: (0, 0, p)),
            pl.BlockSpec((2, GROUP, 128), lambda p: (0, 0, p)),
            pl.BlockSpec((8, size, 128), lambda p: (0, p, 0)),
            pl.BlockSpec((8, size, 128), lambda p: (0, p, 0)),
        ],
        scratch_shapes=[
            pltpu.VMEM((2 * HALF, MPOS), BF),
            pltpu.VMEM((2 * HALF, 128), BF),
            pltpu.VMEM((2 * HALF, 128), BF),
            pltpu.VMEM((WINDOW, 128), F32),
            pltpu.VMEM((WINDOW, 128), F32),
            pltpu.VMEM((2 * HALF, 128), F32),
            pltpu.VMEM((MPOS, 2 * HALF), F32),
            pltpu.VMEM((2, MPOS, MPOS), F32),
            pltpu.VMEM((D, OWN), F32),
            pltpu.VMEM((OWN, OWN), F32),
        ],
        compiler_params=params(),
        cost_estimate=cost(14 * pairs),
    )(scal, doc_col, doc_row, q, k, v, table, *hots, xw, sums, ctx, ctx, dctx, dattn, lse)


WIDEN = pltpu.VMEM((2, 2, 8, 48, D), BF)
SHRINK = pltpu.VMEM((8, 2, 96, D), BF)
MERGE = pltpu.VMEM((2, 8, 48, D), BF)


def feed_up(scal, xw, mine, other, smalls, owner, near, near_owner, spreads, wg):
    arrays = (mine, other, smalls, owner, near, near_owner, *spreads)
    return pl.pallas_call(
        feed_up_kernel,
        name="feed_up",
        grid=(1,),
        out_shape=(
            shape((GROUP, D), F32),
            shape((GROUP, 128), F32),
            shape((GROUP, D), BF),
            shape((GROUP, D), F32),
            shape((GROUP, D), BF),
            shape((2, GROUP, D), BF),
            shape((2, GROUP, D), F32),
        ),
        in_specs=[SMEM, pl.BlockSpec((GROUP, D), lambda p: (1, 0))]
        + [whole(*a.shape) for a in arrays]
        + [HBM],
        out_specs=[
            whole(GROUP, D),
            whole(GROUP, 128),
            whole(GROUP, D),
            whole(GROUP, D),
            whole(GROUP, D),
            whole(2, GROUP, D),
            whole(2, GROUP, D),
        ],
        scratch_shapes=[
            MERGE,
            WIDEN,
            SHRINK,
            pltpu.VMEM((GROUP, D), BF),
            pltpu.VMEM((2, 1, D), F32),
            pltpu.SemaphoreType.DMA((10,)),
        ],
        compiler_params=params(),
        cost_estimate=cost(10),
    )(scal, xw, *arrays, wg)


def feed_back(scal, base, got, cot, cot_other, slope, smalls, owner, spread, group, wg):
    return pl.pallas_call(
        feed_back_kernel,
        name="feed_back",
        out_shape=(
            shape((HALF, D), BF),
            shape((GROUP, D), BF),
            shape((2, GROUP, D), BF),
            shape((GROUP, D), F32),
            shape((GROUP, D), BF),
            shape((16, D), F32),
        ),
        in_specs=[SMEM] + [VM] * 9 + [HBM],
        out_specs=[VM] * 6,
        scratch_shapes=[
            WIDEN,
            SHRINK,
            pltpu.VMEM((GROUP, D), BF),
            pltpu.VMEM((GROUP, D), BF),
            pltpu.SemaphoreType.DMA((6,)),
        ],
        compiler_params=params(),
        cost_estimate=cost(9),
    )(scal, base, got, cot, cot_other, slope, smalls, owner, spread, group, wg)


def feed_close(scal, base, got, unit1, rstd1, sums, smalls, owner, spread, group, wg):
    return pl.pallas_call(
        feed_close_kernel,
        name="feed_close",
        out_shape=(
            shape((HALF, D), F32),
            shape((GROUP, D), BF),
            shape((GROUP, OWN), BF),
            shape((16, D), F32),
        ),
        in_specs=[SMEM] + [VM] * 9 + [HBM],
        out_specs=[VM] * 4,
        scratch_shapes=[
            MERGE,
            pltpu.VMEM((GROUP, D), F32),
            pltpu.SemaphoreType.DMA((4,)),
        ],
        compiler_params=params(),
        cost_estimate=cost(5),
    )(scal, base, got, unit1, rstd1, sums, smalls, owner, spread, group, wg)


def weight_grads(scal, act, ddown, nlow, dup):
    return pl.pallas_call(
        weight_grad_kernel,
        name="weight_grads",
        out_shape=(shape((8, 192, D), BF), shape((8, 192, D), BF)),
        in_specs=[SMEM] + [VM] * 4,
        out_specs=[VM] * 2,
        scratch_shapes=[pltpu.VMEM((2 * D, D), F32), pltpu.VMEM((2, D, D), F32)],
        compiler_params=params(),
        cost_estimate=cost(7),
    )(scal, act, ddown, nlow, dup)


def project_back(scal, parts, dh1, gathered):
    def kernel(scal, *refs):
        project_back_kernel(scal, [refs[:4], refs[4:8]], *refs[8:])

    return pl.pallas_call(
        kernel,
        name="project_back",
        out_shape=(shape((HALF, D), F32), shape((HALF, D), BF)),
        in_specs=[SMEM] + [VM] * 9 + [HBM],
        out_specs=[VM] * 2,
        scratch_shapes=[
            pltpu.VMEM((9, D, 128), BF),
            pltpu.VMEM((GROUP, 3 * OWN), BF),
            pltpu.SemaphoreType.DMA((16,)),
        ],
        compiler_params=params(),
        cost_estimate=cost(6),
    )(scal, *[x for part in parts for x in part], dh1, gathered)


def swap(value, axis, bit):
    count = lax.axis_size(axis)
    return lax.ppermute(value, axis, [(i, i ^ bit) for i in range(count)])


def shifted(value, axis, steps):
    count = lax.axis_size(axis)
    leading, last = (max(0, -steps), min(count, count - steps))
    return lax.ppermute(value, axis, [(source, source + steps) for source in range(leading, last)])


def tie(*values):
    return lax.optimization_barrier(values)


CORE, ALONG_Y, SIDE = ("fsdp", 1), ("fsdp", 2), ("seq", 1)


def along_z(values):
    return [swap(values[z], "fsdp", 4 * z) for z in range(1, 4)]


def add(mine, got):
    return (mine.astype(F32) + got.astype(F32)).astype(mine.dtype)


def by_core(value):
    return value.reshape(2, 4, *value.shape[1:])


def sum_core(keep, got):
    keep = by_core(keep)
    return add(keep[0], got[0]), add(keep[1], got[1])


def sum_y(keep, got):
    return tuple(add(keep[z], got[z]) for z in range(4))


def sum_z(mine, got):
    total = mine.astype(F32)
    for value in got:
        total = total + value.astype(F32)
    return total.astype(mine.dtype)


def in_order(flag, mine, other, axis):
    first = jnp.where(flag == 0, mine, other)
    second = jnp.where(flag == 0, other, mine)
    return jnp.concatenate([first, second], axis=axis)


def locate(index, opening, finish, stream_rows):
    document = jnp.sum((finish[None, :] <= index[:, None]).astype(jnp.int32), axis=1)
    begin = jnp.max(jnp.where(opening[None, :] <= index[:, None], opening[None, :], 0), axis=1)
    inside = (index >= 0) & (index < stream_rows)
    document = jnp.where(inside, document, -1)
    position = (index - begin) % MPOS
    return document, position


def own_columns(weight, nf, side, place):
    rows = weight.shape[0]
    weight = weight.reshape(rows, 3, 2, OWN)
    core = place % 2
    keep = lax.dynamic_index_in_dim(weight, side, 2, False).reshape(rows, 3 * OWN)
    give = lax.dynamic_index_in_dim(weight, 1 - side, 2, False).reshape(rows, 3 * OWN)
    straight, crossed, near = [], [], []
    for s in range(2):
        for f in range(nf):
            here = s * nf + f
            if f % 2 == s:
                straight.append((here, (1 - s) * nf + f))
            else:
                crossed.append((here, (1 - s) * nf + (f ^ 1)))
                near.append((here, s * nf + (f ^ 1)))
    axes = ("seq", "fsdp")
    same = core == side
    mine = jnp.where(same, keep, lax.ppermute(give, axes, straight))
    other = jnp.where(same, lax.ppermute(keep, axes, near), lax.ppermute(give, axes, crossed))
    return in_order(core, mine, other, 0)


def per_device(
    incoming_state,
    projection_matrix_triple,
    merge_matrix,
    widen_matrix,
    shrink_matrix,
    offset_table,
    norm_scales,
    widen_offset,
    trainable_gate_scores,
    gate_perturbation,
    softening_scale,
    passage_extents,
    result_cotangent,
):
    BOTH = ("seq", "fsdp")
    ns, nf = lax.axis_size("seq"), lax.axis_size("fsdp")
    count = ns * nf
    fast = nf == 16
    side, place = lax.axis_index("seq"), lax.axis_index("fsdp")
    tokens = incoming_state.reshape(HALF, D)
    cot = result_cotangent.reshape(HALF, D)
    stream_rows = GROUP * nf
    rows = projection_matrix_triple.shape[0]
    zero = jnp.zeros((), jnp.int32)
    core, unit = (place % 2, place // 2) if fast else (zero, zero)

    relaxed = jax.nn.sigmoid(
        (trainable_gate_scores + gate_perturbation) / softening_scale[:, None, None]
    )
    relaxed_low = relaxed.astype(BF)
    wide_cols, up_cols = D // count, FF // count
    pad_to = lambda value: jnp.pad(value, ((0, 0), (0, 128 - value.shape[1])))
    packed = jnp.concatenate(
        [
            pad_to(offset_table),
            pad_to(norm_scales),
            pad_to(widen_offset.reshape(1, up_cols)),
            jnp.zeros((7, 128), BF),
        ],
        axis=0,
    )
    lane, row = jnp.arange(D, dtype=jnp.int32)[None, :], jnp.arange(128, dtype=jnp.int32)[:, None]
    spread, group = (lane % wide_cols == row).astype(BF), lane // wide_cols
    spread_up, group_up = (lane % up_cols == row).astype(BF), lane // up_cols

    finish = jnp.cumsum(passage_extents)
    opening = finish - passage_extents
    base = place * GROUP - GROUP
    doc, pos = locate(base + jnp.arange(WINDOW, dtype=jnp.int32), opening, finish, stream_rows)
    edges = base + GROUP + jnp.asarray([0, HALF - 1, HALF, GROUP - 1], jnp.int32)
    edge_begin = jnp.max(jnp.where(opening[None, :] <= edges[:, None], opening[None, :], 0), axis=1)
    edge_end = jnp.min(
        jnp.where(finish[None, :] > edges[:, None], finish[None, :], stream_rows), axis=1
    )
    lows = jnp.clip((edge_begin - base) // CHUNK, 0, 6)
    highs = jnp.clip((edge_end - base + CHUNK - 1) // CHUNK, 0, 6)
    scal = jnp.stack(
        [unit, core, side, lows[0], highs[1], lows[2], highs[3], zero]
    ).astype(jnp.int32)
    before = shifted(tokens, "fsdp", 1)
    after = shifted(tokens, "fsdp", -1)
    other_tokens = swap(tokens, "seq", 1)
    if fast:
        halves = widen_matrix.reshape(rows, 2, FF // 2)
        keep = lax.dynamic_index_in_dim(halves, side, 1, False)
        give = lax.dynamic_index_in_dim(halves, 1 - side, 1, False)
        mine = jnp.concatenate([keep, merge_matrix], axis=1)[None]
        got = swap(jnp.concatenate([give, merge_matrix], axis=1)[None], *SIDE)
        wide = in_order(side, mine, got, 0)
        wide = jnp.concatenate(
            [wide[:, :, : FF // 2].reshape(2, rows, 2, D), wide[:, :, FF // 2 :].reshape(2, rows, 2, OWN)],
            axis=3,
        )
        mine = lax.dynamic_index_in_dim(wide, core, 2, False)
        sent = lax.dynamic_index_in_dim(wide, 1 - core, 2, False)
        wide = in_order(core, mine, swap(sent, *CORE), 1)
        shard = jnp.concatenate(
            [
                shrink_matrix,
                wide[:, :, :D].reshape(96, D),
                wide[:, :, D:].transpose(1, 0, 2).reshape(48, D),
            ],
            axis=0,
        )
        wq = own_columns(projection_matrix_triple, nf, side, place)
        pack = jnp.concatenate(
            [
                relaxed_low.reshape(6, 32, 4, 128).transpose(0, 2, 1, 3).reshape(768, 128),
                wq.reshape(48, 9, 128).transpose(1, 0, 2).reshape(432, 128),
                packed,
                jnp.zeros((32, 128), BF),
            ],
            axis=0,
        )
        gathered = lax.all_gather(pack, "fsdp", axis=0, tiled=True)
        other_tokens, before, after, scal, pos, doc = tie(
            other_tokens, before, after, scal, pos, doc
        )
        other_before = swap(before, *SIDE)
        other_after = swap(after, *SIDE)
        other_before, other_after, shard, cot = tie(other_before, other_after, shard, cot)
        wg = lax.all_gather(shard, "fsdp", axis=0, tiled=True).reshape(8, 2, 240, D)
        cot_other = swap(cot, *SIDE)
        cot_other, gathered = tie(cot_other, gathered)
        weights, table = gathered.reshape(16, 26, 48, 128), gathered.reshape(16, 39, 32, 128)
        near_owner = jnp.arange(nf, dtype=jnp.int32)[:, None]
        near = weights[:, 25, 0:16].transpose(1, 0, 2)
    else:
        other_before = swap(before, "seq", 1)
        other_after = swap(after, "seq", 1)
        full = lax.all_gather(projection_matrix_triple, BOTH, axis=0, tiled=True)
        full = lax.dynamic_index_in_dim(full.reshape(D, 3, 2, OWN), side, 2, False)
        full = full.reshape(2, 8, 48, 9, 128).transpose(1, 0, 3, 2, 4).reshape(16, 9, 48, 128)
        table = lax.all_gather(relaxed_low, "fsdp", axis=1, tiled=True)
        table = table.reshape(6, 16, 32, 4, 128).transpose(1, 0, 3, 2, 4).reshape(16, 24, 32, 128)
        weights = jnp.concatenate([table.reshape(16, 16, 48, 128), full], axis=1)
        smalls = lax.all_gather(packed[None], BOTH, axis=0, tiled=True).transpose(1, 0, 2)
        near = lax.dynamic_slice_in_dim(smalls, side * nf, nf, 1)
        near_owner = jnp.arange(nf, dtype=jnp.int32)[:, None]
        owner = jnp.arange(count, dtype=jnp.int32)[:, None]
        cot_other = swap(cot, *SIDE)
        up = lax.all_gather(widen_matrix, BOTH, axis=0, tiled=True)
        up = lax.dynamic_slice_in_dim(up, side * (FF // 2), FF // 2, 1)
        up = up.reshape(2, 8, 48, 2, D).transpose(1, 3, 0, 2, 4).reshape(8, 2, 96, D)
        down = lax.all_gather(shrink_matrix, "fsdp", axis=0, tiled=True).reshape(8, 2, 96, D)
        out = lax.all_gather(merge_matrix, BOTH, axis=0, tiled=True)
        out = out.reshape(2, 8, 48, 2, OWN).transpose(1, 3, 2, 0, 4).reshape(8, 2, 48, D)
        wg = jnp.concatenate([down, up, out], axis=2)

    pos_col, doc_col = pos.reshape(WINDOW, 1), doc.reshape(WINDOW, 1)
    pos_row, doc_row = pos.reshape(6, 1, CHUNK), doc.reshape(6, 1, CHUNK)
    pieces = (tokens, before, after, other_tokens, other_before, other_after)
    q, k, v, xw = project(scal, pieces, weights, near, near_owner, spread, group)
    if fast:
        far = swap(near, "seq", 1)
        smalls = jnp.concatenate([near, far], axis=1)
        owner = jnp.concatenate([side * nf + near_owner, (1 - side) * nf + near_owner], axis=0)
        q, smalls = tie(q, smalls)
    ctx, lse, *hots = attend(scal, pos_col, pos_row, doc_col, doc_row, q, k, v, table)
    ctx_other = swap(ctx, *SIDE)
    unit1, rstd1, nlow, base_up, send_up, act, slope = feed_up(
        scal, xw, ctx, ctx_other, smalls, owner, near, near_owner,
        (spread, group, spread_up, group_up), wg,
    )
    lay, ddown, dup, base_down, send_down, sums = feed_back(
        scal, base_up, swap(send_up, *SIDE), cot, cot_other, slope, smalls, owner, spread, group, wg
    )
    got_down = swap(send_down, *SIDE)
    feed = weight_grads(scal, act, ddown, nlow, dup)
    got_down, feed = tie(got_down, feed)
    if fast:
        feed_got = swap(by_core(feed[1]), *CORE)
    closed = feed_close(
        scal, base_down, got_down, unit1, rstd1, sums, smalls, owner, spread, group, wg
    )
    if fast:
        closed, feed_got = tie(closed, feed_got)
        feed = sum_core(feed[0], feed_got)
    dh1, dattn, dctx, sums = closed

    def back(first, pairs, dctx):
        dq, own, low, high, keep, send = attend_back(
            first, pairs, scal, doc_col, doc_row, q, k, v, table, hots, xw, sums, ctx, dctx,
            dattn, lse,
        )
        return dq, own, low, high, (keep, send)

    own_cols = lambda values, at, size: lax.dynamic_slice_in_dim(values, at * size, size, 1)
    if fast:
        both_ways = lambda high, low: (shifted(high, "fsdp", 1), shifted(low, "fsdp", -1))
        feed_got = swap(feed[1], *ALONG_Y)
        outs0, feed_got = tie(back(0, 2, dctx), feed_got)
        dq0, own0, low0, high0, part0 = outs0
        feed = sum_y(feed[0], feed_got)
        part0_got = swap(by_core(part0[1]), *CORE)
        part0_got, feed = tie(part0_got, feed)
        part0 = sum_core(part0[0], part0_got)
        part0, dctx = tie(part0, dctx)
        part0_got = swap(part0[1], *ALONG_Y)
        feed_got = along_z(feed)
        ways0 = both_ways(high0, low0)
        outs1, part0_got, feed_got, ways0 = tie(back(2, 1, dctx), part0_got, feed_got, ways0)
        dq1, own1, low1, high1, part1 = outs1
        part0, shard = sum_y(part0[0], part0_got), sum_z(feed[0], feed_got)
        part1_got = swap(by_core(part1[1]), *CORE)
        ways1 = both_ways(high1, low1)
        part0_got = along_z(part0)
        part1_got, ways1 = tie(part1_got, ways1)
        part1 = sum_core(part1[0], part1_got)
        part1_got = swap(part1[1], *ALONG_Y)
        backed = project_back(scal, ((dq0, own0, *ways0), (dq1, own1, *ways1)), dh1, weights)
        (dx, dx_send), part1_got, part0_got = tie(backed, part1_got, part0_got)
        part1, part0 = sum_y(part1[0], part1_got), sum_z(part0[0], part0_got)
        part1 = sum_z(part1[0], along_z(part1))
        dx_got = swap(dx_send, *SIDE)
        blocks = [part0[:PART_MORE], part0[PART_MORE:], part1]
        masks = [
            block[PART_TABLE:PART_SUMS].reshape(2, 4, 32, 128).transpose(0, 2, 1, 3)
            for block in blocks
        ]
        masks = [mask.reshape(2, 32, MPOS) for mask in masks]
        pair_sums = [block[PART_SUMS : PART_SUMS + 2] for block in blocks]
        weight = jnp.stack([block[:PART_TABLE].reshape(3, 2, rows, 128) for block in blocks], axis=1)
        mine = lax.dynamic_index_in_dim(weight, side, 2, False)
        sent = lax.dynamic_index_in_dim(weight, 1 - side, 2, False)
        token_sums = jnp.stack([block[PART:PART_OUT] for block in blocks[:2]]).reshape(6, 16, 128)
        sums = token_sums.transpose(1, 0, 2).reshape(16, D).astype(F32)
        outs = jnp.stack([block[PART_OUT : PART_OUT + 3 * rows] for block in blocks[:2]])
        grad_w_out = outs.reshape(6, rows, 128).transpose(1, 0, 2).reshape(rows, D).astype(F32)
        got = swap(sent.reshape(-1, 128), *SIDE)
        got = got.reshape(3, 3, rows, 128)
        table_total = jnp.concatenate(masks, axis=0).astype(F32)
        mine = mine.transpose(2, 0, 1, 3).reshape(rows, 3, 1, OWN)
        got = got.transpose(2, 0, 1, 3).reshape(rows, 3, 1, OWN)
        grad_w_qkv = in_order(side, mine, got, 2).reshape(rows, 3 * D).astype(F32)
        head_sums = jnp.concatenate(pair_sums, axis=1).astype(F32)
        head_grads = own_cols(head_sums, place, wide_cols)
        grad_w_down = shard[:96].astype(F32)
        wide = shard[96:192].reshape(2, 2, rows, D).transpose(0, 2, 1, 3).reshape(2, rows, FF // 2)
        mine = lax.dynamic_index_in_dim(wide, side, 0, False)
        got = swap(lax.dynamic_index_in_dim(wide, 1 - side, 0, False), *SIDE)
        grad_w_up = in_order(side, mine, got, 1).astype(F32)
    else:
        scatter = partial(lax.psum_scatter, axis_name=BOTH, scatter_dimension=0, tiled=True)
        outs = [back(0, 2, dctx), back(2, 1, dctx)]
        dx, dx_send = project_back(
            scal,
            [
                (dq, own, shifted(high, "fsdp", 1), shifted(low, "fsdp", -1))
                for dq, own, low, high, _ in outs
            ],
            dh1,
            weights,
        )
        dx_got = swap(dx_send, "seq", 1)

        def plain(pair):
            both = jnp.stack(pair, axis=1)
            return jnp.stack([both[4 * (u & 1) + (u >> 1)] for u in range(8)], axis=0)

        first, second = plain(outs[0][4]), plain(outs[1][4])
        parts = [first[:, :, :PART_MORE], first[:, :, PART_MORE:], second]
        table_grad = jnp.stack([p[:, :, PART_TABLE:PART_SUMS] for p in parts])
        table_grad = table_grad.reshape(3, 8, 2, 2, 4, 32, 128).transpose(0, 3, 1, 2, 5, 4, 6)
        table_total = lax.psum_scatter(
            table_grad.reshape(6, MPOS, MPOS), "fsdp", scatter_dimension=1, tiled=True
        ).astype(F32)
        head_rows = jnp.stack([p[:, :, :PART_TABLE] for p in parts])
        head_rows = head_rows.reshape(3, 8, 2, 3, 2, 24, 128).transpose(4, 1, 2, 5, 3, 0, 6)
        head_rows = head_rows.reshape(D, 3, 1, OWN)
        blank = jnp.zeros_like(head_rows)
        both = jnp.concatenate(
            [jnp.where(side == 0, head_rows, blank), jnp.where(side == 0, blank, head_rows)], axis=2
        )
        grad_w_qkv = scatter(both.reshape(D, 3 * D)).astype(F32)
        pair_sums = [p[0, 0, PART_SUMS : PART_SUMS + 2].astype(F32) for p in parts]
        head_sums = lax.psum(jnp.concatenate(pair_sums, axis=1), "fsdp")
        head_grads = own_cols(head_sums, place, wide_cols)
        def placed(value, axis):
            blank = jnp.zeros_like(value)
            sides = [jnp.where(side == 0, value, blank), jnp.where(side == 0, blank, value)]
            return jnp.concatenate(sides, axis=axis)

        gg = plain(feed).reshape(16, 192, D)
        grad_w_down = scatter(placed(gg[:, :96].reshape(FF // 2, D), 0)).astype(F32)
        up = gg[:, 96:192].reshape(16, 2, 2, 24, D).transpose(1, 0, 3, 2, 4).reshape(D, FF // 2)
        grad_w_up = scatter(placed(up, 1)).astype(F32)
        out = jnp.stack([p[:, :, PART_OUT : PART_OUT + 72] for p in parts[:2]])
        out = out.reshape(2, 8, 2, 3, 24, 128).transpose(1, 2, 4, 0, 3, 5).reshape(OWN, D)
        grad_w_out = scatter(placed(out, 0)).astype(F32)
        sums = lax.psum(sums, "fsdp")
    ours = own_cols(sums[:6], side * nf + place, wide_cols)
    grad_biases = jnp.concatenate([head_grads, ours[:4]], axis=0)
    grad_gains = ours[4:]
    grad_bias_up = lax.dynamic_slice_in_dim(
        sums[8:10].reshape(-1), place * up_cols, up_cols, 0
    )
    input_grad = dx + dx_got.astype(F32)
    mask_logit_gradient = (
        table_total * relaxed * (1.0 - relaxed) / softening_scale[:, None, None]
    )
    return (
        lay.reshape(1, HALF, D),
        input_grad.reshape(1, HALF, D),
        grad_w_qkv,
        grad_w_out,
        grad_w_up,
        grad_w_down,
        grad_biases,
        grad_gains,
        grad_bias_up,
        mask_logit_gradient,
    )


def solution(mesh):
    rows = P(("seq", "fsdp"), None)
    columns = P(None, ("seq", "fsdp"))
    block = P("fsdp", "seq", None)
    table = P("seq", "fsdp", None)
    return jax.shard_map(
        per_device,
        mesh=mesh,
        in_specs=(
            block, rows, rows, rows, rows, columns, columns, P(("seq", "fsdp")),
            table, table, P("seq"), P(), block,
        ),
        out_specs=(
            block, block, rows, rows, rows, rows, columns, columns, P(("seq", "fsdp")), table,
        ),
        check_vma=False,
    )
```

time: 1210 us -> 360 us (0.30); the launches traced: 1190 us -> 359 us
  waiting for transfers between devices: 571 us -> 106 us
  matrix products: 194 us -> 0 us
  blocking collectives: 183 us -> 0 us
  Pallas kernels: 0 us -> 123 us
  other arithmetic: 133 us -> 21.7 us
  local copies, waits for them, and re-layouts: 71.7 us -> 24.4 us
  starting transfers between devices: 23.1 us -> 67.5 us
    reduce_scatter x4 -> x0, waiting for transfers between devices: 347 us -> none  [the longest x1 142 us: per_device(): lax.psum_scatter(grad_w_up, ('seq', 'fsdp'), scatter_dimension=0, tiled=T...]
    dot_general x66 -> x0, matrix products: 194 us -> none  [the longest x28 78 us: right_dot(): lax.dot_general(left, right, (((1,), (1,)), ((), ())), preferred_element_...]
    unnamed x11 -> x2, waiting for transfers between devices: 127 us -> 0.03 us
    pallas_call x0 -> x9, Pallas kernels: none -> 123 us  [the longest x2 42.2 us: attend_back(): pl.pallas_call(attend_back_kernel, name=f'attend_back_{first}', grid=(pai...]
    scatter-add x12 -> x0, other arithmetic: 86.7 us -> none  [the longest x6 63 us: head_backward(): columns = jax.ops.segment_sum(lookup_grad.T, key_pos, num_segments=MPOS)]
    unnamed x2 -> x0, blocking collectives: 85.8 us -> none
    all_gather x2 -> x0, blocking collectives: 83.6 us -> none  [the longest x1 43.5 us: per_device(): lax.all_gather(offsets_turned, ('seq', 'fsdp'), axis=0, tiled=True)]
    ppermute x2 -> x31, waiting for transfers between devices: 19.5 us -> 80.1 us  [the longest x28 80 us: swap(): return lax.ppermute(value, axis, [(i, i ^ bit) for i in range(count)])]
  transfers between devices with their start and end apart: 17 -> 39, of which waited for: 12 -> 16; matrix products, arithmetic and copies ran while one was open for 11% -> 9% of each run, Pallas kernels for 0% -> 28%
where the time goes in v2:
time: 360 us; the launch traced here: 359 us
  Pallas kernels  123 us (34%)
  waiting for transfers between devices  106 us (29%)
  starting transfers between devices  67.5 us (19%)
  local copies, waits for them, and re-layouts  24.4 us (7%)
  other arithmetic  21.7 us (6%)
  between operations  15.1 us (4%)
    ppermute x28, waiting for transfers between devices, swap(): return lax.ppermute(value, axis, [(i, i ^ bit) for i in range(count)])  80 us
    ppermute x28, starting transfers between devices, swap(): return lax.ppermute(value, axis, [(i, i ^ bit) for i in range(count)])  42.6 us
    pallas_call x2, Pallas kernels, attend_back(): pl.pallas_call(attend_back_kernel, name=f'attend_back_{first}', grid=(pai...  42.2 us
    pallas_call x1, Pallas kernels, attend(): pl.pallas_call(attend_kernel, name='attend', grid=(3,), out_shape=(shape(...  29.2 us
    ppermute x6, starting transfers between devices, shifted(): lax.ppermute(value, axis, [(source, source + steps) for source in range(l...  16.1 us
    pallas_call x1, Pallas kernels, feed_up(): pl.pallas_call(feed_up_kernel, name='feed_up', grid=(1,), out_shape=(shap...  13.1 us
    all_gather x1, waiting for transfers between devices, per_device(): wg = lax.all_gather(shard, 'fsdp', axis=0, tiled=True).reshape(8, 2, 240, D)  12.5 us
    pallas_call x1, Pallas kernels, feed_back(): pl.pallas_call(feed_back_kernel, name='feed_back', out_shape=(shape((HALF...  10.8 us
  transfers between devices with their start and end apart: 39, of which 16 were waited for; matrix products, arithmetic and copies ran while one was open for 9% of the time, Pallas kernels for 28%

profile of v2, /device:TPU:1, one launch (start us, length us, event | category | flops | bytes accessed | tf_op | source)
XLA Modules:
  0.0 358.7 jit_solution(6717258095187938803)
XLA Ops:
  7.3 0.9 reshape.437
  8.9 4.5 %collective-permute-start.10 = (bf16[24,1152]{1,0:T(8,128)(2,1)S(1)}, bf16[24,1152]{1,0:T(8,128)(2,1)S(1)}, u32[]{:S(2)}, u32[]{:S(2)}) collective-permute-start(bf16[24,1152]{1,0:T(8,128)(2,1)S(1)} %bitcast.207), channel_id=1, source_target_pairs={{1,16},{3,18},{5,20},{7,22},{9,24},{11,26},{13,28},{15,30},{16,1},... | collective-permute-start | bytes 165896 | tf_op jit(solution)/shard_map/ppermute | solution.py:967
  13.4 1.3 collective-permute-start.8
  14.8 2.9 collective-permute-start.9
  17.7 2.1 fusion.47
  20.2 3.2 concatenate.52
  23.9 4.4 %collective-permute-start.1 = (bf16[256,768]{1,0:T(8,128)(2,1)S(1)}, bf16[256,768]{1,0:T(8,128)(2,1)S(1)}, u32[]{:S(2)}, u32[]{:S(2)}) collective-permute-start(bf16[256,768]{1,0:T(8,128)(2,1)S(1)} %bitcast.225), channel_id=1, source_target_pairs={{0,1},{1,2},{2,3},{3,4},{4,5},{5,6},{6,7},{7,8},{8,9},{9,10},{10,1... | collective-permute-start | bytes 1179656 | tf_op jit(solution)/shard_map/ppermute | solution.py:896
  28.4 1.9 collective-permute-start.2
  32.2 4.6 %collective-permute-done.5 = bf16[1,24,2304]{2,1,0:T(8,128)(2,1)S(1)} collective-permute-done((bf16[1,24,2304]{2,1,0:T(8,128)(2,1)S(1)}, bf16[1,24,2304]{2,1,0:T(8,128)(2,1)S(1)}, u32[]{:S(2)}, u32[]{:S(2)}) %collective-permute-start.5) | collective-permute-done | bytes 110624 | tf_op jit(solution)/shard_map/ppermute | solution.py:890
  38.9 3.3 stack.36.scal
  42.7 1.0 collective-permute-start.4
  44.6 8.4 %collective-permute-done.3.y0 = bf16[256,768]{1,0:T(8,128)(2,1)S(1)} collective-permute-done((bf16[256,768]{1,0:T(8,128)(2,1)S(1)}, bf16[256,768]{1,0:T(8,128)(2,1)S(1)}, u32[]{:S(2)}, u32[]{:S(2)}) %collective-permute-start.3) | collective-permute-done | bytes 393248 | tf_op jit(solution)/shard_map/ppermute | solution.py:890
  53.0 8.5 %collective-permute-done.4.y2 = bf16[256,768]{1,0:T(8,128)(2,1)S(1)} collective-permute-done((bf16[256,768]{1,0:T(8,128)(2,1)S(1)}, bf16[256,768]{1,0:T(8,128)(2,1)S(1)}, u32[]{:S(2)}, u32[]{:S(2)}) %collective-permute-start.4) | collective-permute-done | bytes 393248 | tf_op jit(solution)/shard_map/ppermute | solution.py:890
  64.0 1.1 reshape.478.pos_col
  65.8 1.2 reshape.479.doc_col
  67.5 5.3 %collective-permute-done.7.cot_other = bf16[256,768]{1,0:T(8,128)(2,1)S(1)} collective-permute-done((bf16[256,768]{1,0:T(8,128)(2,1)S(1)}, bf16[256,768]{1,0:T(8,128)(2,1)S(1)}, u32[]{:S(2)}, u32[]{:S(2)}) %collective-permute-start.7) | collective-permute-done | bytes 393248 | tf_op jit(solution)/shard_map/ppermute | solution.py:890
  72.8 8.6 %all-gather.3.cloned.1.call-done = bf16[19968,128]{1,0:T(8,128)(2,1)} async-done(((bf16[1248,128]{1,0:T(8,128)(2,1)}), bf16[19968,128]{1,0:T(8,128)(2,1)}) %all-gather.3.cloned.1.call-update) | async-done | bytes 5111824 | tf_op jit(solution)/shard_map/all_gather | solution.py:1066
  82.2 1.2 collective-permute-start.11
  84.7 8.4 %project.1 = (bf16[512,384]{1,0:T(8,128)(2,1)}, bf16[1536,384]{1,0:T(8,128)(2,1)}, bf16[1536,384]{1,0:T(8,128)(2,1)}, bf16[1536,768]{1,0:T(8,128)(2,1)}) custom-call(s32[8]{0:T(128)} %stack.36.scal, bf16[256,768]{1,0:T(8,128)(2,1)} %bitcast.223, bf16[256,768]{1,0:T(8,128)(2,1)} %copy-done.17, bf16[256,768]{1,0:T(8,128)(2,1)} %copy-done.18, ...), custom_call_target="tpu_custom_call" | custom-call | flops 10350000128 | bytes 1000 | tf_op jit(solution)/shard_map/project/pallas_call | solution.py:639
  93.1 29.2 %attend.1 = (bf16[2,256,384]{2,1,0:T(8,128)(2,1)}, f32[3,8,512]{2,1,0:T(8,128)}, bf16[1536,512]{1,0:T(8,128)(2,1)}, bf16[6,512,256]{2,1,0:T(8,128)(2,1)}) custom-call(s32[8]{0:T(128)} %stack.36.scal, s32[1536,1]{1,0:T(8,128)} %reshape.478.pos_col, s32[6,1,256]{2,1,0:T(1,128)} %reshape.445.pos_row, s32[1536,1]{1,0:T(8,128)} %reshape.479.doc_col, ...), custom_call_target="tpu_custom_call" | custom-call | flops 29899999232 | bytes 1000 | tf_op jit(solution)/shard_map/attend/pallas_call | solution.py:664
  124.9 4.7 %collective-permute-done.12.ctx_other = bf16[2,256,384]{2,1,0:T(8,128)(2,1)S(1)} collective-permute-done((bf16[2,256,384]{2,1,0:T(8,128)(2,1)}, bf16[2,256,384]{2,1,0:T(8,128)(2,1)S(1)}, u32[]{:S(2)}, u32[]{:S(2)}) %collective-permute-start.12) | collective-permute-done | bytes 393248 | tf_op jit(solution)/shard_map/ppermute | solution.py:890
  129.6 12.5 %all-gather.5.cloned.1.call-done = bf16[3840,768]{1,0:T(8,128)(2,1)} async-done(((bf16[240,768]{1,0:T(8,128)(2,1)}), bf16[3840,768]{1,0:T(8,128)(2,1)}) %all-gather.5.cloned.1.call-update) | async-done | bytes 5898256 | tf_op jit(solution)/shard_map/all_gather | solution.py:1073
  142.7 13.1 %feed_up.1 = (f32[512,768]{1,0:T(8,128)}, f32[512,128]{1,0:T(8,128)}, bf16[512,768]{1,0:T(8,128)(2,1)}, f32[512,768]{1,0:T(8,128)}, bf16[512,768]{1,0:T(8,128)(2...) custom-call(s32[8]{0:T(128)} %stack.36.scal, bf16[1536,768]{1,0:T(8,128)(2,1)} %get-tuple-element.117.x.xw, ...), custom_call_target="tpu_custom_call" | custom-call | flops 11500000256 | bytes 1000 | tf_op jit(solution)/shard_map/feed_up/pallas_call | solution.py:769
  155.8 1.3 collective-permute-start.13
  157.1 17.9 %collective-permute-done.13.got = bf16[512,768]{1,0:T(8,128)(2,1)S(1)} collective-permute-done((bf16[512,768]{1,0:T(8,128)(2,1)}, bf16[512,768]{1,0:T(8,128)(2,1)S(1)}, u32[]{:S(2)}, u32[]{:S(2)}) %collective-permute-start.13) | collective-permute-done | bytes 786464 | tf_op jit(solution)/shard_map/ppermute | solution.py:890
  175.0 0.9 copy-done.13
  175.9 10.8 %feed_back.1 = (bf16[256,768]{1,0:T(8,128)(2,1)}, bf16[512,768]{1,0:T(8,128)(2,1)}, bf16[2,512,768]{2,1,0:T(8,128)(2,1)}, f32[512,768]{1,0:T(8,128)}, bf16[512,768]{1,0:T(8,128)(2,1)}, /*index=5*/f32[16,768]{1,0:T(8,128)}) custom-call(s32[8]{0:T(128)} %stack.36.scal, f32[512,768]{1,0:T(8,128)} %get-tuple-element.127.base, bf16[512,768]{1,0:T(8,128)(2,1)} %copy-done.13, ...), custom_call_target="tpu_custom_call" | custom-call | flops 10350000128 | bytes 1000 | tf_op jit(solution)/shard_map/feed_back/pallas_call | solution.py:808
  186.6 1.3 collective-permute-start.14
  187.9 7.3 %weight_grads.1 = (bf16[8,192,768]{2,1,0:T(8,128)(2,1)}, bf16[8,192,768]{2,1,0:T(8,128)(2,1)}) custom-call(s32[8]{0:T(128)} %stack.36.scal, bf16[2,512,768]{2,1,0:T(8,128)(2,1)} %get-tuple-element.136.act, bf16[512,768]{1,0:T(8,128)(2,1)} %get-tuple-element.137.ddown, bf16[512,768]{1,0:T(8,128)(2,1)} %get-tuple-element.138.nlow, ...), custom_call_target="tpu_custom_call" | custom-call | flops 8049999872 | bytes 1000 | tf_op jit(solution)/shard_map/weight_grads/pallas_call | solution.py:856
  195.3 9.6 %collective-permute-done.14.got = bf16[512,768]{1,0:T(8,128)(2,1)S(1)} collective-permute-done((bf16[512,768]{1,0:T(8,128)(2,1)}, bf16[512,768]{1,0:T(8,128)(2,1)S(1)}, u32[]{:S(2)}, u32[]{:S(2)}) %collective-permute-start.14) | collective-permute-done | bytes 786464 | tf_op jit(solution)/shard_map/ppermute | solution.py:890
  204.9 2.0 collective-permute-start.15
  206.9 6.4 %feed_close.1 = (f32[256,768]{1,0:T(8,128)}, bf16[512,768]{1,0:T(8,128)(2,1)}, bf16[512,384]{1,0:T(8,128)(2,1)}, f32[16,768]{1,0:T(8,128)}) custom-call(s32[8]{0:T(128)} %stack.36.scal, f32[512,768]{1,0:T(8,128)} %get-tuple-element.134.base, bf16[512,768]{1,0:T(8,128)(2,1)} %copy-done.12, f32[512,768]{1,0:T(8,128)} %get-tuple-element.143.unit1, ...), custom_call_target="tpu_custom_call" | custom-call | flops 5750000128 | bytes 1000 | tf_op jit(solution)/shard_map/feed_close/pallas_call | solution.py:834
  213.3 3.2 fusion
  216.8 26.9 %attend_back_0.1 = (bf16[512,256]{1,0:T(8,128)(2,1)}, f32[2,512,256]{2,1,0:T(8,128)}, bf16[2,512,256]{2,1,0:T(8,128)(2,1)}, bf16[2,512,256]{2,1,0:T(8,128)(2,1)}...) custom-call(s32[8]{0:T(128)} %stack.36.scal, s32[1536,1]{1,0:T(8,128)} %reshape.479.doc_col, ...), custom_call_target="tpu_custom_call" | custom-call | flops 32199999488 | bytes 1000 | tf_op jit(solution)/shard_map/attend_back_0/pallas_call | solution.py:707
  243.8 1.0 copy-done.3
  244.8 1.4 collective-permute-start.17
  246.2 2.8 collective-permute-start.22
  249.0 2.3 collective-permute-start.23
  251.3 2.5 fusion.14
  253.8 1.6 fusion.2
  255.4 1.0 collective-permute-start.18
  257.2 1.2 collective-permute-start.20
  258.4 2.2 collective-permute-done.22.refs_2_
  260.6 15.3 %attend_back_2.1 = (bf16[512,128]{1,0:T(8,128)(2,1)}, f32[2,512,128]{2,1,0:T(8,128)}, bf16[2,512,128]{2,1,0:T(8,128)(2,1)}, bf16[2,512,128]{2,1,0:T(8,128)(2,1)}...) custom-call(s32[8]{0:T(128)} %stack.36.scal, s32[1536,1]{1,0:T(8,128)} %reshape.479.doc_col, ...), custom_call_target="tpu_custom_call" | custom-call | flops 16099999744 | bytes 1000 | tf_op jit(solution)/shard_map/attend_back_2/pallas_call | solution.py:707
  275.9 3.0 collective-permute-done.21
  278.9 5.9 %collective-permute-done.18 = bf16[4,1088,128]{2,1,0:T(8,128)(2,1)S(1)} collective-permute-done((bf16[4,1088,128]{2,1,0:T(8,128)(2,1)}, bf16[4,1088,128]{2,1,0:T(8,128)(2,1)S(1)}, u32[]{:S(2)}, u32[]{:S(2)}) %collective-permute-start.18) | collective-permute-done | bytes 1114144 | tf_op jit(solution)/shard_map/ppermute | solution.py:890
  284.9 1.2 add_convert_fusion
  287.1 1.3 collective-permute-start.36
  288.4 1.1 fusion.17
  289.5 3.6 %collective-permute-start.28 = (bf16[1088,128]{1,0:T(8,128)(2,1)}, bf16[1088,128]{1,0:T(8,128)(2,1)}, u32[]{:S(2)}, u32[]{:S(2)}) collective-permute-start(bf16[1088,128]{1,0:T(8,128)(2,1)} %get-tuple-element.226), channel_id=1, source_target_pairs={{0,4},{1,5},{2,6},{3,7},{4,0},{5,1},{6,2},{7,3},{8,12},{9,13},{10,... | collective-permute-start | bytes 835592 | tf_op jit(solution)/shard_map/ppermute | solution.py:890
  293.9 2.3 collective-permute-start.25
  296.1 2.3 collective-permute-start.26
  299.3 2.0 collective-permute-start.30
  301.3 3.0 collective-permute-done.26.refs_7_
  305.2 7.4 %collective-permute-start.27 = (bf16[4,416,128]{2,1,0:T(8,128)(2,1)S(1)}, bf16[4,416,128]{2,1,0:T(8,128)(2,1)S(1)}, u32[]{:S(2)}, u32[]{:S(2)}) collective-permute-start(bf16[4,416,128]{2,1,0:T(8,128)(2,1)S(1)} %get-tuple-element.228), channel_id=1, source_target_pairs={{0,2},{1,3},{2,0},{3,1},{4,6},{5,7},{6,4},{7,5},{8,10},{9,11},{10,... | collective-permute-start | bytes 1277960 | tf_op jit(solution)/shard_map/ppermute | solution.py:890
  312.5 6.1 %project_back.1 = (f32[256,768]{1,0:T(8,128)}, bf16[256,768]{1,0:T(8,128)(2,1)}) custom-call(s32[8]{0:T(128)} %stack.36.scal, bf16[512,256]{1,0:T(8,128)(2,1)} %get-tuple-element.163.refs_0_, f32[2,512,256]{2,1,0:T(8,128)} %get-tuple-element.164.refs_1_, bf16[2,512,256]{2,1,0:T(8,128)(2,1)} %collective-permute-done.22.refs_2_, ...), custom_call_target="tpu_custom_call" | custom-call | flops 6899999744 | bytes 1000 | tf_op jit(solution)/shard_map/project_back/pallas_call | solution.py:872
  318.6 3.5 collective-permute-done.27
  322.2 1.3 fusion.8
  324.4 10.8 %collective-permute-start.32 = (bf16[416,128]{1,0:T(8,128)(2,1)S(1)}, bf16[416,128]{1,0:T(8,128)(2,1)S(1)}, u32[]{:S(2)}, u32[]{:S(2)}) collective-permute-start(bf16[416,128]{1,0:T(8,128)(2,1)S(1)} %get-tuple-element.229), channel_id=1, source_target_pairs={{0,4},{1,5},{2,6},{3,7},{4,0},{5,1},{6,2},{7,3},{8,12},{9,13},{10,... | collective-permute-start | bytes 319496 | tf_op jit(solution)/shard_map/ppermute | solution.py:890
  335.2 2.2 collective-permute-start.34
  339.0 6.4 %collective-permute-done.33 = bf16[416,128]{1,0:T(8,128)(2,1)S(1)} collective-permute-done((bf16[416,128]{1,0:T(8,128)(2,1)S(1)}, bf16[416,128]{1,0:T(8,128)(2,1)S(1)}, u32[]{:S(2)}, u32[]{:S(2)}) %collective-permute-start.33) | collective-permute-done | bytes 106528 | tf_op jit(solution)/shard_map/ppermute | solution.py:890
  347.5 2.1 collective-permute-done.35
  350.0 0.9 reshape.474
  350.9 0.9 add_bitcast_fusion
  (209 shorter events, 24.9 us)
Async XLA Ops:
  7.2 12.7 %copy-start.10 = (bf16[6,24]{1,0:T(8,128)(2,1)S(1)}, bf16[6,24]{1,0:T(8,128)(2,1)}, u32[]{:S(2)}) copy-start(bf16[6,24]{1,0:T(8,128)(2,1)} %param.19) | copy-start | bytes 868
  7.2 12.7 %copy-start.28 = (bf16[2,24]{1,0:T(2,128)(2,1)S(1)}, bf16[2,24]{1,0:T(2,128)(2,1)}, u32[]{:S(2)}) copy-start(bf16[2,24]{1,0:T(2,128)(2,1)} %param.20) | copy-start | bytes 292
  7.2 12.7 %copy-start.29 = (bf16[96]{0:T(256)(128)(2,1)S(1)}, bf16[96]{0:T(256)(128)(2,1)}, u32[]{:S(2)}) copy-start(bf16[96]{0:T(256)(128)(2,1)} %param.21) | copy-start | bytes 580
  7.2 74.2 %all-gather.3.cloned.1.call-start = ((), (), s32[]{:S(2)}) async-start(), calls=%async_computation | async-start | bytes 5431296 | tf_op jit(solution)/shard_map/all_gather | solution.py:1066
  8.9 11.0 %collective-permute-start.10 = (bf16[24,1152]{1,0:T(8,128)(2,1)S(1)}, bf16[24,1152]{1,0:T(8,128)(2,1)S(1)}, u32[]{:S(2)}, u32[]{:S(2)}) collective-permute-start(bf16[24,1152]{1,0:T(8,128)(2,1)S(1)} %bitcast.207), channel_id=1, source_target_pairs={{1,16},{3,18},{5,20},{7,22},{9,24},{11,26},{13,28},{15,30},{16,1},... | collective-permute-start | bytes 165896 | tf_op jit(solution)/shard_map/ppermute | solution.py:967
  13.4 6.5 %collective-permute-start.8 = (bf16[24,1152]{1,0:T(8,128)(2,1)S(1)}, bf16[24,1152]{1,0:T(8,128)(2,1)S(1)}, u32[]{:S(2)}, u32[]{:S(2)}) collective-permute-start(bf16[24,1152]{1,0:T(8,128)(2,1)S(1)} %bitcast.208), channel_id=1, source_target_pairs={{0,16},{2,18},{4,20},{6,22},{8,24},{10,26},{12,28},{14,30},{17,1},... | collective-permute-start | bytes 165896 | tf_op jit(solution)/shard_map/ppermute | solution.py:966
  14.8 5.2 %collective-permute-start.9 = (bf16[24,1152]{1,0:T(8,128)(2,1)S(1)}, bf16[24,1152]{1,0:T(8,128)(2,1)S(1)}, u32[]{:S(2)}, u32[]{:S(2)}) collective-permute-start(bf16[24,1152]{1,0:T(8,128)(2,1)S(1)} %bitcast.194), channel_id=1, source_target_pairs={{1,0},{3,2},{5,4},{7,6},{9,8},{11,10},{13,12},{15,14},{16,17},{18,... | collective-permute-start | bytes 165896 | tf_op jit(solution)/shard_map/ppermute | solution.py:967
  19.8 10.5 %copy-start.6 = (bf16[24,3072]{1,0:T(8,128)(2,1)S(1)}, bf16[24,3072]{1,0:T(8,128)(2,1)}, u32[]{:S(2)}) copy-start(bf16[24,3072]{1,0:T(8,128)(2,1)} %param.17) | copy-start | bytes 442372
  19.9 10.8 %copy-start.7 = (bf16[24,768]{1,0:T(8,128)(2,1)S(1)}, bf16[24,768]{1,0:T(8,128)(2,1)}, u32[]{:S(2)}) copy-start(bf16[24,768]{1,0:T(8,128)(2,1)} %param.16) | copy-start | bytes 110596
  20.0 10.9 %copy-start.11 = (s32[32]{0:T(128)S(1)}, s32[32]{0:T(128)}, u32[]{:S(2)}) copy-start(s32[32]{0:T(128)} %param.25) | copy-start | bytes 388
  20.0 11.2 %copy-start.30 = (s32[4]{0:T(128)S(1)}, s32[4]{0:T(128)}, u32[]{:S(2)}) copy-start(s32[4]{0:T(128)} %constant.172.clone) | copy-start | bytes 52
  23.4 118.7 %all-gather.5.cloned.1.call-start = ((), (), s32[]{:S(2)}) async-start(), calls=%async_computation.1 | async-start | bytes 6266880 | tf_op jit(solution)/shard_map/all_gather | solution.py:1073
  23.4 18.7 %collective-permute-start = (bf16[256,768]{1,0:T(8,128)(2,1)S(1)}, bf16[256,768]{1,0:T(8,128)(2,1)S(1)}, u32[]{:S(2)}, u32[]{:S(2)}) collective-permute-start(bf16[256,768]{1,0:T(8,128)(2,1)S(1)} %bitcast.224), channel_id=1, source_target_pairs={{0,16},{16,0},{1,17},{17,1},{2,18},{18,2},{3,19},{19,3},{4,20},{20... | collective-permute-start | bytes 1179656 | tf_op jit(solution)/shard_map/ppermute | solution.py:890
  23.9 18.2 %collective-permute-start.1 = (bf16[256,768]{1,0:T(8,128)(2,1)S(1)}, bf16[256,768]{1,0:T(8,128)(2,1)S(1)}, u32[]{:S(2)}, u32[]{:S(2)}) collective-permute-start(bf16[256,768]{1,0:T(8,128)(2,1)S(1)} %bitcast.225), channel_id=1, source_target_pairs={{0,1},{1,2},{2,3},{3,4},{4,5},{5,6},{6,7},{7,8},{8,9},{9,10},{10,1... | collective-permute-start | bytes 1179656 | tf_op jit(solution)/shard_map/ppermute | solution.py:896
  28.4 13.8 %collective-permute-start.2 = (bf16[256,768]{1,0:T(8,128)(2,1)S(1)}, bf16[256,768]{1,0:T(8,128)(2,1)S(1)}, u32[]{:S(2)}, u32[]{:S(2)}) collective-permute-start(bf16[256,768]{1,0:T(8,128)(2,1)S(1)} %bitcast.226), channel_id=1, source_target_pairs={{1,0},{2,1},{3,2},{4,3},{5,4},{6,5},{7,6},{8,7},{9,8},{10,9},{11,1... | collective-permute-start | bytes 1179656 | tf_op jit(solution)/shard_map/ppermute | solution.py:896
  30.8 6.0 %collective-permute-start.5 = (bf16[1,24,2304]{2,1,0:T(8,128)(2,1)S(1)}, bf16[1,24,2304]{2,1,0:T(8,128)(2,1)S(1)}, u32[]{:S(2)}, u32[]{:S(2)}) collective-permute-start(bf16[1,24,2304]{2,1,0:T(8,128)(2,1)S(1)} %fusion.25), channel_id=1, source_target_pairs={{0,16},{16,0},{1,17},{17,1},{2,18},{18,2},{3,19},{19,3},{4,20},{20... | collective-permute-start | bytes 331784 | tf_op jit(solution)/shard_map/ppermute | solution.py:890
  36.9 6.9 %copy-start.8 = (bf16[96,768]{1,0:T(8,128)(2,1)S(1)}, bf16[96,768]{1,0:T(8,128)(2,1)}, u32[]{:S(2)}) copy-start(bf16[96,768]{1,0:T(8,128)(2,1)} %param.18) | copy-start | bytes 442372
  37.6 25.2 %copy-start.15 = (bf16[1,256,768]{2,1,0:T(8,128)(2,1)S(1)}, bf16[1,256,768]{2,1,0:T(8,128)(2,1)}, u32[]{:S(2)}) copy-start(bf16[1,256,768]{2,1,0:T(8,128)(2,1)} %param.26) | copy-start | bytes 1179652
  37.7 6.1 %collective-permute-start.6 = (bf16[2,24,1152]{2,1,0:T(8,128)(2,1)S(1)}, bf16[2,24,1152]{2,1,0:T(8,128)(2,1)S(1)}, u32[]{:S(2)}, u32[]{:S(2)}) collective-permute-start(bf16[2,24,1152]{2,1,0:T(8,128)(2,1)S(1)} %bitcast.202), channel_id=1, source_target_pairs={{0,1},{1,0},{2,3},{3,2},{4,5},{5,4},{6,7},{7,6},{8,9},{9,8},{10,11... | collective-permute-start | bytes 331784 | tf_op jit(solution)/shard_map/ppermute | solution.py:890
  42.2 23.0 %copy-start.16 = (bf16[256,768]{1,0:T(8,128)(2,1)}, bf16[256,768]{1,0:T(8,128)(2,1)S(1)}, u32[]{:S(2)}) copy-start(bf16[256,768]{1,0:T(8,128)(2,1)S(1)} %collective-permute-done.y1) | copy-start | bytes 1179652
  42.2 23.0 %copy-start.17 = (bf16[256,768]{1,0:T(8,128)(2,1)}, bf16[256,768]{1,0:T(8,128)(2,1)S(1)}, u32[]{:S(2)}) copy-start(bf16[256,768]{1,0:T(8,128)(2,1)S(1)} %collective-permute-done.1.x0) | copy-start | bytes 1179652
  42.2 23.0 %copy-start.18 = (bf16[256,768]{1,0:T(8,128)(2,1)}, bf16[256,768]{1,0:T(8,128)(2,1)S(1)}, u32[]{:S(2)}) copy-start(bf16[256,768]{1,0:T(8,128)(2,1)S(1)} %collective-permute-done.2.x2) | copy-start | bytes 1179652
  42.2 10.8 %collective-permute-start.3 = (bf16[256,768]{1,0:T(8,128)(2,1)S(1)}, bf16[256,768]{1,0:T(8,128)(2,1)S(1)}, u32[]{:S(2)}, u32[]{:S(2)}) collective-permute-start(bf16[256,768]{1,0:T(8,128)(2,1)S(1)} %collective-permute-done.1.x0), channel_id=1, source_target_pairs={{0,16},{16,0},{1,17},{17,1},{2,18},{18,2},{3,19},{19,3},{4,20},{20... | collective-permute-start | bytes 1179656 | tf_op jit(solution)/shard_map/ppermute | solution.py:890
  42.7 18.8 %collective-permute-start.4 = (bf16[256,768]{1,0:T(8,128)(2,1)S(1)}, bf16[256,768]{1,0:T(8,128)(2,1)S(1)}, u32[]{:S(2)}, u32[]{:S(2)}) collective-permute-start(bf16[256,768]{1,0:T(8,128)(2,1)S(1)} %collective-permute-done.2.x2), channel_id=1, source_target_pairs={{0,16},{16,0},{1,17},{17,1},{2,18},{18,2},{3,19},{19,3},{4,20},{20... | collective-permute-start | bytes 1179656 | tf_op jit(solution)/shard_map/ppermute | solution.py:890
  53.0 31.6 %copy-start.21 = (bf16[256,768]{1,0:T(8,128)(2,1)}, bf16[256,768]{1,0:T(8,128)(2,1)S(1)}, u32[]{:S(2)}) copy-start(bf16[256,768]{1,0:T(8,128)(2,1)S(1)} %collective-permute-done.3.y0) | copy-start | bytes 1179652
  61.5 23.1 %copy-start.22 = (bf16[256,768]{1,0:T(8,128)(2,1)}, bf16[256,768]{1,0:T(8,128)(2,1)S(1)}, u32[]{:S(2)}) copy-start(bf16[256,768]{1,0:T(8,128)(2,1)S(1)} %collective-permute-done.4.y2) | copy-start | bytes 1179652
  62.8 10.0 %collective-permute-start.7 = (bf16[256,768]{1,0:T(8,128)(2,1)S(1)}, bf16[256,768]{1,0:T(8,128)(2,1)S(1)}, u32[]{:S(2)}, u32[]{:S(2)}) collective-permute-start(bf16[256,768]{1,0:T(8,128)(2,1)S(1)} %bitcast.228), channel_id=1, source_target_pairs={{0,16},{16,0},{1,17},{17,1},{2,18},{18,2},{3,19},{19,3},{4,20},{20... | collective-permute-start | bytes 1179656 | tf_op jit(solution)/shard_map/ppermute | solution.py:890
  72.8 20.3 %copy-start.20 = (bf16[256,768]{1,0:T(8,128)(2,1)}, bf16[256,768]{1,0:T(8,128)(2,1)S(1)}, u32[]{:S(2)}) copy-start(bf16[256,768]{1,0:T(8,128)(2,1)S(1)} %collective-permute-done.7.cot_other) | copy-start | bytes 1179652
  82.2 10.9 %collective-permute-start.11 = (bf16[16,16,128]{2,0,1:T(8,128)(2,1)S(1)}, bf16[16,16,128]{2,0,1:T(8,128)(2,1)S(1)}, u32[]{:S(2)}, u32[]{:S(2)}) collective-permute-start(bf16[16,16,128]{2,0,1:T(8,128)(2,1)S(1)} %slice_bitcast_fusion), channel_id=1, source_target_pairs={{0,16},{16,0},{1,17},{17,1},{2,18},{18,2},{3,19},{19,3},{4,20},{20... | collective-permute-start | bytes 196616 | tf_op jit(solution)/shard_map/ppermute | solution.py:890
  122.3 7.3 %collective-permute-start.12 = (bf16[2,256,384]{2,1,0:T(8,128)(2,1)}, bf16[2,256,384]{2,1,0:T(8,128)(2,1)S(1)}, u32[]{:S(2)}, u32[]{:S(2)}) collective-permute-start(bf16[2,256,384]{2,1,0:T(8,128)(2,1)} %get-tuple-element.124.ctx_mine.ctx.ctx_all), channel_id=1, source_target_pairs={{0,16},{16,0},{1,17},{17,1},{2,18},{18,2},{3,19},{19,3},{4,20},{20... | collective-permute-start | bytes 1179656 | tf_op jit(solution)/shard_map/ppermute | solution.py:890
  129.6 13.1 %copy-start.23 = (bf16[2,256,384]{2,1,0:T(8,128)(2,1)}, bf16[2,256,384]{2,1,0:T(8,128)(2,1)S(1)}, u32[]{:S(2)}) copy-start(bf16[2,256,384]{2,1,0:T(8,128)(2,1)S(1)} %collective-permute-done.12.ctx_other) | copy-start | bytes 1179652
  155.8 19.2 %collective-permute-start.13 = (bf16[512,768]{1,0:T(8,128)(2,1)}, bf16[512,768]{1,0:T(8,128)(2,1)S(1)}, u32[]{:S(2)}, u32[]{:S(2)}) collective-permute-start(bf16[512,768]{1,0:T(8,128)(2,1)} %get-tuple-element.128), channel_id=1, source_target_pairs={{0,16},{16,0},{1,17},{17,1},{2,18},{18,2},{3,19},{19,3},{4,20},{20... | collective-permute-start | bytes 2359304 | tf_op jit(solution)/shard_map/ppermute | solution.py:890
  186.6 18.3 %collective-permute-start.14 = (bf16[512,768]{1,0:T(8,128)(2,1)}, bf16[512,768]{1,0:T(8,128)(2,1)S(1)}, u32[]{:S(2)}, u32[]{:S(2)}) collective-permute-start(bf16[512,768]{1,0:T(8,128)(2,1)} %get-tuple-element.135), channel_id=1, source_target_pairs={{0,16},{16,0},{1,17},{17,1},{2,18},{18,2},{3,19},{19,3},{4,20},{20... | collective-permute-start | bytes 2359304 | tf_op jit(solution)/shard_map/ppermute | solution.py:890
  204.9 8.4 %collective-permute-start.15 = (bf16[2,4,192,768]{3,2,1,0:T(8,128)(2,1)}, bf16[2,4,192,768]{3,2,1,0:T(8,128)(2,1)}, u32[]{:S(2)}, u32[]{:S(2)}) collective-permute-start(bf16[2,4,192,768]{3,2,1,0:T(8,128)(2,1)} %bitcast.220), channel_id=1, source_target_pairs={{0,1},{1,0},{2,3},{3,2},{4,5},{5,4},{6,7},{7,6},{8,9},{9,8},{10,11... | collective-permute-start | bytes 7077896 | tf_op jit(solution)/shard_map/ppermute | solution.py:890
  206.9 6.4 %copy-start = (bf16[8,192,768]{2,1,0:T(8,128)(2,1)S(1)}, bf16[8,192,768]{2,1,0:T(8,128)(2,1)}, u32[]{:S(2)}) copy-start(bf16[8,192,768]{2,1,0:T(8,128)(2,1)} %get-tuple-element.161) | copy-start | bytes 7077892
  216.5 27.2 %collective-permute-start.16 = (bf16[4,192,768]{2,1,0:T(8,128)(2,1)}, bf16[4,192,768]{2,1,0:T(8,128)(2,1)S(1)}, u32[]{:S(2)}, u32[]{:S(2)}) collective-permute-start(bf16[4,192,768]{2,1,0:T(8,128)(2,1)} %get-tuple-element.217), channel_id=1, source_target_pairs={{0,2},{1,3},{2,0},{3,1},{4,6},{5,7},{6,4},{7,5},{8,10},{9,11},{10,... | collective-permute-start | bytes 3538952 | tf_op jit(solution)/shard_map/ppermute | solution.py:890
  244.8 9.0 %collective-permute-start.17 = (bf16[2,4,1088,128]{3,2,1,0:T(8,128)(2,1)}, bf16[2,4,1088,128]{3,2,1,0:T(8,128)(2,1)S(1)}, u32[]{:S(2)}, u32[]{:S(2)}) collective-permute-start(bf16[2,4,1088,128]{3,2,1,0:T(8,128)(2,1)} %bitcast.221), channel_id=1, source_target_pairs={{0,1},{1,0},{2,3},{3,2},{4,5},{5,4},{6,7},{7,6},{8,9},{9,8},{10,11... | collective-permute-start | bytes 6684680 | tf_op jit(solution)/shard_map/ppermute | solution.py:890
  246.2 14.4 %collective-permute-start.22 = (bf16[2,512,256]{2,1,0:T(8,128)(2,1)}, bf16[2,512,256]{2,1,0:T(8,128)(2,1)}, u32[]{:S(2)}, u32[]{:S(2)}) collective-permute-start(bf16[2,512,256]{2,1,0:T(8,128)(2,1)} %get-tuple-element.180), channel_id=1, source_target_pairs={{0,1},{1,2},{2,3},{3,4},{4,5},{5,6},{6,7},{7,8},{8,9},{9,10},{10,1... | collective-permute-start | bytes 1572872 | tf_op jit(solution)/shard_map/ppermute | solution.py:896
  249.0 26.9 %collective-permute-start.23 = (bf16[2,512,256]{2,1,0:T(8,128)(2,1)}, bf16[2,512,256]{2,1,0:T(8,128)(2,1)}, u32[]{:S(2)}, u32[]{:S(2)}) collective-permute-start(bf16[2,512,256]{2,1,0:T(8,128)(2,1)} %get-tuple-element.181), channel_id=1, source_target_pairs={{1,0},{2,1},{3,2},{4,3},{5,4},{6,5},{7,6},{8,7},{9,8},{10,9},{11,1... | collective-permute-start | bytes 1572872 | tf_op jit(solution)/shard_map/ppermute | solution.py:896
  255.4 29.4 %collective-permute-start.18 = (bf16[4,1088,128]{2,1,0:T(8,128)(2,1)}, bf16[4,1088,128]{2,1,0:T(8,128)(2,1)S(1)}, u32[]{:S(2)}, u32[]{:S(2)}) collective-permute-start(bf16[4,1088,128]{2,1,0:T(8,128)(2,1)} %get-tuple-element.176), channel_id=1, source_target_pairs={{0,2},{1,3},{2,0},{3,1},{4,6},{5,7},{6,4},{7,5},{8,10},{9,11},{10,... | collective-permute-start | bytes 3342344 | tf_op jit(solution)/shard_map/ppermute | solution.py:890
  256.5 19.4 %collective-permute-start.19 = (bf16[192,768]{1,0:T(8,128)(2,1)}, bf16[192,768]{1,0:T(8,128)(2,1)S(1)}, u32[]{:S(2)}, u32[]{:S(2)}) collective-permute-start(bf16[192,768]{1,0:T(8,128)(2,1)} %get-tuple-element.177), channel_id=1, source_target_pairs={{0,4},{1,5},{2,6},{3,7},{4,0},{5,1},{6,2},{7,3},{8,12},{9,13},{10,... | collective-permute-start | bytes 884744 | tf_op jit(solution)/shard_map/ppermute | solution.py:890
  257.2 18.7 %collective-permute-start.20 = (bf16[192,768]{1,0:T(8,128)(2,1)}, bf16[192,768]{1,0:T(8,128)(2,1)}, u32[]{:S(2)}, u32[]{:S(2)}) collective-permute-start(bf16[192,768]{1,0:T(8,128)(2,1)} %get-tuple-element.178), channel_id=1, source_target_pairs={{0,8},{1,9},{2,10},{3,11},{4,12},{5,13},{6,14},{7,15},{8,0},{9,1},... | collective-permute-start | bytes 884744 | tf_op jit(solution)/shard_map/ppermute | solution.py:890
  260.6 18.3 %collective-permute-start.21 = (bf16[192,768]{1,0:T(8,128)(2,1)}, bf16[192,768]{1,0:T(8,128)(2,1)}, u32[]{:S(2)}, u32[]{:S(2)}) collective-permute-start(bf16[192,768]{1,0:T(8,128)(2,1)} %get-tuple-element.179), channel_id=1, source_target_pairs={{0,12},{1,13},{2,14},{3,15},{4,8},{5,9},{6,10},{7,11},{8,4},{9,5},... | collective-permute-start | bytes 884744 | tf_op jit(solution)/shard_map/ppermute | solution.py:890
  284.9 20.1 %collective-permute-start.24 = (bf16[2,4,416,128]{3,2,1,0:T(8,128)(2,1)}, bf16[2,4,416,128]{3,2,1,0:T(8,128)(2,1)S(1)}, u32[]{:S(2)}, u32[]{:S(2)}) collective-permute-start(bf16[2,4,416,128]{3,2,1,0:T(8,128)(2,1)} %bitcast.222), channel_id=1, source_target_pairs={{0,1},{1,0},{2,3},{3,2},{4,5},{5,4},{6,7},{7,6},{8,9},{9,8},{10,11... | collective-permute-start | bytes 2555912 | tf_op jit(solution)/shard_map/ppermute | solution.py:890
  287.0 6.8 %copy-start.25 = (bf16[2,512,128]{2,1,0:T(8,128)(2,1)S(1)}, bf16[2,512,128]{2,1,0:T(8,128)(2,1)}, u32[]{:S(2)}) copy-start(bf16[2,512,128]{2,1,0:T(8,128)(2,1)} %get-tuple-element.187) | copy-start | bytes 786436
  287.1 9.1 %copy-start.24 = (bf16[2,512,128]{2,1,0:T(8,128)(2,1)S(1)}, bf16[2,512,128]{2,1,0:T(8,128)(2,1)}, u32[]{:S(2)}) copy-start(bf16[2,512,128]{2,1,0:T(8,128)(2,1)} %get-tuple-element.188) | copy-start | bytes 786436
  287.1 17.9 %copy-start.4 = (bf16[8,416,128]{2,1,0:T(8,128)(2,1)S(1)}, bf16[8,416,128]{2,1,0:T(8,128)(2,1)}, u32[]{:S(2)}) copy-start(bf16[8,416,128]{2,1,0:T(8,128)(2,1)} %get-tuple-element.194) | copy-start | bytes 2555908
  287.1 9.0 %collective-permute-start.36 = (bf16[24,1536]{1,0:T(8,128)(2,1)S(1)}, bf16[24,1536]{1,0:T(8,128)(2,1)S(1)}, u32[]{:S(2)}, u32[]{:S(2)}) collective-permute-start(bf16[24,1536]{1,0:T(8,128)(2,1)S(1)} %dynamic-slice_bitcast_fusion), channel_id=1, source_target_pairs={{0,16},{16,0},{1,17},{17,1},{2,18},{18,2},{3,19},{19,3},{4,20},{20... | collective-permute-start | bytes 221192 | tf_op jit(solution)/shard_map/ppermute | solution.py:890
  289.5 29.1 %collective-permute-start.28 = (bf16[1088,128]{1,0:T(8,128)(2,1)}, bf16[1088,128]{1,0:T(8,128)(2,1)}, u32[]{:S(2)}, u32[]{:S(2)}) collective-permute-start(bf16[1088,128]{1,0:T(8,128)(2,1)} %get-tuple-element.226), channel_id=1, source_target_pairs={{0,4},{1,5},{2,6},{3,7},{4,0},{5,1},{6,2},{7,3},{8,12},{9,13},{10,... | collective-permute-start | bytes 835592 | tf_op jit(solution)/shard_map/ppermute | solution.py:890
  293.1 25.6 %collective-permute-start.29 = (bf16[1088,128]{1,0:T(8,128)(2,1)}, bf16[1088,128]{1,0:T(8,128)(2,1)}, u32[]{:S(2)}, u32[]{:S(2)}) collective-permute-start(bf16[1088,128]{1,0:T(8,128)(2,1)} %get-tuple-element.225), channel_id=1, source_target_pairs={{0,8},{1,9},{2,10},{3,11},{4,12},{5,13},{6,14},{7,15},{8,0},{9,1},... | collective-permute-start | bytes 835592 | tf_op jit(solution)/shard_map/ppermute | solution.py:890
  293.9 5.4 %collective-permute-start.25 = (bf16[2,512,128]{2,1,0:T(8,128)(2,1)S(1)}, bf16[2,512,128]{2,1,0:T(8,128)(2,1)S(1)}, u32[]{:S(2)}, u32[]{:S(2)}) collective-permute-start(bf16[2,512,128]{2,1,0:T(8,128)(2,1)S(1)} %copy-done.25), channel_id=1, source_target_pairs={{0,1},{1,2},{2,3},{3,4},{4,5},{5,6},{6,7},{7,8},{8,9},{9,10},{10,1... | collective-permute-start | bytes 786440 | tf_op jit(solution)/shard_map/ppermute | solution.py:896
  296.1 8.1 %collective-permute-start.26 = (bf16[2,512,128]{2,1,0:T(8,128)(2,1)S(1)}, bf16[2,512,128]{2,1,0:T(8,128)(2,1)S(1)}, u32[]{:S(2)}, u32[]{:S(2)}) collective-permute-start(bf16[2,512,128]{2,1,0:T(8,128)(2,1)S(1)} %copy-done.24), channel_id=1, source_target_pairs={{1,0},{2,1},{3,2},{4,3},{5,4},{6,5},{7,6},{8,7},{9,8},{10,9},{11,1... | collective-permute-start | bytes 786440 | tf_op jit(solution)/shard_map/ppermute | solution.py:896
  299.3 5.0 %copy-start.26 = (bf16[2,512,128]{2,1,0:T(8,128)(2,1)}, bf16[2,512,128]{2,1,0:T(8,128)(2,1)S(1)}, u32[]{:S(2)}) copy-start(bf16[2,512,128]{2,1,0:T(8,128)(2,1)S(1)} %collective-permute-done.25.refs_6_) | copy-start | bytes 786436
  299.3 19.4 %collective-permute-start.30 = (bf16[1088,128]{1,0:T(8,128)(2,1)}, bf16[1088,128]{1,0:T(8,128)(2,1)}, u32[]{:S(2)}, u32[]{:S(2)}) collective-permute-start(bf16[1088,128]{1,0:T(8,128)(2,1)} %get-tuple-element.224), channel_id=1, source_target_pairs={{0,12},{1,13},{2,14},{3,15},{4,8},{5,9},{6,10},{7,11},{8,4},{9,5},... | collective-permute-start | bytes 835592 | tf_op jit(solution)/shard_map/ppermute | solution.py:890
  305.2 17.0 %collective-permute-start.27 = (bf16[4,416,128]{2,1,0:T(8,128)(2,1)S(1)}, bf16[4,416,128]{2,1,0:T(8,128)(2,1)S(1)}, u32[]{:S(2)}, u32[]{:S(2)}) collective-permute-start(bf16[4,416,128]{2,1,0:T(8,128)(2,1)S(1)} %get-tuple-element.228), channel_id=1, source_target_pairs={{0,2},{1,3},{2,0},{3,1},{4,6},{5,7},{6,4},{7,5},{8,10},{9,11},{10,... | collective-permute-start | bytes 1277960 | tf_op jit(solution)/shard_map/ppermute | solution.py:890
  323.5 14.6 %copy-start.19 = (bf16[256,768]{1,0:T(8,128)(2,1)S(1)}, bf16[256,768]{1,0:T(8,128)(2,1)}, u32[]{:S(2)}) copy-start(bf16[256,768]{1,0:T(8,128)(2,1)} %get-tuple-element.199) | copy-start | bytes 1179652
  324.3 21.7 %copy-start.2 = (f32[6,32,512]{2,1,0:T(8,128)S(1)}, f32[6,32,512]{2,1,0:T(8,128)}, u32[]{:S(2)}) copy-start(f32[6,32,512]{2,1,0:T(8,128)} %get-tuple-element.215) | copy-start | bytes 1179652
  324.3 21.7 %copy-start.9 = (f32[6]{0:T(128)S(1)}, f32[6]{0:T(128)}, u32[]{:S(2)}) copy-start(f32[6]{0:T(128)} %param.24) | copy-start | bytes 76
  324.4 14.5 %collective-permute-start.32 = (bf16[416,128]{1,0:T(8,128)(2,1)S(1)}, bf16[416,128]{1,0:T(8,128)(2,1)S(1)}, u32[]{:S(2)}, u32[]{:S(2)}) collective-permute-start(bf16[416,128]{1,0:T(8,128)(2,1)S(1)} %get-tuple-element.229), channel_id=1, source_target_pairs={{0,4},{1,5},{2,6},{3,7},{4,0},{5,1},{6,2},{7,3},{8,12},{9,13},{10,... | collective-permute-start | bytes 319496 | tf_op jit(solution)/shard_map/ppermute | solution.py:890
  335.2 10.2 %collective-permute-start.33 = (bf16[416,128]{1,0:T(8,128)(2,1)S(1)}, bf16[416,128]{1,0:T(8,128)(2,1)S(1)}, u32[]{:S(2)}, u32[]{:S(2)}) collective-permute-start(bf16[416,128]{1,0:T(8,128)(2,1)S(1)} %get-tuple-element.231), channel_id=1, source_target_pairs={{0,8},{1,9},{2,10},{3,11},{4,12},{5,13},{6,14},{7,15},{8,0},{9,1},... | collective-permute-start | bytes 319496 | tf_op jit(solution)/shard_map/ppermute | solution.py:890
  335.2 10.2 %collective-permute-start.34 = (bf16[416,128]{1,0:T(8,128)(2,1)S(1)}, bf16[416,128]{1,0:T(8,128)(2,1)S(1)}, u32[]{:S(2)}, u32[]{:S(2)}) collective-permute-start(bf16[416,128]{1,0:T(8,128)(2,1)S(1)} %get-tuple-element.230), channel_id=1, source_target_pairs={{0,12},{1,13},{2,14},{3,15},{4,8},{5,9},{6,10},{7,11},{8,4},{9,5},... | collective-permute-start | bytes 319496 | tf_op jit(solution)/shard_map/ppermute | solution.py:890
  338.1 12.8 %collective-permute-start.31 = (bf16[256,768]{1,0:T(8,128)(2,1)S(1)}, bf16[256,768]{1,0:T(8,128)(2,1)S(1)}, u32[]{:S(2)}, u32[]{:S(2)}) collective-permute-start(bf16[256,768]{1,0:T(8,128)(2,1)S(1)} %copy-done.19), channel_id=1, source_target_pairs={{0,16},{16,0},{1,17},{17,1},{2,18},{18,2},{3,19},{19,3},{4,20},{20... | collective-permute-start | bytes 1179656 | tf_op jit(solution)/shard_map/ppermute | solution.py:890
  345.6 5.3 %copy-start.5 = (f32[256,768]{1,0:T(8,128)S(1)}, f32[256,768]{1,0:T(8,128)}, u32[]{:S(2)}) copy-start(f32[256,768]{1,0:T(8,128)} %get-tuple-element.198) | copy-start | bytes 2359300
  345.6 4.0 %collective-permute-start.35 = (bf16[216,128]{1,0:T(8,128)(2,1)S(1)}, bf16[216,128]{1,0:T(8,128)(2,1)S(1)}, u32[]{:S(2)}, u32[]{:S(2)}) collective-permute-start(bf16[216,128]{1,0:T(8,128)(2,1)S(1)} %bitcast.206), channel_id=1, source_target_pairs={{0,16},{16,0},{1,17},{17,1},{2,18},{18,2},{3,19},{19,3},{4,20},{20... | collective-permute-start | bytes 165896 | tf_op jit(solution)/shard_map/ppermute | solution.py:890
  (6 other events, 10.8 us)
Sparse Core Ops, SparseCore 0:
  23.5 57.8 all-gather.2
  83.7 58.4 all-gather.4
